TPU v7x, 32 devices: a whole 2x2x4 slice. The times are simulated.
32 devices in a mesh: row: 4 (over y, x), col: 8 (over z, core).
Axes of the slice: x: 2, y: 2, z: 4, core: 2. Of those that a mesh axis runs over, the one named last changes fastest.
Arguments:
- positions: float32 [3, 4096, 128], P(None, ('row', 'col')), may hold values from -6 to 6
- block_links: int32 [2, 4096], replicated, may hold values from 0 to 4095, as said below
- panel_points: int32 [4, 256], replicated, may hold values from 0 to 524287
Outputs:
- smoothed: float32 [3, 8192, 128], P(None, ('row', 'col'))
- velocity: float32 [4, 3, 256], P('row', None, 'col')
Inputs may be any that keep to these rules, and one draw needn't show every extreme that they name: block_links[0, b] is an owner device, numbered in the order of row+col; block_links[1] is a permutation of the 4096 blocks whose cycles are the loops, and all blocks of one loop have one owner. The 128 blocks of one device, b // 128, include at most 8 of any one owner, and in every draw one owner has exactly 8 blocks on every device.
All inputs are finite; a program needn't handle non-finite values.
Results may differ from a plain program's by a relative error of at most 0.0003.
Values sent between devices are 32-bit elements; how exact they have to be, the bound alone decides.
No kernel may reach another device: no remote copies, remote signals or barrier semaphores. Data moves between devices by JAX's collectives and lax.ppermute only.
A program may use at most 128 MiB of HBM per device.

v0:
```python
import math

import jax
import jax.numpy as jnp
from jax import lax
from jax.sharding import PartitionSpec as P

SWEEPS = 2


SMOOTH_RATE = 0.25
CORE_SQUARED = 0.01


def cross_three(left_vec, right_vec):
    return jnp.stack(
        [
            left_vec[1] * right_vec[2] - left_vec[2] * right_vec[1],
            left_vec[2] * right_vec[0] - left_vec[0] * right_vec[2],
            left_vec[0] * right_vec[1] - left_vec[1] * right_vec[0],
        ]
    )


def neighbours(points, next_slot, prev_slot):
    ahead = jnp.concatenate([points[:, :, 1:], points[:, next_slot, :1]], axis=2)
    behind = jnp.concatenate([points[:, prev_slot, -1:], points[:, :, :-1]], axis=2)
    return (behind, ahead)


def smooth_loops(points, next_slot, prev_slot):
    for sweep_no in range(SWEEPS):
        behind, ahead = neighbours(points, next_slot, prev_slot)
        points = points + SMOOTH_RATE * (behind - 2.0 * points + ahead)
    return points


def panel_sums(targets, sources):
    centres = sources[:3]
    segments = sources[3:]
    inner = lax.dot_general(
        targets, centres, (((0,), (0,)), ((), ())), precision=lax.Precision.HIGHEST
    )
    squared = (
        jnp.sum(targets * targets, 0)[:, None]
        + jnp.sum(centres * centres, 0)[None, :]
        - 2.0 * inner
        + CORE_SQUARED
    )
    weights = 1.0 / (squared * jnp.sqrt(squared))
    features = jnp.concatenate([segments, cross_three(segments, centres)], 0)
    return lax.dot_general(
        weights, features, (((1,), (1,)), ((), ())), precision=lax.Precision.HIGHEST
    )


def tiled_sums(targets, piece, running, largest):
    blocks = piece.shape[1]
    block_len = piece.shape[2]
    group = max(
        [
            size_try
            for size_try in (1, 2, 4, 8, 16, 32, 64, 128)
            if blocks % size_try == 0 and size_try <= largest
        ]
    )

    def one_tile(turn, accum):
        tile = lax.dynamic_slice_in_dim(piece, turn * group, group, 1).reshape(6, group * block_len)
        return accum + panel_sums(targets, tile)

    return lax.fori_loop(0, blocks // group, one_tile, running)


def shards(positions, block_links, panel_points):
    devices = lax.axis_size(("row", "col"))
    my_index = lax.axis_index(("row", "col"))
    slots = positions.shape[1]
    block_len = positions.shape[2]
    capacity = 2 * slots // devices
    held_slots = devices * capacity
    owners = block_links[0]
    follows = block_links[1]
    blocks_all = owners.shape[0]
    counter = jnp.arange(blocks_all, dtype=jnp.int32)
    precedes = jnp.zeros_like(follows).at[follows].set(counter)
    owner_grid = owners.reshape(devices, slots)
    same_owner = owner_grid[:, :, None] == owner_grid[:, None, :]
    earlier = jnp.arange(slots)[None, :] < jnp.arange(slots)[:, None]
    ranks = jnp.sum(jnp.logical_and(same_owner, earlier[None]), axis=2).reshape(blocks_all)
    places = counter // slots * capacity + ranks
    my_owner = lax.dynamic_slice_in_dim(owners, my_index * slots, slots)
    my_rank = lax.dynamic_slice_in_dim(ranks, my_index * slots, slots)
    outgoing_slot = my_owner * capacity + my_rank
    outgoing = (
        jnp.zeros((3, held_slots, block_len), jnp.float32).at[:, outgoing_slot, :].set(positions)
    )
    arrived = lax.all_to_all(outgoing, ("row", "col"), split_axis=1, concat_axis=1, tiled=True)
    is_owned = owners == my_index
    held_ids = (
        jnp.full((held_slots,), blocks_all, jnp.int32)
        .at[jnp.where(is_owned, places, held_slots)]
        .set(counter, mode="drop")
    )
    live = held_ids < blocks_all
    safe_ids = jnp.minimum(held_ids, blocks_all - 1)
    slot_index = jnp.arange(held_slots, dtype=jnp.int32)
    next_slot = jnp.where(live, places[follows[safe_ids]], slot_index)
    prev_slot = jnp.where(live, places[precedes[safe_ids]], slot_index)
    smoothed = smooth_loops(arrived, next_slot, prev_slot)
    behind, ahead = neighbours(smoothed, next_slot, prev_slot)
    segments = ahead - smoothed
    centres = 0.5 * (ahead + smoothed)
    sources = jnp.concatenate([centres, segments], 0)
    wanted = panel_points.reshape(-1)
    wanted_block = wanted // block_len
    wanted_point = wanted % block_len
    wanted_mine = owners[wanted_block] == my_index
    picked = smoothed[:, places[wanted_block], wanted_point]
    local_targets = jnp.where(wanted_mine[None, :], picked, 0.0)
    all_targets = lax.psum(local_targets, ("row", "col"))
    panel = panel_points.shape[1]
    col_count = lax.axis_size("col")
    share = panel // col_count
    scale = 1.0 / (math.pi * math.sqrt(blocks_all * block_len))
    targets = lax.dynamic_slice_in_dim(all_targets, lax.axis_index("row") * panel, panel, 1)
    zero_sums = jnp.zeros((panel, 6), jnp.float32)
    sums = tiled_sums(targets, lax.all_gather(sources, "row", axis=1, tiled=True), zero_sums, 128)
    partial_velocity = scale * (cross_three(sums[:, :3].T, targets) - sums[:, 3:].T)
    summed = lax.psum(partial_velocity, "col")
    velocity_part = lax.dynamic_slice_in_dim(summed, lax.axis_index("col") * share, share, 1)
    return (smoothed, velocity_part[None])


def solution(mesh):
    placed = (P(None, ("row", "col"), None), P(), P())
    return jax.shard_map(
        shards,
        mesh=mesh,
        in_specs=placed,
        out_specs=(P(None, ("row", "col"), None), P("row", None, "col")),
        check_vma=False,
    )
```

profile of v0, /device:TPU:0, one launch (start us, length us, event | category | flops | bytes accessed | tf_op | source)
XLA Modules:
  0.0 509.0 jit_solution(11690375834123952606)
XLA Ops:
  9.1 1.3 convert_reduce_fusion
  11.4 12.5 %scatter_fusion = f32[3,256,128]{2,0,1:T(4,128)} fusion(f32[3,256,128]{2,0,1:T(4,128)} %broadcast_in_dim.36, s32[128]{0:T(128)S(1)} %compare_select_fusion.13, f32[128,3,128]{2,1,0:T(4,128)S(1)} %copy.77), kind=kCustom, calls=%fused_computation.12 | custom fusion | bytes 590336 | tf_op jit(solution)/shard_map/scatter | solution.py:96
  23.9 7.3 %all-to-all-start = ((f32[3,256,128]{2,0,1:T(4,128)}), f32[3,256,128]{2,0,1:T(4,128)S(1)}, u32[]{:S(2)}, u32[]{:S(2)}) async-start(f32[3,256,128]{2,0,1:T(4,128)} %scatter_fusion), calls=%async_computation | async-start | bytes 1048576 | tf_op jit(solution)/shard_map/all_to_all | solution.py:98
  32.1 15.5 %scatter_custom_fusion.1 = s32[256]{0:T(256)S(1)} fusion(s32[4096]{0:T(1024)S(1)} %bitcast.119, s32[4096]{0:T(1024)S(1)} %iota.31, s32[]{:T(128)} %constant.150.clone.1), kind=kCustom, calls=%fused_computation.120 | custom fusion | bytes 1028 | tf_op jit(solution)/shard_map/scatter | solution.py:103
  47.7 15.7 %scatter_custom_fusion.2 = s32[4096]{0:T(1024)S(1)} fusion(s32[4096]{0:T(1024)S(1)} %bitcast.118, s32[4096]{0:T(1024)S(1)} %iota.33, s32[]{:T(128)} %constant.145.clone.1), kind=kCustom, calls=%fused_computation.84 | custom fusion | bytes 16388 | tf_op jit(solution)/shard_map/scatter | solution.py:86
  63.4 1.7 gather_fusion.3
  65.1 1.7 gather_fusion
  66.9 1.7 gather_fusion.1
  68.6 1.7 gather_fusion.4
  70.4 8.3 %copy.78 = f32[3,256,128]{0,2,1:T(8,128)} copy(f32[3,256,128]{2,0,1:T(4,128)S(1)} %all-to-all-done) | data formatting | bytes 786432 | tf_op jit(solution)/shard_map/all_to_all | solution.py:98
  78.7 2.3 gather_fusion.5
  81.0 2.3 gather_fusion.2
  83.3 1.7 copy.83
  85.0 1.7 copy.80
  88.1 8.3 %copy.84 = f32[3,256,128]{0,2,1:T(8,128)} copy(f32[3,256,128]{2,0,1:T(4,128)S(1)} %fusion.22) | data formatting | bytes 786432 | tf_op jit(solution)/shard_map/add | solution.py:34
  96.4 2.3 gather_fusion.6
  98.8 2.3 gather_fusion.7
  101.1 1.7 copy.86
  102.8 1.7 copy.89
  105.5 8.7 %copy.90 = f32[3,256,128]{0,2,1:T(8,128)} copy(f32[3,256,128]{2,0,1:T(4,128)S(1)} %fusion.25) | data formatting | bytes 786432 | tf_op jit(solution)/shard_map/add | solution.py:34
  114.2 2.3 gather_fusion.11
  116.5 1.7 copy.93
  119.9 6.2 %gather_fusion.9 = s32[1024]{0:T(1024)S(1)} fusion(s32[4096]{0:T(1024)S(1)} %fusion.28, s32[1024]{0:T(1024)S(1)} %broadcast_clamp_fusion), kind=kCustom, calls=%fused_computation.9 | custom fusion | bytes 12288 | tf_op jit(solution)/shard_map/gather | solution.py:119
  126.1 6.2 %gather_fusion.8 = s32[1024]{0:T(1024)S(1)} fusion(s32[4096]{0:T(1024)S(1)} %bitcast.99, s32[1024]{0:T(1024)S(1)} %broadcast_clamp_fusion), kind=kCustom, calls=%fused_computation.8 | custom fusion | bytes 12288 | tf_op jit(solution)/shard_map/gather | solution.py:118
  133.1 10.5 %gather_fusion.10 = f32[1024,3]{1,0:T(8,128)S(1)} fusion(f32[3,256,128]{0,2,1:T(8,128)} %copy.90, s32[1024]{0:T(1024)S(1)} %bitcast.101), kind=kCustom, calls=%fused_computation.10 | custom fusion | bytes 32768 | tf_op jit(solution)/shard_map/gather | solution.py:119
  143.8 49.0 %psum.14 = f32[3,1024]{0,1:T(8,128)S(1)} all-reduce(f32[3,1024]{0,1:T(8,128)S(1)} %select_bitcast_fusion), channel_id=1, replica_groups=mesh['row'=4,'col'=8] {'row','col'}, use_global_device_ids=true, to_apply=%region_4.5 | all-reduce | flops 3072 | bytes 24576 | tf_op jit(solution)/shard_map/psum | solution.py:121
  193.5 293.5 %while.16 = (s32[]{:T(128)}, f32[256,6]{0,1:T(8,128)S(1)}, f32[256]{0:T(256)S(1)}, f32[6,1024,128]{2,1,0:T(8,128)}, f32[3,256]{1,0:T(4,128)S(1)}, /*index=5*/s32...) while((s32[]{:T(128)}, f32[256,6]{0,1:T(8,128)S(1)}, ...), condition=%wide.region_8.9_spmd.clone, body=%wide.region_6.8_spmd.clone.sunk | while | flops 478678016 | bytes 36061472 | solution.py:72
  194.7 1.1 dynamic-slice_bitcast_fusion.4
  195.9 25.7 %sqrt_multiply_fusion.2 = f32[256,16384]{0,1:T(8,128)S(1)} fusion(f32[3,256]{1,0:T(4,128)S(1)} %get-tuple-element.277, f32[16384]{0:T(1024)S(1)} %bitcast.107, f32[256]{0:T(256)S(1)} %get-tuple-element.275, f32[1,3,128,128]{3,2,1,0:T(8,128)S(1)} %get-tuple-element.240), kind=kOutput, calls=%fused_computation.15.clone.1 | convolution fusion | flops 171966464 | bytes 17043456 | tf_op jit(solution)/shard_map/while/body/eval_jaxpr/dot_general | solution.py:41
  221.6 8.7 %fusion.67 = f32[256,6]{0,1:T(8,128)S(1)} fusion(f32[256,16384]{0,1:T(8,128)S(1)} %sqrt_multiply_fusion.2, f32[1,16384]{1,0:T(1,128)S(1)} %bitcast.106, f32[1,16384]{1,0:T(1,128)S(1)} %bitcast.105, f32[1,16384]{1,0:T(1,128)S(1)} %bitcast.104, f32[3,16384]{1,0:T(4,128)S(1)} %bitcast.102, f32[256,6]{0,1:T(8,128)S(1)} %get-tuple-element.260, ...), kind=kOutput, calls=%fused_computation.23.clone.1 | convolution fusion | flops 306482176 | bytes 17182720 | tf_op jit(solution)/shard_map/while/body/eval_jaxpr/dot_general | solution.py:52
  231.3 1.1 dynamic-slice_bitcast_fusion.4
  232.6 25.7 %sqrt_multiply_fusion.2 = f32[256,16384]{0,1:T(8,128)S(1)} fusion(f32[3,256]{1,0:T(4,128)S(1)} %get-tuple-element.277, f32[16384]{0:T(1024)S(1)} %bitcast.107, f32[256]{0:T(256)S(1)} %get-tuple-element.275, f32[1,3,128,128]{3,2,1,0:T(8,128)S(1)} %get-tuple-element.240), kind=kOutput, calls=%fused_computation.15.clone.1 | convolution fusion | flops 171966464 | bytes 17043456 | tf_op jit(solution)/shard_map/while/body/eval_jaxpr/dot_general | solution.py:41
  258.2 8.7 %fusion.67 = f32[256,6]{0,1:T(8,128)S(1)} fusion(f32[256,16384]{0,1:T(8,128)S(1)} %sqrt_multiply_fusion.2, f32[1,16384]{1,0:T(1,128)S(1)} %bitcast.106, f32[1,16384]{1,0:T(1,128)S(1)} %bitcast.105, f32[1,16384]{1,0:T(1,128)S(1)} %bitcast.104, f32[3,16384]{1,0:T(4,128)S(1)} %bitcast.102, f32[256,6]{0,1:T(8,128)S(1)} %get-tuple-element.260, ...), kind=kOutput, calls=%fused_computation.23.clone.1 | convolution fusion | flops 306482176 | bytes 17182720 | tf_op jit(solution)/shard_map/while/body/eval_jaxpr/dot_general | solution.py:52
  268.0 1.1 dynamic-slice_bitcast_fusion.4
  269.2 25.7 %sqrt_multiply_fusion.2 = f32[256,16384]{0,1:T(8,128)S(1)} fusion(f32[3,256]{1,0:T(4,128)S(1)} %get-tuple-element.277, f32[16384]{0:T(1024)S(1)} %bitcast.107, f32[256]{0:T(256)S(1)} %get-tuple-element.275, f32[1,3,128,128]{3,2,1,0:T(8,128)S(1)} %get-tuple-element.240), kind=kOutput, calls=%fused_computation.15.clone.1 | convolution fusion | flops 171966464 | bytes 17043456 | tf_op jit(solution)/shard_map/while/body/eval_jaxpr/dot_general | solution.py:41
  294.9 8.7 %fusion.67 = f32[256,6]{0,1:T(8,128)S(1)} fusion(f32[256,16384]{0,1:T(8,128)S(1)} %sqrt_multiply_fusion.2, f32[1,16384]{1,0:T(1,128)S(1)} %bitcast.106, f32[1,16384]{1,0:T(1,128)S(1)} %bitcast.105, f32[1,16384]{1,0:T(1,128)S(1)} %bitcast.104, f32[3,16384]{1,0:T(4,128)S(1)} %bitcast.102, f32[256,6]{0,1:T(8,128)S(1)} %get-tuple-element.260, ...), kind=kOutput, calls=%fused_computation.23.clone.1 | convolution fusion | flops 306482176 | bytes 17182720 | tf_op jit(solution)/shard_map/while/body/eval_jaxpr/dot_general | solution.py:52
  304.7 1.1 dynamic-slice_bitcast_fusion.4
  305.9 25.7 %sqrt_multiply_fusion.2 = f32[256,16384]{0,1:T(8,128)S(1)} fusion(f32[3,256]{1,0:T(4,128)S(1)} %get-tuple-element.277, f32[16384]{0:T(1024)S(1)} %bitcast.107, f32[256]{0:T(256)S(1)} %get-tuple-element.275, f32[1,3,128,128]{3,2,1,0:T(8,128)S(1)} %get-tuple-element.240), kind=kOutput, calls=%fused_computation.15.clone.1 | convolution fusion | flops 171966464 | bytes 17043456 | tf_op jit(solution)/shard_map/while/body/eval_jaxpr/dot_general | solution.py:41
  331.5 8.7 %fusion.67 = f32[256,6]{0,1:T(8,128)S(1)} fusion(f32[256,16384]{0,1:T(8,128)S(1)} %sqrt_multiply_fusion.2, f32[1,16384]{1,0:T(1,128)S(1)} %bitcast.106, f32[1,16384]{1,0:T(1,128)S(1)} %bitcast.105, f32[1,16384]{1,0:T(1,128)S(1)} %bitcast.104, f32[3,16384]{1,0:T(4,128)S(1)} %bitcast.102, f32[256,6]{0,1:T(8,128)S(1)} %get-tuple-element.260, ...), kind=kOutput, calls=%fused_computation.23.clone.1 | convolution fusion | flops 306482176 | bytes 17182720 | tf_op jit(solution)/shard_map/while/body/eval_jaxpr/dot_general | solution.py:52
  342.5 25.7 %sqrt_multiply_fusion.2 = f32[256,16384]{0,1:T(8,128)S(1)} fusion(f32[3,256]{1,0:T(4,128)S(1)} %get-tuple-element.277, f32[16384]{0:T(1024)S(1)} %bitcast.107, f32[256]{0:T(256)S(1)} %get-tuple-element.275, f32[1,3,128,128]{3,2,1,0:T(8,128)S(1)} %get-tuple-element.240), kind=kOutput, calls=%fused_computation.15.clone.1 | convolution fusion | flops 171966464 | bytes 17043456 | tf_op jit(solution)/shard_map/while/body/eval_jaxpr/dot_general | solution.py:41
  368.2 8.7 %fusion.67 = f32[256,6]{0,1:T(8,128)S(1)} fusion(f32[256,16384]{0,1:T(8,128)S(1)} %sqrt_multiply_fusion.2, f32[1,16384]{1,0:T(1,128)S(1)} %bitcast.106, f32[1,16384]{1,0:T(1,128)S(1)} %bitcast.105, f32[1,16384]{1,0:T(1,128)S(1)} %bitcast.104, f32[3,16384]{1,0:T(4,128)S(1)} %bitcast.102, f32[256,6]{0,1:T(8,128)S(1)} %get-tuple-element.260, ...), kind=kOutput, calls=%fused_computation.23.clone.1 | convolution fusion | flops 306482176 | bytes 17182720 | tf_op jit(solution)/shard_map/while/body/eval_jaxpr/dot_general | solution.py:52
  379.2 25.7 %sqrt_multiply_fusion.2 = f32[256,16384]{0,1:T(8,128)S(1)} fusion(f32[3,256]{1,0:T(4,128)S(1)} %get-tuple-element.277, f32[16384]{0:T(1024)S(1)} %bitcast.107, f32[256]{0:T(256)S(1)} %get-tuple-element.275, f32[1,3,128,128]{3,2,1,0:T(8,128)S(1)} %get-tuple-element.240), kind=kOutput, calls=%fused_computation.15.clone.1 | convolution fusion | flops 171966464 | bytes 17043456 | tf_op jit(solution)/shard_map/while/body/eval_jaxpr/dot_general | solution.py:41
  404.9 8.7 %fusion.67 = f32[256,6]{0,1:T(8,128)S(1)} fusion(f32[256,16384]{0,1:T(8,128)S(1)} %sqrt_multiply_fusion.2, f32[1,16384]{1,0:T(1,128)S(1)} %bitcast.106, f32[1,16384]{1,0:T(1,128)S(1)} %bitcast.105, f32[1,16384]{1,0:T(1,128)S(1)} %bitcast.104, f32[3,16384]{1,0:T(4,128)S(1)} %bitcast.102, f32[256,6]{0,1:T(8,128)S(1)} %get-tuple-element.260, ...), kind=kOutput, calls=%fused_computation.23.clone.1 | convolution fusion | flops 306482176 | bytes 17182720 | tf_op jit(solution)/shard_map/while/body/eval_jaxpr/dot_general | solution.py:52
  415.8 25.7 %sqrt_multiply_fusion.2 = f32[256,16384]{0,1:T(8,128)S(1)} fusion(f32[3,256]{1,0:T(4,128)S(1)} %get-tuple-element.277, f32[16384]{0:T(1024)S(1)} %bitcast.107, f32[256]{0:T(256)S(1)} %get-tuple-element.275, f32[1,3,128,128]{3,2,1,0:T(8,128)S(1)} %get-tuple-element.240), kind=kOutput, calls=%fused_computation.15.clone.1 | convolution fusion | flops 171966464 | bytes 17043456 | tf_op jit(solution)/shard_map/while/body/eval_jaxpr/dot_general | solution.py:41
  441.5 8.7 %fusion.67 = f32[256,6]{0,1:T(8,128)S(1)} fusion(f32[256,16384]{0,1:T(8,128)S(1)} %sqrt_multiply_fusion.2, f32[1,16384]{1,0:T(1,128)S(1)} %bitcast.106, f32[1,16384]{1,0:T(1,128)S(1)} %bitcast.105, f32[1,16384]{1,0:T(1,128)S(1)} %bitcast.104, f32[3,16384]{1,0:T(4,128)S(1)} %bitcast.102, f32[256,6]{0,1:T(8,128)S(1)} %get-tuple-element.260, ...), kind=kOutput, calls=%fused_computation.23.clone.1 | convolution fusion | flops 306482176 | bytes 17182720 | tf_op jit(solution)/shard_map/while/body/eval_jaxpr/dot_general | solution.py:52
  452.5 25.7 %sqrt_multiply_fusion.2 = f32[256,16384]{0,1:T(8,128)S(1)} fusion(f32[3,256]{1,0:T(4,128)S(1)} %get-tuple-element.277, f32[16384]{0:T(1024)S(1)} %bitcast.107, f32[256]{0:T(256)S(1)} %get-tuple-element.275, f32[1,3,128,128]{3,2,1,0:T(8,128)S(1)} %get-tuple-element.240), kind=kOutput, calls=%fused_computation.15.clone.1 | convolution fusion | flops 171966464 | bytes 17043456 | tf_op jit(solution)/shard_map/while/body/eval_jaxpr/dot_general | solution.py:41
  478.2 8.7 %fusion.67 = f32[256,6]{0,1:T(8,128)S(1)} fusion(f32[256,16384]{0,1:T(8,128)S(1)} %sqrt_multiply_fusion.2, f32[1,16384]{1,0:T(1,128)S(1)} %bitcast.106, f32[1,16384]{1,0:T(1,128)S(1)} %bitcast.105, f32[1,16384]{1,0:T(1,128)S(1)} %bitcast.104, f32[3,16384]{1,0:T(4,128)S(1)} %bitcast.102, f32[256,6]{0,1:T(8,128)S(1)} %get-tuple-element.260, ...), kind=kOutput, calls=%fused_computation.23.clone.1 | convolution fusion | flops 306482176 | bytes 17182720 | tf_op jit(solution)/shard_map/while/body/eval_jaxpr/dot_general | solution.py:52
  487.5 13.8 %psum.15 = f32[3,256]{1,0:T(4,128)S(1)} all-reduce(f32[3,256]{1,0:T(4,128)S(1)} %fusion.41), channel_id=1, replica_groups=mesh['row'=4,'col'=8] {'col'}, use_global_device_ids=true, to_apply=%region_9.10 | all-reduce | flops 768 | bytes 6144 | tf_op jit(solution)/shard_map/psum | solution.py:130
  (73 shorter events, 24.5 us)
Async XLA Ops:
  23.9 46.5 %all-to-all-start = ((f32[3,256,128]{2,0,1:T(4,128)}), f32[3,256,128]{2,0,1:T(4,128)S(1)}, u32[]{:S(2)}, u32[]{:S(2)}) async-start(f32[3,256,128]{2,0,1:T(4,128)} %scatter_fusion), calls=%async_computation | async-start | bytes 1048576 | tf_op jit(solution)/shard_map/all_to_all | solution.py:98
  31.2 162.3 %all-gather.2.cloned.1.call-start = ((), (), s32[]{:S(2)}) async-start(), calls=%async_computation.1 | async-start | bytes 3932160 | tf_op jit(solution)/shard_map/all_gather | solution.py:128
  96.4 23.4 %copy-start = (s32[4,256]{1,0:T(4,128)S(1)}, s32[4,256]{1,0:T(4,128)}, u32[]{:S(2)}) copy-start(s32[4,256]{1,0:T(4,128)} %param.7) | copy-start | bytes 12292
Sparse Core Ops, SparseCore 0:
  120.0 48.0 all-gather.1
where the time goes:
time: 514 us; the launch traced here: 509 us
  matrix products  275 us (54%)
  local copies, waits for them, and re-layouts  127 us (25%)
  blocking collectives  62.8 us (12%)
  other arithmetic  21.6 us (4%)
  between operations  14.6 us (3%)
  starting transfers between devices  7.35 us (1%)
    dot_general x8, matrix products, panel_sums(): lax.dot_general(targets, centres, (((0,), (0,)), ((), ())), precision=lax...  205 us
    dot_general x8, matrix products, panel_sums(): lax.dot_general(weights, features, (((1,), (1,)), ((), ())), precision=la...  70 us
    psum x1, blocking collectives, shards(): all_targets = lax.psum(local_targets, ('row', 'col'))  49 us
    add x2, local copies, waits for them, and re-layouts, smooth_loops(): points = points + SMOOTH_RATE * (behind - 2.0 * points + ahead)  17 us
    gather x2, local copies, waits for them, and re-layouts, shards(): picked = smoothed[:, places[wanted_block], wanted_point]  16.7 us
    scatter x1, local copies, waits for them, and re-layouts, shards(): precedes = jnp.zeros_like(follows).at[follows].set(counter)  15.7 us
    scatter x1, local copies, waits for them, and re-layouts, shards(): held_ids = jnp.full((held_slots,), blocks_all, jnp.int32).at[jnp.where(is...  15.5 us
    psum x1, blocking collectives, shards(): summed = lax.psum(partial_velocity, 'col')  13.8 us
  transfers between devices with their start and end apart: 2, of which 0 were waited for; matrix products, arithmetic and copies ran while one was open for 12% of the time, Pallas kernels for 0%

commit v1 on v0

v1 whole, which is shorter than its diff:
```python
import functools
import math

import jax
import jax.numpy as jnp
from jax import lax
from jax.experimental import pallas as pl
from jax.experimental.pallas import tpu as pltpu
from jax.sharding import PartitionSpec as P

CORE_SQUARED = 0.01
F32 = jnp.float32
BF16 = jnp.bfloat16
LANES = 128
DEPTH = 32
FEATS = 16
EDGES = 5
AXES = ("row", "col")


def iota(shape, dim):
    return lax.broadcasted_iota(jnp.int32, shape, dim)


def three_parts(value):
    first = value.astype(BF16)
    rest = value - first.astype(F32)
    second = rest.astype(BF16)
    third = (rest - second.astype(F32)).astype(BF16)
    return (first, second, third)


def dot(left, right):
    return jnp.dot(left, right, preferred_element_type=F32)


def pick(onehot, value):
    first, second, third = three_parts(value)
    return dot(onehot, first) + dot(onehot, second) + dot(onehot, third)


def as_columns(row):
    return jnp.transpose(jnp.broadcast_to(row.astype(F32), (LANES, row.shape[1])))


def shifted(value, steps):
    return pltpu.roll(value, (-steps) % LANES, 1)


def five_taps(far_left, left, here, right, far_right):
    return (far_left + far_right + 4.0 * (left + right) + 6.0 * here) * 0.0625


def cross(left_vec, right_vec):
    return [
        left_vec[1] * right_vec[2] - left_vec[2] * right_vec[1],
        left_vec[2] * right_vec[0] - left_vec[0] * right_vec[2],
        left_vec[0] * right_vec[1] - left_vec[1] * right_vec[0],
    ]


def source_rows(here, ahead, keep=None):
    segment = [a - h for a, h in zip(ahead, here)]
    centre = [0.5 * (a + h) for a, h in zip(ahead, here)]
    if keep is not None:
        segment = [jnp.where(keep, s, 0.0) for s in segment]
    near = []
    for value in centre:
        one, two, three = [part.astype(F32) for part in three_parts(value)]
        near += [one, two, three, one, two, one]
    norm = centre[0] * centre[0] + centre[1] * centre[1] + centre[2] * centre[2]
    near += [part.astype(F32) for part in three_parts(norm)]
    near += [jnp.ones_like(norm)] * 3
    terms = segment + cross(segment, centre)
    tops = [value.astype(BF16).astype(F32) for value in terms]
    sums = tops + [value - top for value, top in zip(terms, tops)]
    return near, sums


def target_rows(targets):
    rows = []
    for value in targets:
        one, two, three = [part.astype(F32) for part in three_parts(-2.0 * value)]
        rows += [one, one, one, two, two, three]
    norm = targets[0] * targets[0] + targets[1] * targets[1] + targets[2] * targets[2]
    rows += [jnp.ones_like(norm)] * 3
    rows += [part.astype(F32) for part in three_parts(norm + CORE_SQUARED)]
    return rows


def pair_sums(near, sums, target_side):
    squared = lax.dot_general(
        near, target_side, (((0,), (0,)), ((), ())), preferred_element_type=F32
    )
    root = lax.rsqrt(squared)
    weight = root * root * root
    top = weight.astype(BF16)
    rest = (weight - top.astype(F32)).astype(BF16)
    return dot(sums, top) + dot(sums, rest)


def prep_kernel(cap, me_ref, pos_ref, links_ref, panel_ref, part_ref, out_ref, near_ref, sums_ref, near_scr, sums_scr):
    me = me_ref[0]
    blocks = pos_ref.shape[1]
    held = out_ref.shape[1]
    total = links_ref.shape[1]
    copies = part_ref.shape[0]
    base = me * blocks
    mine = pl.ds(pl.multiple_of(base, LANES), blocks)
    lane = iota((blocks, LANES), 1)
    ids = iota((blocks, LANES), 0) + base

    wanted = jnp.concatenate([panel_ref[r : r + 1, :] for r in range(panel_ref.shape[0])], axis=1)
    count = wanted.shape[1]
    shift = LANES.bit_length() - 1
    wanted_block = lax.shift_right_logical(wanted, shift)
    wanted_point = jnp.bitwise_and(wanted, LANES - 1)

    follow_col = as_columns(links_ref[1:2, mine]).astype(jnp.int32)[:, :1]
    found = jnp.zeros((blocks, LANES), F32)
    lane_f = lane.astype(F32)
    for r in range(total // LANES):
        row = links_ref[1:2, r * LANES : (r + 1) * LANES]
        found = found + jnp.where(row == ids, lane_f + float(r * LANES), 0.0)
    precede_col = jnp.sum(found, axis=1, keepdims=True).astype(jnp.int32)

    held_here = wanted_block == (iota((blocks, count), 0) + base)
    before = jnp.logical_and(wanted_point < 2, follow_col == wanted_block)
    after = jnp.logical_and(wanted_point >= LANES - 2, precede_col == wanted_block)
    onehot = jnp.concatenate(
        [
            jnp.where(held_here, 1.0, 0.0).astype(BF16),
            jnp.where(jnp.logical_or(before, after), 1.0, 0.0).astype(BF16),
        ],
        axis=0,
    )
    at_point = iota((LANES, count), 0) == wanted_point

    here_all = []
    for c in range(3):
        x = pos_ref[c]
        rolled = {s: shifted(x, s) for s in (-2, -1, 1, 2)}
        inner = {
            s: jnp.where((lane >= -s) if s < 0 else (lane < LANES - s), v, 0.0)
            for s, v in rolled.items()
        }
        outer = {s: rolled[s] - inner[s] for s in rolled}
        own = five_taps(inner[-2], inner[-1], x, inner[1], inner[2])
        other = five_taps(outer[-2], outer[-1], 0.0, outer[1], outer[2])
        here_all.append(own)
        both = jnp.transpose(jnp.concatenate([own, other], axis=0))
        one, two, three = three_parts(both)
        values = dot(one, onehot) + dot(two, onehot) + dot(three, onehot)
        row = jnp.sum(jnp.where(at_point, values, 0.0), axis=0, keepdims=True)
        per = count // LANES
        for i in range(per):
            part_ref[:, c * per + i, :] = jnp.broadcast_to(
                row[:, i * LANES : (i + 1) * LANES], (copies, LANES)
            )

    owner_row = links_ref[0:1, mine]
    owner_col = as_columns(owner_row).astype(jnp.int32)
    same = jnp.logical_and(owner_col == owner_row, iota((blocks, blocks), 0) < iota((blocks, blocks), 1))
    rank = jnp.sum(jnp.where(same, 1.0, 0.0), axis=0, keepdims=True).astype(jnp.int32)
    slot = owner_row * cap + rank
    into = jnp.where(iota((held, blocks), 0) == slot, 1.0, 0.0).astype(BF16)
    for c in range(3):
        out_ref[c] = pick(into, pos_ref[c])

    ahead_all = [shifted(v, 1) for v in here_all]
    keep = jnp.logical_and(lane >= 2, lane <= LANES - 4)
    near, sums = source_rows(here_all, ahead_all, keep)
    near_scr[...] = jnp.zeros_like(near_scr)
    sums_scr[...] = jnp.zeros_like(sums_scr)
    for k, value in enumerate(near):
        near_scr[pl.ds(k, blocks, stride=DEPTH), :] = value
    for k, value in enumerate(sums):
        sums_scr[pl.ds(k, blocks, stride=FEATS), :] = value
    for b in range(blocks):
        near_ref[:, b * LANES : (b + 1) * LANES] = near_scr[b * DEPTH : (b + 1) * DEPTH, :].astype(BF16)
        sums_ref[:, b * LANES : (b + 1) * LANES] = sums_scr[b * FEATS : (b + 1) * FEATS, :].astype(BF16)


def pair_kernel(tile, parts, part_ref, near_ref, sums_ref, acc_ref, side_ref, target_ref, rows_scr):
    added = jnp.sum(part_ref[...], axis=0)
    per = added.shape[0] // 3
    targets = [
        jnp.concatenate([added[c * per + i : c * per + i + 1, :] for i in range(per)], axis=1)
        for c in range(3)
    ]
    rows_scr[...] = jnp.zeros_like(rows_scr)
    for c in range(3):
        target_ref[c : c + 1, :] = targets[c]
    for k, row in enumerate(target_rows(targets)):
        rows_scr[k : k + 1, :] = row
    side_ref[...] = rows_scr[...].astype(BF16)
    count = side_ref.shape[1]
    piece = tile // parts

    def one_tile(turn, running):
        result = []
        for s in range(parts):
            at = pl.ds(pl.multiple_of(turn * tile + s * piece, piece), piece)
            result.append(running[s] + pair_sums(near_ref[:, at], sums_ref[:, at], side_ref[...]))
        return tuple(result)

    zeros = tuple(jnp.zeros((FEATS, count), F32) for s in range(parts))
    running = lax.fori_loop(0, near_ref.shape[1] // tile, one_tile, zeros)
    acc_ref[...] = sum(running[1:], running[0])


def owner_kernel(cap, scale, me_ref, links_ref, arrived_ref, side_ref, target_ref, acc_ref, smooth_ref, vel_ref, owner_scr, follow_scr, near_scr, sums_scr):
    me = me_ref[0]
    held = arrived_ref.shape[1]
    devices = owner_scr.shape[0]
    for r in range(devices):
        owner_scr[r : r + 1, :] = links_ref[0:1, r * LANES : (r + 1) * LANES]
        follow_scr[r : r + 1, :] = links_ref[1:2, r * LANES : (r + 1) * LANES]
    owned = jnp.where(owner_scr[...] == me, 1.0, 0.0)
    upper = jnp.where(iota((LANES, LANES), 0) < iota((LANES, LANES), 1), 1.0, 0.0)
    rank = dot(owned.astype(BF16), upper.astype(BF16))
    shift = LANES.bit_length() - 1
    follow = follow_scr[...]
    table = jnp.concatenate(
        [
            owned,
            rank,
            lax.shift_right_logical(follow, shift).astype(F32),
            jnp.bitwise_and(follow, LANES - 1).astype(F32),
        ],
        axis=1,
    ).astype(BF16)
    cap_shift = cap.bit_length() - 1
    slot = iota((held, devices), 0)
    spread = jnp.where(
        lax.shift_right_logical(slot, cap_shift) == iota((held, devices), 1), 1.0, 0.0
    ).astype(BF16)
    wide = dot(spread, table)
    slots = iota((held, LANES), 0)
    seat = jnp.bitwise_and(slots, cap - 1).astype(F32)
    hit = jnp.logical_and(wide[:, :LANES] == 1.0, wide[:, LANES : 2 * LANES] == seat)
    number = (lax.shift_right_logical(slots, cap_shift) * LANES + iota((held, LANES), 1)).astype(F32)
    target_no = wide[:, 2 * LANES : 3 * LANES] * float(LANES) + wide[:, 3 * LANES :]
    live = jnp.sum(jnp.where(hit, 1.0, 0.0), axis=1, keepdims=True)
    id_col = jnp.sum(jnp.where(hit, number, 0.0), axis=1, keepdims=True) + live - 1.0
    next_col = jnp.sum(jnp.where(hit, target_no, 0.0), axis=1, keepdims=True) + 2.0 * live - 2.0
    id_row = jnp.transpose(jnp.broadcast_to(id_col, (held, LANES)))[:1, :]
    next_row = jnp.transpose(jnp.broadcast_to(next_col, (held, LANES)))[:1, :]
    to_next = jnp.where(next_col == id_row, 1.0, 0.0).astype(BF16)
    to_prev = jnp.where(id_col == next_row, 1.0, 0.0).astype(BF16)

    lane = iota((held, LANES), 1)
    here_rows = []
    ahead_rows = []
    for c in range(3):
        x = arrived_ref[c]
        after = pick(to_next, x)
        before = pick(to_prev, x)
        at = {0: x}
        for s in (-2, -1):
            at[s] = jnp.where(lane < -s, shifted(before, s), shifted(x, s))
        for s in (1, 2, 3):
            at[s] = jnp.where(lane >= LANES - s, shifted(after, s), shifted(x, s))
        y = five_taps(at[-2], at[-1], at[0], at[1], at[2])
        smooth_ref[c] = y
        ahead = five_taps(at[-1], at[0], at[1], at[2], at[3])
        y_t = jnp.transpose(y)
        ahead_t = jnp.transpose(ahead)
        here_rows.append(jnp.concatenate([y_t[:2], y_t[LANES - 3 :]], axis=0))
        ahead_rows.append(jnp.concatenate([ahead_t[:2], ahead_t[LANES - 3 :]], axis=0))
    near, sums = source_rows(here_rows, ahead_rows)
    near_scr[...] = jnp.zeros_like(near_scr)
    sums_scr[...] = jnp.zeros_like(sums_scr)
    for k, value in enumerate(near):
        for e in range(EDGES):
            near_scr[k : k + 1, e * held : (e + 1) * held] = value[e : e + 1, :]
    for k, value in enumerate(sums):
        for e in range(EDGES):
            sums_scr[k : k + 1, e * held : (e + 1) * held] = value[e : e + 1, :]
    acc = acc_ref[...] + pair_sums(near_scr[...].astype(BF16), sums_scr[...].astype(BF16), side_ref[...])
    terms = acc[0:6] + acc[6:12]
    targets = [target_ref[c : c + 1, :] for c in range(3)]
    turned = cross([terms[c : c + 1, :] for c in range(3)], targets)
    for c in range(3):
        vel_ref[c : c + 1, :] = scale * (turned[c] - terms[3 + c : 4 + c, :])


def shards(positions, block_links, panel_points):
    devices = lax.axis_size(AXES)
    me = lax.axis_index(AXES).astype(jnp.int32).reshape(1)
    blocks = positions.shape[1]
    cap = 2 * blocks // devices
    held = devices * cap
    total = block_links.shape[1]
    points = blocks * LANES
    panel = panel_points.shape[1]
    count = panel_points.shape[0] * panel
    share = panel // lax.axis_size("col")
    scale = 1.0 / (math.pi * math.sqrt(total * LANES))
    smem = pl.BlockSpec(memory_space=pltpu.SMEM)
    vmem = pl.BlockSpec(memory_space=pltpu.VMEM)
    params = pltpu.CompilerParams(vmem_limit_bytes=48 << 20)
    shape = jax.ShapeDtypeStruct
    rows = 3 * count // LANES

    part, outgoing, near, sums = pl.pallas_call(
        functools.partial(prep_kernel, cap),
        out_shape=(
            shape((devices, rows, LANES), F32),
            shape((3, held, LANES), F32),
            shape((DEPTH, points), BF16),
            shape((FEATS, points), BF16),
        ),
        in_specs=[smem, vmem, vmem, vmem],
        out_specs=[vmem] * 4,
        scratch_shapes=[
            pltpu.VMEM((blocks * DEPTH, LANES), F32),
            pltpu.VMEM((blocks * FEATS, LANES), F32),
        ],
        compiler_params=params,
        name="prep",
    )(me, positions, block_links, panel_points)
    parts = lax.all_to_all(part, AXES, split_axis=0, concat_axis=0, tiled=True)
    arrived = lax.all_to_all(outgoing, AXES, split_axis=1, concat_axis=1, tiled=True)
    acc, side, targets = pl.pallas_call(
        functools.partial(pair_kernel, min(points, 2048), 4),
        out_shape=(
            shape((FEATS, count), F32),
            shape((DEPTH, count), BF16),
            shape((3, count), F32),
        ),
        in_specs=[vmem] * 3,
        out_specs=[vmem] * 3,
        scratch_shapes=[pltpu.VMEM((DEPTH, count), F32)],
        compiler_params=params,
        name="pairs",
    )(parts, near, sums)
    smoothed, velocity = pl.pallas_call(
        functools.partial(owner_kernel, cap, scale),
        out_shape=(shape((3, held, LANES), F32), shape((3, count), F32)),
        in_specs=[smem] + [vmem] * 5,
        out_specs=[vmem] * 2,
        scratch_shapes=[
            pltpu.VMEM((devices, LANES), jnp.int32),
            pltpu.VMEM((devices, LANES), jnp.int32),
            pltpu.VMEM((DEPTH, EDGES * held), F32),
            pltpu.VMEM((FEATS, EDGES * held), F32),
        ],
        compiler_params=params,
        name="owners",
    )(me, block_links, arrived, side, targets, acc)
    shares = lax.all_to_all(
        velocity.reshape(3, devices, share), AXES, split_axis=1, concat_axis=1, tiled=True
    )
    return (smoothed, jnp.sum(shares, axis=1)[None])


def solution(mesh):
    placed = (P(None, AXES, None), P(), P())
    return jax.shard_map(
        shards,
        mesh=mesh,
        in_specs=placed,
        out_specs=(P(None, AXES, None), P("row", None, "col")),
        check_vma=False,
    )
```

time: 514 us -> 85 us (0.17)
  matrix products: 275 us -> 0 us
  local copies, waits for them, and re-layouts: 127 us -> 3.35 us
  Pallas kernels: 0 us -> 31.7 us
  blocking collectives: 62.8 us -> 32.8 us
  other arithmetic: 21.6 us -> 0.04 us
  between operations: 14.6 us -> 0.7 us
  waiting for transfers between devices: 0.02 us -> 13.5 us
    dot_general x16 -> x0, matrix products: 275 us -> none  [the longest x8 205 us: panel_sums(): lax.dot_general(targets, centres, (((0,), (0,)), ((), ())), precision=lax...]
    psum x2 -> x0, blocking collectives: 62.8 us -> none  [the longest x1 49 us: shards(): all_targets = lax.psum(local_targets, ('row', 'col'))]
    gather x17 -> x0, local copies, waits for them, and re-layouts: 49.7 us -> none  [the longest x2 16.7 us: shards(): picked = smoothed[:, places[wanted_block], wanted_point]]
    scatter x3 -> x0, local copies, waits for them, and re-layouts: 43.7 us -> none  [the longest x1 15.7 us: shards(): precedes = jnp.zeros_like(follows).at[follows].set(counter)]
    all_to_all x0 -> x2, blocking collectives: none -> 32.8 us  [the longest x1 23.5 us: shards(): lax.all_to_all(outgoing, AXES, split_axis=1, concat_axis=1, tiled=True)]
    pallas_call x0 -> x3, Pallas kernels: none -> 31.7 us  [the longest x1 23.9 us: shards(): pl.pallas_call(functools.partial(pair_kernel, min(points, 2048), 4), out_...]
    add x2 -> x0, local copies, waits for them, and re-layouts: 17 us -> none  [smooth_loops(): points = points + SMOOTH_RATE * (behind - 2.0 * points + ahead)]
    all_to_all x1, waiting for transfers between devices: 0.01 us -> 13.5 us  [shards(): parts = lax.all_to_all(part, AXES, split_axis=0, concat_axis=0, tiled=True)]
  transfers between devices with their start and end apart: 2 -> 1, of which waited for: 0 -> 1; matrix products, arithmetic and copies ran while one was open for 12% -> 0% of each run, Pallas kernels for 0% -> 0%
where the time goes in v1:
time: 85 us; the launch traced here: 84.6 us
  blocking collectives  32.8 us (39%)
  Pallas kernels  31.7 us (37%)
  waiting for transfers between devices  13.5 us (16%)
  local copies, waits for them, and re-layouts  3.35 us (4%)
  starting transfers between devices  2.6 us (3%)
    pallas_call x1, Pallas kernels, shards(): pl.pallas_call(functools.partial(pair_kernel, min(points, 2048), 4), out_...  23.9 us
    all_to_all x1, blocking collectives, shards(): lax.all_to_all(outgoing, AXES, split_axis=1, concat_axis=1, tiled=True)  23.5 us
    all_to_all x1, waiting for transfers between devices, shards(): parts = lax.all_to_all(part, AXES, split_axis=0, concat_axis=0, tiled=True)  13.5 us
    all_to_all x1, blocking collectives, shards(): lax.all_to_all(velocity.reshape(3, devices, share), AXES, split_axis=1, c...  9.31 us
    pallas_call x1, Pallas kernels, shards(): pl.pallas_call(functools.partial(prep_kernel, cap), out_shape=(shape((dev...  4.13 us
    pallas_call x1, Pallas kernels, shards(): pl.pallas_call(functools.partial(owner_kernel, cap, scale), out_shape=(sh...  3.6 us
    unnamed x9, local copies, waits for them, and re-layouts  2.93 us
    all_to_all x1, starting transfers between devices, shards(): parts = lax.all_to_all(part, AXES, split_axis=0, concat_axis=0, tiled=True)  2.6 us
  transfers between devices with their start and end apart: 1, of which 1 were waited for; matrix products, arithmetic and copies ran while one was open for 0% of the time, Pallas kernels for 0%

profile of v1, /device:TPU:0, one launch (start us, length us, event | category | flops | bytes accessed | tf_op | source)
XLA Modules:
  0.0 84.6 jit_solution(16308793881417531166)
XLA Ops:
  0.6 0.0 copy-start.3
  0.6 0.7 copy-done.3
  1.3 0.0 copy-start
  1.3 0.9 %copy-done = f32[3,128,128]{2,1,0:T(8,128)S(1)} copy-done((f32[3,128,128]{2,1,0:T(8,128)S(1)}, f32[3,128,128]{2,1,0:T(8,128)}, u32[]{:S(2)}) %copy-start) | copy-done | bytes 196632
  2.2 0.0 copy-start.1
  2.3 0.8 copy-done.1
  3.0 4.1 %prep.1 = (f32[32,24,128]{2,1,0:T(8,128)}, f32[3,256,128]{2,1,0:T(8,128)S(1)}, bf16[32,16384]{1,0:T(8,128)(2,1)S(1)}, bf16[16,16384]{1,0:T(8,128)(2,1)S(1)}) custom-call(s32[1]{0:T(128)} %bitcast.me_ref, f32[3,128,128]{2,1,0:T(8,128)S(1)} %copy-done, s32[2,4096]{1,0:T(2,128)S(1)} %copy-done.1, s32[4,256]{1,0:T(4,128)S(1)} %copy-done.3), custom_call_target="tpu_custom_call" | custom-call | tf_op jit(solution)/shard_map/prep/pallas_call | solution.py:306
  7.1 0.3 copy.6
  7.4 23.5 %all_to_all.15 = f32[3,256,128]{2,0,1:T(4,128)S(1)} all-to-all(f32[3,256,128]{2,0,1:T(4,128)S(1)} %copy.6), channel_id=1, replica_groups=mesh['row'=4,'col'=8] {'row','col'}, dimensions={1} | all-to-all | bytes 786432 | tf_op jit(solution)/shard_map/all_to_all | solution.py:324
  30.9 2.6 %all-to-all-start.1 = ((f32[32,24,128]{2,1,0:T(8,128)}), f32[32,24,128]{2,1,0:T(8,128)S(1)}, u32[]{:S(2)}, u32[]{:S(2)}) async-start(f32[32,24,128]{2,1,0:T(8,128)} %get-tuple-element.12), calls=%async_computation.1 | async-start | bytes 786432 | tf_op jit(solution)/shard_map/all_to_all | solution.py:323
  33.5 13.5 %all-to-all-done.1.part_ref = f32[32,24,128]{2,1,0:T(8,128)S(1)} async-done(((f32[32,24,128]{2,1,0:T(8,128)}), f32[32,24,128]{2,1,0:T(8,128)S(1)}, u32[]{:S(2)}, u32[]{:S(2)}) %all-to-all-start.1) | async-done | bytes 393248 | tf_op jit(solution)/shard_map/all_to_all | solution.py:323
  47.0 0.0 copy-start.2
  47.0 23.9 %pairs.1 = (f32[16,1024]{1,0:T(8,128)S(1)}, bf16[32,1024]{1,0:T(8,128)(2,1)S(1)}, f32[3,1024]{1,0:T(4,128)S(1)}) custom-call(f32[32,24,128]{2,1,0:T(8,128)S(1)} %all-to-all-done.1.part_ref, bf16[32,16384]{1,0:T(8,128)(2,1)S(1)} %get-tuple-element.13.near_ref, bf16[16,16384]{1,0:T(8,128)(2,1)S(1)} %get-tuple-element.14.sums_ref), custom_call_target="tpu_custom_call" | custom-call | tf_op jit(solution)/shard_map/pairs/pallas_call | solution.py:325
  71.0 0.0 copy-done.2
  71.0 3.6 %owners.1 = (f32[3,256,128]{2,1,0:T(8,128)}, f32[3,1024]{1,0:T(4,128)S(1)}) custom-call(s32[1]{0:T(128)} %bitcast.me_ref, s32[2,4096]{1,0:T(2,128)S(1)} %copy-done.2, f32[3,256,128]{2,1,0:T(8,128)S(1)} %copy.7.arrived_ref, bf16[32,1024]{1,0:T(8,128)(2,1)S(1)} %get-tuple-element.15.side_ref, f32[3,1024]{1,0:T(4,128)S(1)} %get-tuple-element.16.target_ref, ...), custom_call_target="tpu_custom_call" | custom-call | tf_op jit(solution)/shard_map/owners/pallas_call | solution.py:338
  74.6 0.1 reshape.11
  74.7 9.3 %all_to_all.16 = f32[3,32,32]{2,0,1:T(4,128)S(1)} all-to-all(f32[3,32,32]{2,0,1:T(4,128)S(1)} %copy.8), channel_id=1, replica_groups=mesh['row'=4,'col'=8] {'row','col'}, dimensions={1} | all-to-all | bytes 24576 | tf_op jit(solution)/shard_map/all_to_all | solution.py:352
  84.1 0.6 copy.9
  (3 shorter events, 0.1 us)
Async XLA Ops:
  0.6 0.7 copy-start.3
  1.3 0.9 %copy-start = (f32[3,128,128]{2,1,0:T(8,128)S(1)}, f32[3,128,128]{2,1,0:T(8,128)}, u32[]{:S(2)}) copy-start(f32[3,128,128]{2,1,0:T(8,128)} %pos_ref.1) | copy-start | bytes 589828
  2.2 0.8 copy-start.1
  30.9 16.1 %all-to-all-start.1 = ((f32[32,24,128]{2,1,0:T(8,128)}), f32[32,24,128]{2,1,0:T(8,128)S(1)}, u32[]{:S(2)}, u32[]{:S(2)}) async-start(f32[32,24,128]{2,1,0:T(8,128)} %get-tuple-element.12), calls=%async_computation.1 | async-start | bytes 786432 | tf_op jit(solution)/shard_map/all_to_all | solution.py:323
  47.0 23.9 %copy-start.2 = (s32[2,4096]{1,0:T(2,128)S(1)}, s32[2,4096]{1,0:T(2,128)}, u32[]{:S(2)}) copy-start(s32[2,4096]{1,0:T(2,128)} %links_ref.3) | copy-start | bytes 98308

commit v2 on v1

v2 whole, which is shorter than its diff:
```python
import functools
import math

import jax
import jax.numpy as jnp
from jax import lax
from jax.experimental import pallas as pl
from jax.experimental.pallas import tpu as pltpu
from jax.sharding import PartitionSpec as P

CORE_SQUARED = 0.01
F32 = jnp.float32
BF16 = jnp.bfloat16
LANES = 128
LANE_BITS = 7
DEPTH = 32
FEATS = 16
EDGES = 5
AXES = ("row", "col")


def iota(shape, dim):
    return lax.broadcasted_iota(jnp.int32, shape, dim)


def three_parts(value):
    first = value.astype(BF16)
    rest = value - first.astype(F32)
    second = rest.astype(BF16)
    third = (rest - second.astype(F32)).astype(BF16)
    return (first, second, third)


def dot(left, right):
    return jnp.dot(left, right, preferred_element_type=F32)


def pick(onehot, value):
    first, second, third = three_parts(value)
    return dot(onehot, first) + dot(onehot, second) + dot(onehot, third)


def as_columns(row):
    return jnp.transpose(jnp.broadcast_to(row.astype(F32), (LANES, row.shape[1])))


def shifted(value, steps):
    return pltpu.roll(value, (-steps) % LANES, 1)


def five_taps(far_left, left, here, right, far_right):
    return (far_left + far_right + 4.0 * (left + right) + 6.0 * here) * 0.0625


def cross(left_vec, right_vec):
    return [
        left_vec[1] * right_vec[2] - left_vec[2] * right_vec[1],
        left_vec[2] * right_vec[0] - left_vec[0] * right_vec[2],
        left_vec[0] * right_vec[1] - left_vec[1] * right_vec[0],
    ]


def source_rows(here, ahead, keep=None):
    segment = [a - h for a, h in zip(ahead, here)]
    centre = [0.5 * (a + h) for a, h in zip(ahead, here)]
    if keep is not None:
        segment = [jnp.where(keep, s, 0.0) for s in segment]
    near = []
    for value in centre:
        one, two, three = [part.astype(F32) for part in three_parts(value)]
        near += [one, two, three, one, two, one]
    norm = centre[0] * centre[0] + centre[1] * centre[1] + centre[2] * centre[2]
    near += [part.astype(F32) for part in three_parts(norm)]
    near += [jnp.ones_like(norm)] * 3
    terms = segment + cross(segment, centre)
    tops = [value.astype(BF16).astype(F32) for value in terms]
    sums = tops + [value - top for value, top in zip(terms, tops)]
    return near, sums


def target_rows(targets):
    rows = []
    for value in targets:
        one, two, three = [part.astype(F32) for part in three_parts(-2.0 * value)]
        rows += [one, one, one, two, two, three]
    norm = targets[0] * targets[0] + targets[1] * targets[1] + targets[2] * targets[2]
    rows += [jnp.ones_like(norm)] * 3
    rows += [part.astype(F32) for part in three_parts(norm + CORE_SQUARED)]
    return rows


def pair_sums(near, sums, target_side):
    squared = lax.dot_general(
        near, target_side, (((0,), (0,)), ((), ())), preferred_element_type=F32
    )
    root = lax.rsqrt(squared)
    weight = root * root * root
    top = weight.astype(BF16)
    rest = (weight - top.astype(F32)).astype(BF16)
    return dot(sums, top) + dot(sums, rest)


def my_place():
    return lax.axis_index("row") * lax.axis_size("col") + lax.axis_index("col")


def fetch(pairs, sems):
    copies = [
        pltpu.make_async_copy(source, target, sems.at[k]) for k, (source, target) in enumerate(pairs)
    ]
    for copy in copies:
        copy.start()
    for copy in copies:
        copy.wait()


def target_kernel(pos_hbm, links_hbm, panel_hbm, keep_ref, send_ref, pos_ref, links_ref, panel_ref, sems):
    fetch([(pos_hbm, pos_ref), (links_hbm, links_ref), (panel_hbm, panel_ref)], sems)
    blocks = pos_ref.shape[1]
    total = links_ref.shape[1]
    base = my_place() * blocks
    mine = pl.ds(pl.multiple_of(base, LANES), blocks)
    lane = iota((blocks, LANES), 1)
    ids = iota((blocks, LANES), 0) + base

    wanted = jnp.concatenate([panel_ref[r : r + 1, :] for r in range(panel_ref.shape[0])], axis=1)
    count = wanted.shape[1]
    wanted_block = lax.shift_right_logical(wanted, LANE_BITS)
    wanted_point = jnp.bitwise_and(wanted, LANES - 1)

    follow_col = as_columns(links_ref[1:2, mine]).astype(jnp.int32)[:, :1]
    found = jnp.zeros((blocks, LANES), F32)
    lane_f = lane.astype(F32)
    for r in range(total // LANES):
        row = links_ref[1:2, r * LANES : (r + 1) * LANES]
        found = found + jnp.where(row == ids, lane_f + float(r * LANES), 0.0)
    precede_col = jnp.sum(found, axis=1, keepdims=True).astype(jnp.int32)

    held_here = wanted_block == (iota((blocks, count), 0) + base)
    before = jnp.logical_and(wanted_point < 2, follow_col == wanted_block)
    after = jnp.logical_and(wanted_point >= LANES - 2, precede_col == wanted_block)
    onehot = jnp.concatenate(
        [
            jnp.where(held_here, 1.0, 0.0).astype(BF16),
            jnp.where(jnp.logical_or(before, after), 1.0, 0.0).astype(BF16),
        ],
        axis=0,
    )

    stacked = []
    for c in range(3):
        x = pos_ref[c]
        rolled = {s: shifted(x, s) for s in (-2, -1, 1, 2)}
        inner = {
            s: jnp.where((lane >= -s) if s < 0 else (lane < LANES - s), v, 0.0)
            for s, v in rolled.items()
        }
        outer = {s: rolled[s] - inner[s] for s in rolled}
        own = five_taps(inner[-2], inner[-1], x, inner[1], inner[2])
        other = five_taps(outer[-2], outer[-1], 0.0, outer[1], outer[2])
        stacked.append(jnp.transpose(jnp.concatenate([own, other], axis=0)))
    one, two, three = three_parts(jnp.concatenate(stacked, axis=0))
    values = dot(one, onehot) + dot(two, onehot) + dot(three, onehot)
    at_point = iota((LANES, count), 0) == wanted_point
    even = lax.rem(lax.axis_index("col"), 2) == 0
    half = count // 2
    per = half // LANES
    for c in range(3):
        part = jnp.where(at_point, values[c * LANES : (c + 1) * LANES], 0.0)
        row = jnp.sum(part, axis=0, keepdims=True)
        for i in range(per):
            low = row[:, i * LANES : (i + 1) * LANES]
            high = row[:, half + i * LANES : half + (i + 1) * LANES]
            at = slice(c * per + i, c * per + i + 1)
            keep_ref[at, :] = jnp.where(even, low, high)
            send_ref[at, :] = jnp.where(even, high, low)


def owner_links(cap, held, me, links_ref, owner_scr, follow_scr):
    devices = owner_scr.shape[0]
    for r in range(devices):
        owner_scr[r : r + 1, :] = links_ref[0:1, r * LANES : (r + 1) * LANES]
        follow_scr[r : r + 1, :] = links_ref[1:2, r * LANES : (r + 1) * LANES]
    owned = jnp.where(owner_scr[...] == me, 1.0, 0.0)
    upper = jnp.where(iota((LANES, LANES), 0) < iota((LANES, LANES), 1), 1.0, 0.0)
    rank = dot(owned.astype(BF16), upper.astype(BF16))
    follow = follow_scr[...]
    table = jnp.concatenate(
        [
            owned,
            rank,
            lax.shift_right_logical(follow, LANE_BITS).astype(F32),
            jnp.bitwise_and(follow, LANES - 1).astype(F32),
        ],
        axis=1,
    ).astype(BF16)
    cap_shift = cap.bit_length() - 1
    slot = iota((held, devices), 0)
    spread = jnp.where(
        lax.shift_right_logical(slot, cap_shift) == iota((held, devices), 1), 1.0, 0.0
    ).astype(BF16)
    wide = dot(spread, table)
    slots = iota((held, LANES), 0)
    seat = jnp.bitwise_and(slots, cap - 1).astype(F32)
    hit = jnp.logical_and(wide[:, :LANES] == 1.0, wide[:, LANES : 2 * LANES] == seat)
    number = (lax.shift_right_logical(slots, cap_shift) * LANES + iota((held, LANES), 1)).astype(F32)
    target_no = wide[:, 2 * LANES : 3 * LANES] * float(LANES) + wide[:, 3 * LANES :]
    live = jnp.sum(jnp.where(hit, 1.0, 0.0), axis=1, keepdims=True)
    id_col = jnp.sum(jnp.where(hit, number, 0.0), axis=1, keepdims=True) + live - 1.0
    next_col = jnp.sum(jnp.where(hit, target_no, 0.0), axis=1, keepdims=True) + 2.0 * live - 2.0
    id_row = jnp.transpose(jnp.broadcast_to(id_col, (held, LANES)))[:1, :]
    next_row = jnp.transpose(jnp.broadcast_to(next_col, (held, LANES)))[:1, :]
    to_next = jnp.where(next_col == id_row, 1.0, 0.0).astype(BF16)
    to_prev = jnp.where(id_col == next_row, 1.0, 0.0).astype(BF16)
    return to_next, to_prev


def source_kernel(cap, pos_ref, links_ref, out_ref, near_ref, sums_ref, next_ref, prev_ref, near_scr, sums_scr, owner_scr, follow_scr):
    me = my_place()
    blocks = pos_ref.shape[1]
    devices = out_ref.shape[0]
    held = devices * cap
    mine = pl.ds(pl.multiple_of(me * blocks, LANES), blocks)
    lane = iota((blocks, LANES), 1)

    owner_row = links_ref[0:1, mine]
    owner_col = as_columns(owner_row).astype(jnp.int32)
    same = jnp.logical_and(owner_col == owner_row, iota((blocks, blocks), 0) < iota((blocks, blocks), 1))
    rank = jnp.sum(jnp.where(same, 1.0, 0.0), axis=0, keepdims=True).astype(jnp.int32)
    slot = owner_row * cap + rank
    into = jnp.where(iota((held, blocks), 0) == slot, 1.0, 0.0).astype(BF16)
    here_all = []
    for c in range(3):
        x = pos_ref[c]
        placed = pick(into, x)
        for d in range(devices):
            out_ref[d, c * cap : (c + 1) * cap, :] = placed[d * cap : (d + 1) * cap, :]
        here_all.append(five_taps(shifted(x, -2), shifted(x, -1), x, shifted(x, 1), shifted(x, 2)))

    ahead_all = [shifted(v, 1) for v in here_all]
    keep = jnp.logical_and(lane >= 2, lane <= LANES - 4)
    near, sums = source_rows(here_all, ahead_all, keep)
    near_scr[...] = jnp.zeros_like(near_scr)
    sums_scr[...] = jnp.zeros_like(sums_scr)
    for k, value in enumerate(near):
        near_scr[pl.ds(k, blocks, stride=DEPTH), :] = value
    for k, value in enumerate(sums):
        sums_scr[pl.ds(k, blocks, stride=FEATS), :] = value
    for b in range(blocks):
        near_ref[:, b * LANES : (b + 1) * LANES] = near_scr[b * DEPTH : (b + 1) * DEPTH, :].astype(BF16)
        sums_ref[:, b * LANES : (b + 1) * LANES] = sums_scr[b * FEATS : (b + 1) * FEATS, :].astype(BF16)
    next_ref[...], prev_ref[...] = owner_links(cap, held, me, links_ref, owner_scr, follow_scr)


def pair_kernel(tile, parts, part_ref, near_ref, sums_ref, acc_ref, side_ref, target_ref, rows_scr):
    halves = []
    for h in range(2):
        added = part_ref[h]
        for d in range(h + 2, part_ref.shape[0], 2):
            added = added + part_ref[d]
        halves.append(added)
    per = part_ref.shape[1] // 3
    targets = [
        jnp.concatenate([v[c * per + i : c * per + i + 1, :] for v in halves for i in range(per)], axis=1)
        for c in range(3)
    ]
    rows_scr[...] = jnp.zeros_like(rows_scr)
    for c in range(3):
        target_ref[c : c + 1, :] = targets[c]
    for k, row in enumerate(target_rows(targets)):
        rows_scr[k : k + 1, :] = row
    side_ref[...] = rows_scr[...].astype(BF16)
    count = side_ref.shape[1]
    piece = tile // parts

    def one_tile(turn, running):
        result = []
        for s in range(parts):
            at = pl.ds(pl.multiple_of(turn * tile + s * piece, piece), piece)
            result.append(running[s] + pair_sums(near_ref[:, at], sums_ref[:, at], side_ref[...]))
        return tuple(result)

    zeros = tuple(jnp.zeros((FEATS, count), F32) for s in range(parts))
    running = lax.fori_loop(0, near_ref.shape[1] // tile, one_tile, zeros)
    acc_ref[...] = sum(running[1:], running[0])


def held_blocks(cap, arrived_ref, x_scr):
    for c in range(3):
        for d in range(arrived_ref.shape[0]):
            x_scr[c, d * cap : (d + 1) * cap, :] = arrived_ref[d, c * cap : (c + 1) * cap, :]


def pick_rows(rows, onehot):
    filled = jnp.concatenate([rows, jnp.zeros((16 - rows.shape[0], rows.shape[1]), F32)], axis=0)
    parts = dot(jnp.concatenate(three_parts(filled), axis=0), onehot)
    return parts[:16] + parts[16:32] + parts[32:]


def taps_down(rows):
    n = rows.shape[0] - 4
    return five_taps(*[rows[k : k + n] for k in range(5)])


def end_kernel(cap, scale, arrived_ref, next_ref, prev_ref, side_ref, target_ref, acc_ref, vel_ref, x_scr, near_scr, sums_scr):
    held_blocks(cap, arrived_ref, x_scr)
    held = x_scr.shape[1]
    turned = [jnp.transpose(x_scr[c]) for c in range(3)]
    after = pick_rows(jnp.concatenate([t[:3] for t in turned], axis=0), prev_ref[...])
    before = pick_rows(jnp.concatenate([t[LANES - 2 :] for t in turned], axis=0), next_ref[...])
    here = []
    ahead = []
    for c in range(3):
        first = taps_down(jnp.concatenate([before[2 * c : 2 * c + 2], turned[c][:5]], axis=0))
        last = taps_down(jnp.concatenate([turned[c][LANES - 5 :], after[3 * c : 3 * c + 3]], axis=0))
        here.append(jnp.concatenate([first[:2], last[:3]], axis=0))
        ahead.append(jnp.concatenate([first[1:], last[1:]], axis=0))
    near, sums = source_rows(here, ahead)
    near_scr[...] = jnp.zeros_like(near_scr)
    sums_scr[...] = jnp.zeros_like(sums_scr)
    for k, value in enumerate(near):
        for e in range(EDGES):
            near_scr[k : k + 1, e * held : (e + 1) * held] = value[e : e + 1, :]
    for k, value in enumerate(sums):
        for e in range(EDGES):
            sums_scr[k : k + 1, e * held : (e + 1) * held] = value[e : e + 1, :]
    acc = acc_ref[...] + pair_sums(near_scr[...].astype(BF16), sums_scr[...].astype(BF16), side_ref[...])
    terms = acc[0:6] + acc[6:12]
    targets = [target_ref[c : c + 1, :] for c in range(3)]
    turned = cross([terms[c : c + 1, :] for c in range(3)], targets)
    for c in range(3):
        vel_ref[c : c + 1, :] = scale * (turned[c] - terms[3 + c : 4 + c, :])


def smooth_kernel(cap, arrived_ref, next_ref, prev_ref, smooth_ref, x_scr):
    held_blocks(cap, arrived_ref, x_scr)
    held = x_scr.shape[1]
    lane = iota((held, LANES), 1)
    blocks = jnp.concatenate([x_scr[c] for c in range(3)], axis=1)
    around = pick(jnp.concatenate([next_ref[...], prev_ref[...]], axis=0), blocks)
    for c in range(3):
        x = x_scr[c]
        after = around[:held, c * LANES : (c + 1) * LANES]
        before = around[held:, c * LANES : (c + 1) * LANES]
        at = [jnp.where(lane < s, shifted(before, -s), shifted(x, -s)) for s in (2, 1)]
        at.append(x)
        at += [jnp.where(lane >= LANES - s, shifted(after, s), shifted(x, s)) for s in (1, 2)]
        smooth_ref[c] = five_taps(*at)


def shards(positions, block_links, panel_points):
    devices = lax.axis_size(AXES)
    blocks = positions.shape[1]
    cap = 2 * blocks // devices
    held = devices * cap
    total = block_links.shape[1]
    points = blocks * LANES
    panel = panel_points.shape[1]
    count = panel_points.shape[0] * panel
    share = panel // lax.axis_size("col")
    scale = 1.0 / (math.pi * math.sqrt(total * LANES))
    vmem = pl.BlockSpec(memory_space=pltpu.VMEM)
    params = pltpu.CompilerParams(vmem_limit_bytes=40 << 20)
    shape = jax.ShapeDtypeStruct
    rows = 3 * count // LANES

    anywhere = pl.BlockSpec(memory_space=pltpu.HBM)
    keep, send = pl.pallas_call(
        target_kernel,
        out_shape=(shape((rows // 2, LANES), F32), shape((rows // 2, LANES), F32)),
        in_specs=[anywhere] * 3,
        out_specs=[vmem] * 2,
        scratch_shapes=[
            pltpu.VMEM(positions.shape, F32),
            pltpu.VMEM(block_links.shape, jnp.int32),
            pltpu.VMEM(panel_points.shape, jnp.int32),
            pltpu.SemaphoreType.DMA((3,)),
        ],
        compiler_params=pltpu.CompilerParams(vmem_limit_bytes=32 << 20),
        name="targets",
    )(*[pltpu.with_memory_space_constraint(v, pltpu.HBM) for v in (positions, block_links, panel_points)])
    other = [(k, k ^ 1) for k in range(lax.axis_size("col"))]
    chip_part = keep + lax.ppermute(send, "col", other)
    part = jnp.broadcast_to(chip_part[None], (devices, rows // 2, LANES))
    parts = lax.all_to_all(part, AXES, split_axis=0, concat_axis=0, tiled=True)
    outgoing, near, sums, to_next, to_prev = pl.pallas_call(
        functools.partial(source_kernel, cap),
        out_shape=(
            shape((devices, 3 * cap, LANES), F32),
            shape((DEPTH, points), BF16),
            shape((FEATS, points), BF16),
            shape((held, held), BF16),
            shape((held, held), BF16),
        ),
        in_specs=[vmem] * 2,
        out_specs=[vmem] * 5,
        scratch_shapes=[
            pltpu.VMEM((blocks * DEPTH, LANES), F32),
            pltpu.VMEM((blocks * FEATS, LANES), F32),
            pltpu.VMEM((devices, LANES), jnp.int32),
            pltpu.VMEM((devices, LANES), jnp.int32),
        ],
        compiler_params=params,
        cost_estimate=pl.CostEstimate(flops=10**9, bytes_accessed=10**7, transcendentals=0),
        name="sources",
    )(positions, block_links)

    arrived = lax.all_to_all(outgoing, AXES, split_axis=0, concat_axis=0, tiled=True)
    acc, side, targets = pl.pallas_call(
        functools.partial(pair_kernel, min(points, 4096), 8),
        out_shape=(
            shape((FEATS, count), F32),
            shape((DEPTH, count), BF16),
            shape((3, count), F32),
        ),
        in_specs=[vmem] * 3,
        out_specs=[vmem] * 3,
        scratch_shapes=[pltpu.VMEM((DEPTH, count), F32)],
        compiler_params=params,
        cost_estimate=pl.CostEstimate(
            flops=2 * points * count * 40, bytes_accessed=10**7, transcendentals=points * count
        ),
        name="pairs",
    )(parts, near, sums)
    velocity = pl.pallas_call(
        functools.partial(end_kernel, cap, scale),
        out_shape=shape((3, count), F32),
        in_specs=[vmem] * 6,
        out_specs=vmem,
        scratch_shapes=[
            pltpu.VMEM((3, held, LANES), F32),
            pltpu.VMEM((DEPTH, EDGES * held), F32),
            pltpu.VMEM((FEATS, EDGES * held), F32),
        ],
        compiler_params=params,
        name="ends",
    )(arrived, to_next, to_prev, side, targets, acc)
    smoothed = pl.pallas_call(
        functools.partial(smooth_kernel, cap),
        out_shape=shape((3, held, LANES), F32),
        in_specs=[vmem] * 3,
        out_specs=vmem,
        scratch_shapes=[pltpu.VMEM((3, held, LANES), F32)],
        compiler_params=params,
        cost_estimate=pl.CostEstimate(flops=10**9, bytes_accessed=10**7, transcendentals=0),
        name="smooth",
    )(arrived, to_next, to_prev)
    shares = lax.all_to_all(
        velocity.reshape(3, devices, share), AXES, split_axis=1, concat_axis=1, tiled=True
    )
    return (smoothed, jnp.sum(shares, axis=1)[None])


def solution(mesh):
    placed = (P(None, AXES, None), P(), P())
    return jax.shard_map(
        shards,
        mesh=mesh,
        in_specs=placed,
        out_specs=(P(None, AXES, None), P("row", None, "col")),
        check_vma=False,
    )
```

time: 85 us -> 65.8 us (0.77)
  blocking collectives: 32.8 us -> 0 us
  starting transfers between devices: 2.6 us -> 16.1 us
  local copies, waits for them, and re-layouts: 3.35 us -> 2.04 us
  Pallas kernels: 31.7 us -> 32.8 us
    all_to_all x2 -> x0, blocking collectives: 32.8 us -> none  [the longest x1 23.5 us: shards(): lax.all_to_all(outgoing, AXES, split_axis=1, concat_axis=1, tiled=True)]
    all_to_all x0 -> x2, starting transfers between devices: none -> 8.43 us  [the longest x1 5.83 us: shards(): lax.all_to_all(velocity.reshape(3, devices, share), AXES, split_axis=1, c...]
    all_to_all x1, waiting for transfers between devices: 13.5 us -> 7.35 us  [shards(): parts = lax.all_to_all(part, AXES, split_axis=0, concat_axis=0, tiled=True)]
    all_to_all x0 -> x2, waiting for transfers between devices: none -> 5.56 us  [the longest x1 5.55 us: shards(): lax.all_to_all(velocity.reshape(3, devices, share), AXES, split_axis=1, c...]
    all_to_all x1, starting transfers between devices: 2.6 us -> 7.19 us  [shards(): parts = lax.all_to_all(part, AXES, split_axis=0, concat_axis=0, tiled=True)]
    unnamed x9 -> x5, local copies, waits for them, and re-layouts: 2.93 us -> 0.57 us
    pallas_call x3 -> x5, Pallas kernels: 31.7 us -> 32.8 us  [the longest x1 23.3 us: shards(): pl.pallas_call(functools.partial(pair_kernel, min(points, 4096), 8), out_...]
  transfers between devices with their start and end apart: 1 -> 4, of which waited for: 1 -> 3; matrix products, arithmetic and copies ran while one was open for 0% -> 0% of each run, Pallas kernels for 0% -> 43%
where the time goes in v2:
time: 65.8 us; the launch traced here: 65.4 us
  Pallas kernels  32.8 us (50%)
  starting transfers between devices  16.1 us (24%)
  waiting for transfers between devices  13.7 us (21%)
  local copies, waits for them, and re-layouts  2.04 us (3%)
  between operations  0.7 us (1%)
    pallas_call x1, Pallas kernels, shards(): pl.pallas_call(functools.partial(pair_kernel, min(points, 4096), 8), out_...  23.3 us
    all_to_all x1, waiting for transfers between devices, shards(): parts = lax.all_to_all(part, AXES, split_axis=0, concat_axis=0, tiled=True)  7.35 us
    all_to_all x1, starting transfers between devices, shards(): parts = lax.all_to_all(part, AXES, split_axis=0, concat_axis=0, tiled=True)  7.19 us
    all_to_all x1, starting transfers between devices, shards(): lax.all_to_all(velocity.reshape(3, devices, share), AXES, split_axis=1, c...  5.83 us
    all_to_all x1, waiting for transfers between devices, shards(): lax.all_to_all(velocity.reshape(3, devices, share), AXES, split_axis=1, c...  5.55 us
    pallas_call x1, Pallas kernels, shards(): pl.pallas_call(functools.partial(source_kernel, cap), out_shape=(shape((d...  3.02 us
    all_to_all x1, starting transfers between devices, shards(): lax.all_to_all(outgoing, AXES, split_axis=0, concat_axis=0, tiled=True)  2.6 us
    pallas_call x1, Pallas kernels, shards(): pl.pallas_call(target_kernel, out_shape=(shape((rows // 2, LANES), F32),...  2.43 us
  transfers between devices with their start and end apart: 4, of which 3 were waited for; matrix products, arithmetic and copies ran while one was open for 0% of the time, Pallas kernels for 43%

profile of v2, /device:TPU:0, one launch (start us, length us, event | category | flops | bytes accessed | tf_op | source)
XLA Modules:
  0.0 65.4 jit_solution(10833513432268308830)
XLA Ops:
  0.6 2.4 %targets.1 = (f32[12,128]{1,0:T(8,128)S(1)}, f32[12,128]{1,0:T(8,128)S(1)}) custom-call(f32[3,128,128]{2,1,0:T(8,128)} %pos_hbm.1, s32[2,4096]{1,0:T(2,128)} %links_hbm.1, s32[4,256]{1,0:T(4,128)} %panel_hbm.1), custom_call_target="tpu_custom_call" | custom-call | tf_op jit(solution)/shard_map/targets/pallas_call | solution.py:368
  3.1 0.5 collective-permute-start
  3.6 0.8 %collective-permute-done = f32[12,128]{1,0:T(8,128)S(1)} collective-permute-done((f32[12,128]{1,0:T(8,128)S(1)}, f32[12,128]{1,0:T(8,128)S(1)}, u32[]{:S(2)}, u32[]{:S(2)}) %collective-permute-start) | collective-permute-done | bytes 6176 | tf_op jit(solution)/shard_map/ppermute | solution.py:383
  4.4 0.7 %broadcast_in_dim.4 = f32[32,12,128]{2,1,0:T(8,128)} broadcast(f32[12,128]{1,0:T(8,128)S(1)} %add.3), dimensions={1,2} | broadcast | bytes 202752 | tf_op jit(solution)/shard_map/broadcast_in_dim | solution.py:384
  5.1 0.0 copy-start
  5.1 0.0 copy-start.1
  5.1 7.2 %all-to-all-start.1 = ((f32[32,12,128]{2,1,0:T(8,128)}), f32[32,12,128]{2,1,0:T(8,128)S(1)}, u32[]{:S(2)}, u32[]{:S(2)}) async-start(f32[32,12,128]{2,1,0:T(8,128)} %broadcast_in_dim.4), calls=%async_computation.1 | async-start | bytes 524288 | tf_op jit(solution)/shard_map/all_to_all | solution.py:385
  12.3 0.0 copy-done
  12.4 0.0 copy-done.1
  12.4 3.0 %sources.1 = (f32[32,24,128]{2,1,0:T(8,128)}, bf16[32,16384]{1,0:T(8,128)(2,1)S(1)}, bf16[16,16384]{1,0:T(8,128)(2,1)S(1)}, bf16[256,256]{1,0:T(8,128)(2,1)S(1)}, bf16[256,256]{1,0:T(8,128)(2,1)S(1)}) custom-call(f32[3,128,128]{2,1,0:T(8,128)S(1)} %copy-done, s32[2,4096]{1,0:T(2,128)S(1)} %copy-done.1), custom_call_target="tpu_custom_call" | custom-call | flops 1000000000 | bytes 10000000 | tf_op jit(solution)/shard_map/sources/pallas_call | solution.py:386
  15.4 7.3 %all-to-all-done.1.part_ref = f32[32,12,128]{2,1,0:T(8,128)S(1)} async-done(((f32[32,12,128]{2,1,0:T(8,128)}), f32[32,12,128]{2,1,0:T(8,128)S(1)}, u32[]{:S(2)}, u32[]{:S(2)}) %all-to-all-start.1) | async-done | bytes 196640 | tf_op jit(solution)/shard_map/all_to_all | solution.py:385
  22.7 2.6 %all-to-all-start = ((f32[32,24,128]{2,1,0:T(8,128)}), f32[32,24,128]{2,1,0:T(8,128)S(1)}, u32[]{:S(2)}, u32[]{:S(2)}) async-start(f32[32,24,128]{2,1,0:T(8,128)} %get-tuple-element.12), calls=%async_computation | async-start | bytes 786432 | tf_op jit(solution)/shard_map/all_to_all | solution.py:408
  25.3 23.3 %pairs.1 = (f32[16,1024]{1,0:T(8,128)S(1)}, bf16[32,1024]{1,0:T(8,128)(2,1)S(1)}, f32[3,1024]{1,0:T(4,128)S(1)}) custom-call(f32[32,12,128]{2,1,0:T(8,128)S(1)} %all-to-all-done.1.part_ref, bf16[32,16384]{1,0:T(8,128)(2,1)S(1)} %get-tuple-element.17.near_ref, bf16[16,16384]{1,0:T(8,128)(2,1)S(1)} %get-tuple-element.18.sums_ref), custom_call_target="tpu_custom_call" | custom-call | flops 1342177280 | bytes 10000000 | tf_op jit(solution)/shard_map/pairs/pallas_call | solution.py:409
  48.6 0.0 all-to-all-done.arrived_ref
  48.6 2.2 %ends.1 = f32[3,1024]{1,0:T(4,128)S(1)} custom-call(f32[32,24,128]{2,1,0:T(8,128)S(1)} %all-to-all-done.arrived_ref, bf16[256,256]{1,0:T(8,128)(2,1)S(1)} %get-tuple-element.13.next_ref, bf16[256,256]{1,0:T(8,128)(2,1)S(1)} %get-tuple-element.14.prev_ref, bf16[32,1024]{1,0:T(8,128)(2,1)S(1)} %get-tuple-element.19.side_ref, ...), custom_call_target="tpu_custom_call" | custom-call | tf_op jit(solution)/shard_map/ends/pallas_call | solution.py:425
  50.8 0.1 reshape.8
  50.9 0.7 %copy.6 = f32[3,32,32]{2,0,1:T(4,128)} copy(f32[3,32,32]{2,1,0:T(8,128)S(1)} %reshape.8) | data formatting | bytes 24576 | tf_op jit(solution)/shard_map/reshape | solution.py:449
  51.6 5.8 %all-to-all-start.2 = ((f32[3,32,32]{2,0,1:T(4,128)}), f32[3,32,32]{2,0,1:T(4,128)S(1)}, u32[]{:S(2)}, u32[]{:S(2)}) async-start(f32[3,32,32]{2,0,1:T(4,128)} %copy.6), calls=%async_computation.2 | async-start | bytes 131072 | tf_op jit(solution)/shard_map/all_to_all | solution.py:448
  57.4 1.8 %smooth.1 = f32[3,256,128]{2,1,0:T(8,128)} custom-call(f32[32,24,128]{2,1,0:T(8,128)S(1)} %all-to-all-done.arrived_ref, bf16[256,256]{1,0:T(8,128)(2,1)S(1)} %get-tuple-element.13.next_ref, bf16[256,256]{1,0:T(8,128)(2,1)S(1)} %get-tuple-element.14.prev_ref), custom_call_target="tpu_custom_call" | custom-call | flops 1000000000 | bytes 10000000 | tf_op jit(solution)/shard_map/smooth/pallas_call | solution.py:438
  59.2 5.6 %all-to-all-done.2 = f32[3,32,32]{2,0,1:T(4,128)S(1)} async-done(((f32[3,32,32]{2,0,1:T(4,128)}), f32[3,32,32]{2,0,1:T(4,128)S(1)}, u32[]{:S(2)}, u32[]{:S(2)}) %all-to-all-start.2) | async-done | bytes 12320 | tf_op jit(solution)/shard_map/all_to_all | solution.py:448
  64.8 0.6 copy.7
  (2 shorter events, 0.0 us)
Async XLA Ops:
  3.1 1.3 %collective-permute-start = (f32[12,128]{1,0:T(8,128)S(1)}, f32[12,128]{1,0:T(8,128)S(1)}, u32[]{:S(2)}, u32[]{:S(2)}) collective-permute-start(f32[12,128]{1,0:T(8,128)S(1)} %get-tuple-element.16), channel_id=1, source_target_pairs={{0,1},{1,0},{2,3},{3,2},{4,5},{5,4},{6,7},{7,6},{8,9},{9,8},{10,11... | collective-permute-start | bytes 18440 | tf_op jit(solution)/shard_map/ppermute | solution.py:383
  5.1 7.2 %copy-start = (f32[3,128,128]{2,1,0:T(8,128)S(1)}, f32[3,128,128]{2,1,0:T(8,128)}, u32[]{:S(2)}) copy-start(f32[3,128,128]{2,1,0:T(8,128)} %pos_hbm.1) | copy-start | bytes 589828
  5.1 7.2 %copy-start.1 = (s32[2,4096]{1,0:T(2,128)S(1)}, s32[2,4096]{1,0:T(2,128)}, u32[]{:S(2)}) copy-start(s32[2,4096]{1,0:T(2,128)} %links_hbm.1) | copy-start | bytes 98308
  5.1 17.6 %all-to-all-start.1 = ((f32[32,12,128]{2,1,0:T(8,128)}), f32[32,12,128]{2,1,0:T(8,128)S(1)}, u32[]{:S(2)}, u32[]{:S(2)}) async-start(f32[32,12,128]{2,1,0:T(8,128)} %broadcast_in_dim.4), calls=%async_computation.1 | async-start | bytes 524288 | tf_op jit(solution)/shard_map/all_to_all | solution.py:385
  22.7 25.9 %all-to-all-start = ((f32[32,24,128]{2,1,0:T(8,128)}), f32[32,24,128]{2,1,0:T(8,128)S(1)}, u32[]{:S(2)}, u32[]{:S(2)}) async-start(f32[32,24,128]{2,1,0:T(8,128)} %get-tuple-element.12), calls=%async_computation | async-start | bytes 786432 | tf_op jit(solution)/shard_map/all_to_all | solution.py:408
  51.6 13.2 %all-to-all-start.2 = ((f32[3,32,32]{2,0,1:T(4,128)}), f32[3,32,32]{2,0,1:T(4,128)S(1)}, u32[]{:S(2)}, u32[]{:S(2)}) async-start(f32[3,32,32]{2,0,1:T(4,128)} %copy.6), calls=%async_computation.2 | async-start | bytes 131072 | tf_op jit(solution)/shard_map/all_to_all | solution.py:448

commit v3 on v2

--- a/solution.py
+++ b/solution.py
@@ -89,7 +89,7 @@
     return rows
 
 
-def pair_sums(near, sums, target_side):
+def pair_sums(start, near, sums, target_side):
     squared = lax.dot_general(
         near, target_side, (((0,), (0,)), ((), ())), preferred_element_type=F32
     )
@@ -97,7 +97,7 @@
     weight = root * root * root
     top = weight.astype(BF16)
     rest = (weight - top.astype(F32)).astype(BF16)
-    return dot(sums, top) + dot(sums, rest)
+    return start + dot(sums, top) + dot(sums, rest)
 
 
 def my_place():
@@ -114,7 +114,7 @@
         copy.wait()
 
 
-def target_kernel(pos_hbm, links_hbm, panel_hbm, keep_ref, send_ref, pos_ref, links_ref, panel_ref, sems):
+def target_kernel(pos_hbm, links_hbm, panel_hbm, part_ref, pos_ref, links_ref, panel_ref, sems):
     fetch([(pos_hbm, pos_ref), (links_hbm, links_ref), (panel_hbm, panel_ref)], sems)
     blocks = pos_ref.shape[1]
     total = links_ref.shape[1]
@@ -162,18 +162,12 @@
     one, two, three = three_parts(jnp.concatenate(stacked, axis=0))
     values = dot(one, onehot) + dot(two, onehot) + dot(three, onehot)
     at_point = iota((LANES, count), 0) == wanted_point
-    even = lax.rem(lax.axis_index("col"), 2) == 0
-    half = count // 2
-    per = half // LANES
+    per = count // LANES
     for c in range(3):
         part = jnp.where(at_point, values[c * LANES : (c + 1) * LANES], 0.0)
         row = jnp.sum(part, axis=0, keepdims=True)
         for i in range(per):
-            low = row[:, i * LANES : (i + 1) * LANES]
-            high = row[:, half + i * LANES : half + (i + 1) * LANES]
-            at = slice(c * per + i, c * per + i + 1)
-            keep_ref[at, :] = jnp.where(even, low, high)
-            send_ref[at, :] = jnp.where(even, high, low)
+            part_ref[c * per + i : c * per + i + 1, :] = row[:, i * LANES : (i + 1) * LANES]
 
 
 def owner_links(cap, held, me, links_ref, owner_scr, follow_scr):
@@ -253,15 +247,9 @@
 
 
 def pair_kernel(tile, parts, part_ref, near_ref, sums_ref, acc_ref, side_ref, target_ref, rows_scr):
-    halves = []
-    for h in range(2):
-        added = part_ref[h]
-        for d in range(h + 2, part_ref.shape[0], 2):
-            added = added + part_ref[d]
-        halves.append(added)
-    per = part_ref.shape[1] // 3
+    per = part_ref.shape[0] // 3
     targets = [
-        jnp.concatenate([v[c * per + i : c * per + i + 1, :] for v in halves for i in range(per)], axis=1)
+        jnp.concatenate([part_ref[c * per + i : c * per + i + 1, :] for i in range(per)], axis=1)
         for c in range(3)
     ]
     rows_scr[...] = jnp.zeros_like(rows_scr)
@@ -274,15 +262,14 @@
     piece = tile // parts
 
     def one_tile(turn, running):
-        result = []
         for s in range(parts):
             at = pl.ds(pl.multiple_of(turn * tile + s * piece, piece), piece)
-            result.append(running[s] + pair_sums(near_ref[:, at], sums_ref[:, at], side_ref[...]))
-        return tuple(result)
-
-    zeros = tuple(jnp.zeros((FEATS, count), F32) for s in range(parts))
-    running = lax.fori_loop(0, near_ref.shape[1] // tile, one_tile, zeros)
-    acc_ref[...] = sum(running[1:], running[0])
+            running = pair_sums(running, near_ref[:, at], sums_ref[:, at], side_ref[...])
+        return running
+
+    acc_ref[...] = lax.fori_loop(
+        0, near_ref.shape[1] // tile, one_tile, jnp.zeros((FEATS, count), F32)
+    )
 
 
 def held_blocks(cap, arrived_ref, x_scr):
@@ -324,12 +311,16 @@
     for k, value in enumerate(sums):
         for e in range(EDGES):
             sums_scr[k : k + 1, e * held : (e + 1) * held] = value[e : e + 1, :]
-    acc = acc_ref[...] + pair_sums(near_scr[...].astype(BF16), sums_scr[...].astype(BF16), side_ref[...])
+    acc = pair_sums(acc_ref[...], near_scr[...].astype(BF16), sums_scr[...].astype(BF16), side_ref[...])
     terms = acc[0:6] + acc[6:12]
     targets = [target_ref[c : c + 1, :] for c in range(3)]
     turned = cross([terms[c : c + 1, :] for c in range(3)], targets)
-    for c in range(3):
-        vel_ref[c : c + 1, :] = scale * (turned[c] - terms[3 + c : 4 + c, :])
+    velocity = jnp.concatenate(
+        [scale * (turned[c] - terms[3 + c : 4 + c, :]) for c in range(3)], axis=0
+    )
+    share = vel_ref.shape[2]
+    for d in range(vel_ref.shape[0]):
+        vel_ref[d] = velocity[:, d * share : (d + 1) * share]
 
 
 def smooth_kernel(cap, arrived_ref, next_ref, prev_ref, smooth_ref, x_scr):
@@ -346,6 +337,11 @@
         at.append(x)
         at += [jnp.where(lane >= LANES - s, shifted(after, s), shifted(x, s)) for s in (1, 2)]
         smooth_ref[c] = five_taps(*at)
+
+
+def swapped(value, axis, steps):
+    size = lax.axis_size(axis)
+    return [lax.ppermute(value, axis, [(k, k ^ step) for k in range(size)]) for step in steps]
 
 
 def shards(positions, block_links, panel_points):
@@ -365,11 +361,11 @@
     rows = 3 * count // LANES
 
     anywhere = pl.BlockSpec(memory_space=pltpu.HBM)
-    keep, send = pl.pallas_call(
+    part = pl.pallas_call(
         target_kernel,
-        out_shape=(shape((rows // 2, LANES), F32), shape((rows // 2, LANES), F32)),
+        out_shape=shape((rows, LANES), F32),
         in_specs=[anywhere] * 3,
-        out_specs=[vmem] * 2,
+        out_specs=vmem,
         scratch_shapes=[
             pltpu.VMEM(positions.shape, F32),
             pltpu.VMEM(block_links.shape, jnp.int32),
@@ -379,10 +375,9 @@
         compiler_params=pltpu.CompilerParams(vmem_limit_bytes=32 << 20),
         name="targets",
     )(*[pltpu.with_memory_space_constraint(v, pltpu.HBM) for v in (positions, block_links, panel_points)])
-    other = [(k, k ^ 1) for k in range(lax.axis_size("col"))]
-    chip_part = keep + lax.ppermute(send, "col", other)
-    part = jnp.broadcast_to(chip_part[None], (devices, rows // 2, LANES))
-    parts = lax.all_to_all(part, AXES, split_axis=0, concat_axis=0, tiled=True)
+    part = part + swapped(part, "col", [1])[0]
+    part, positions = lax.optimization_barrier((part, positions))
+    part = sum(swapped(part, "row", range(1, lax.axis_size("row"))), part)
     outgoing, near, sums, to_next, to_prev = pl.pallas_call(
         functools.partial(source_kernel, cap),
         out_shape=(
@@ -405,9 +400,12 @@
         name="sources",
     )(positions, block_links)
 
+    outgoing, part = lax.optimization_barrier((outgoing, part))
+    near_by = part + swapped(part, "col", [2])[0]
+    parts = near_by + swapped(near_by, "col", [4])[0]
     arrived = lax.all_to_all(outgoing, AXES, split_axis=0, concat_axis=0, tiled=True)
     acc, side, targets = pl.pallas_call(
-        functools.partial(pair_kernel, min(points, 4096), 8),
+        functools.partial(pair_kernel, min(points, 8192), 16),
         out_shape=(
             shape((FEATS, count), F32),
             shape((DEPTH, count), BF16),
@@ -418,13 +416,13 @@
         scratch_shapes=[pltpu.VMEM((DEPTH, count), F32)],
         compiler_params=params,
         cost_estimate=pl.CostEstimate(
-            flops=2 * points * count * 40, bytes_accessed=10**7, transcendentals=points * count
+            flops=2 * points * count * 1000, bytes_accessed=10**7, transcendentals=0
         ),
         name="pairs",
     )(parts, near, sums)
     velocity = pl.pallas_call(
         functools.partial(end_kernel, cap, scale),
-        out_shape=shape((3, count), F32),
+        out_shape=shape((devices, 3, share), F32),
         in_specs=[vmem] * 6,
         out_specs=vmem,
         scratch_shapes=[
@@ -445,10 +443,8 @@
         cost_estimate=pl.CostEstimate(flops=10**9, bytes_accessed=10**7, transcendentals=0),
         name="smooth",
     )(arrived, to_next, to_prev)
-    shares = lax.all_to_all(
-        velocity.reshape(3, devices, share), AXES, split_axis=1, concat_axis=1, tiled=True
-    )
-    return (smoothed, jnp.sum(shares, axis=1)[None])
+    shares = lax.all_to_all(velocity, AXES, split_axis=0, concat_axis=0, tiled=True)
+    return (smoothed, jnp.sum(shares, axis=0)[None])
 
 
 def solution(mesh):

time: 65.8 us -> 58.8 us (0.89)
  waiting for transfers between devices: 13.7 us -> 10.1 us
  Pallas kernels: 32.8 us -> 29.4 us
  starting transfers between devices: 16.1 us -> 17.7 us
  local copies, waits for them, and re-layouts: 2.04 us -> 0.58 us
    ppermute x1 -> x6, starting transfers between devices: 0.52 us -> 9.09 us  [swapped(): lax.ppermute(value, axis, [(k, k ^ step) for k in range(size)])]
    all_to_all x2 -> x1, starting transfers between devices: 13 us -> 5.66 us  [shards(): lax.all_to_all(velocity, AXES, split_axis=0, concat_axis=0, tiled=True)]
    all_to_all x2 -> x1, waiting for transfers between devices: 12.9 us -> 5.55 us  [shards(): lax.all_to_all(velocity, AXES, split_axis=0, concat_axis=0, tiled=True)]
    pallas_call x2, Pallas kernels: 25.7 us -> 21.6 us  [the longest x1 19.1 us: shards(): pl.pallas_call(functools.partial(pair_kernel, min(points, 8192), 16), out...]
    ppermute x1 -> x6, waiting for transfers between devices: 0.83 us -> 4.51 us  [swapped(): lax.ppermute(value, axis, [(k, k ^ step) for k in range(size)])]
    pallas_call x1, Pallas kernels: 2.19 us -> 2.94 us  [shards(): pl.pallas_call(functools.partial(end_kernel, cap, scale), out_shape=shape...]
    reshape x2 -> x0, local copies, waits for them, and re-layouts: 0.74 us -> none  [shards(): velocity.reshape(3, devices, share)]
    broadcast_in_dim x1 -> x0, local copies, waits for them, and re-layouts: 0.72 us -> none  [shards(): part = jnp.broadcast_to(chip_part[None], (devices, rows // 2, LANES))]
  transfers between devices with their start and end apart: 4 -> 8, of which waited for: 3 -> 4; matrix products, arithmetic and copies ran while one was open for 0% -> 0% of each run, Pallas kernels for 43% -> 41%
where the time goes in v3:
time: 58.8 us; the launch traced here: 58.5 us
  Pallas kernels  29.4 us (50%)
  starting transfers between devices  17.7 us (30%)
  waiting for transfers between devices  10.1 us (17%)
  between operations  0.7 us (1%)
    pallas_call x1, Pallas kernels, shards(): pl.pallas_call(functools.partial(pair_kernel, min(points, 8192), 16), out...  19.1 us
    ppermute x6, starting transfers between devices, swapped(): lax.ppermute(value, axis, [(k, k ^ step) for k in range(size)])  9.09 us
    all_to_all x1, starting transfers between devices, shards(): lax.all_to_all(velocity, AXES, split_axis=0, concat_axis=0, tiled=True)  5.66 us
    all_to_all x1, waiting for transfers between devices, shards(): lax.all_to_all(velocity, AXES, split_axis=0, concat_axis=0, tiled=True)  5.55 us
    ppermute x6, waiting for transfers between devices, swapped(): lax.ppermute(value, axis, [(k, k ^ step) for k in range(size)])  4.51 us
    pallas_call x1, Pallas kernels, shards(): pl.pallas_call(functools.partial(source_kernel, cap), out_shape=(shape((d...  3.02 us
    all_to_all x1, starting transfers between devices, shards(): lax.all_to_all(outgoing, AXES, split_axis=0, concat_axis=0, tiled=True)  2.94 us
    pallas_call x1, Pallas kernels, shards(): pl.pallas_call(functools.partial(end_kernel, cap, scale), out_shape=shape...  2.94 us
  transfers between devices with their start and end apart: 8, of which 4 were waited for; matrix products, arithmetic and copies ran while one was open for 0% of the time, Pallas kernels for 41%

profile of v3, /device:TPU:0, one launch (start us, length us, event | category | flops | bytes accessed | tf_op | source)
XLA Modules:
  0.0 58.5 jit_solution(13938470080328216167)
XLA Ops:
  0.6 0.0 copy-start
  0.6 2.5 %targets.1 = f32[24,128]{1,0:T(8,128)S(1)} custom-call(f32[3,128,128]{2,1,0:T(8,128)} %pos_ref, s32[2,4096]{1,0:T(2,128)} %links_ref.1, s32[4,256]{1,0:T(4,128)} %panel_hbm.1), custom_call_target="tpu_custom_call" | custom-call | tf_op jit(solution)/shard_map/targets/pallas_call | solution.py:364
  3.1 0.0 copy-start.1
  3.2 0.5 collective-permute-start
  3.7 0.8 %collective-permute-done = f32[24,128]{1,0:T(8,128)S(1)} collective-permute-done((f32[24,128]{1,0:T(8,128)S(1)}, f32[24,128]{1,0:T(8,128)S(1)}, u32[]{:S(2)}, u32[]{:S(2)}) %collective-permute-start) | collective-permute-done | bytes 12320 | tf_op jit(solution)/shard_map/ppermute | solution.py:344
  4.5 2.8 %collective-permute-start.1 = (f32[24,128]{1,0:T(8,128)S(1)}, f32[24,128]{1,0:T(8,128)S(1)}, u32[]{:S(2)}, u32[]{:S(2)}) collective-permute-start(f32[24,128]{1,0:T(8,128)S(1)} %add.18), channel_id=1, source_target_pairs={{0,8},{8,0},{16,24},{24,16},{1,9},{9,1},{17,25},{25,17},{2,10},{10... | collective-permute-start | bytes 36872 | tf_op jit(solution)/shard_map/ppermute | solution.py:344
  7.3 1.5 %collective-permute-start.2 = (f32[24,128]{1,0:T(8,128)S(1)}, f32[24,128]{1,0:T(8,128)S(1)}, u32[]{:S(2)}, u32[]{:S(2)}) collective-permute-start(f32[24,128]{1,0:T(8,128)S(1)} %add.18), channel_id=1, source_target_pairs={{0,16},{8,24},{16,0},{24,8},{1,17},{9,25},{17,1},{25,9},{2,18},{10... | collective-permute-start | bytes 36872 | tf_op jit(solution)/shard_map/ppermute | solution.py:344
  8.9 0.0 collective-permute-start.3
  8.9 0.0 copy-done
  8.9 0.0 copy-done.1
  8.9 3.0 %sources.1 = (f32[32,24,128]{2,1,0:T(8,128)}, bf16[32,16384]{1,0:T(8,128)(2,1)S(1)}, bf16[16,16384]{1,0:T(8,128)(2,1)S(1)}, bf16[256,256]{1,0:T(8,128)(2,1)S(1)}, bf16[256,256]{1,0:T(8,128)(2,1)S(1)}) custom-call(f32[3,128,128]{2,1,0:T(8,128)S(1)} %copy-done, s32[2,4096]{1,0:T(2,128)S(1)} %copy-done.1), custom_call_target="tpu_custom_call" | custom-call | flops 1000000000 | bytes 10000000 | tf_op jit(solution)/shard_map/sources/pallas_call | solution.py:381
  11.9 0.0 collective-permute-done.1
  11.9 0.0 collective-permute-done.2
  11.9 1.6 %collective-permute-done.3 = f32[24,128]{1,0:T(8,128)S(1)} collective-permute-done((f32[24,128]{1,0:T(8,128)S(1)}, f32[24,128]{1,0:T(8,128)S(1)}, u32[]{:S(2)}, u32[]{:S(2)}) %collective-permute-start.3) | collective-permute-done | bytes 12320 | tf_op jit(solution)/shard_map/ppermute | solution.py:344
  13.5 1.6 %collective-permute-start.4 = (f32[24,128]{1,0:T(8,128)S(1)}, f32[24,128]{1,0:T(8,128)S(1)}, u32[]{:S(2)}, u32[]{:S(2)}) collective-permute-start(f32[24,128]{1,0:T(8,128)S(1)} %add_add_fusion), channel_id=1, source_target_pairs={{0,2},{1,3},{2,0},{3,1},{4,6},{5,7},{6,4},{7,5},{8,10},{9,11},{10,... | collective-permute-start | bytes 36872 | tf_op jit(solution)/shard_map/ppermute | solution.py:344
  15.0 2.1 %collective-permute-done.4 = f32[24,128]{1,0:T(8,128)S(1)} collective-permute-done((f32[24,128]{1,0:T(8,128)S(1)}, f32[24,128]{1,0:T(8,128)S(1)}, u32[]{:S(2)}, u32[]{:S(2)}) %collective-permute-start.4) | collective-permute-done | bytes 12320 | tf_op jit(solution)/shard_map/ppermute | solution.py:344
  17.2 2.6 %collective-permute-start.5 = (f32[24,128]{1,0:T(8,128)S(1)}, f32[24,128]{1,0:T(8,128)S(1)}, u32[]{:S(2)}, u32[]{:S(2)}) collective-permute-start(f32[24,128]{1,0:T(8,128)S(1)} %add.22), channel_id=1, source_target_pairs={{0,4},{1,5},{2,6},{3,7},{4,0},{5,1},{6,2},{7,3},{8,12},{9,13},{10,... | collective-permute-start | bytes 36872 | tf_op jit(solution)/shard_map/ppermute | solution.py:344
  19.8 2.9 %all-to-all-start = ((f32[32,24,128]{2,1,0:T(8,128)}), f32[32,24,128]{2,1,0:T(8,128)S(1)}, u32[]{:S(2)}, u32[]{:S(2)}) async-start(f32[32,24,128]{2,1,0:T(8,128)} %get-tuple-element.17), calls=%async_computation | async-start | bytes 786432 | tf_op jit(solution)/shard_map/all_to_all | solution.py:406
  22.8 0.0 collective-permute-done.5
  22.8 19.1 %pairs.1 = (f32[16,1024]{1,0:T(8,128)S(1)}, bf16[32,1024]{1,0:T(8,128)(2,1)S(1)}, f32[3,1024]{1,0:T(4,128)S(1)}) custom-call(f32[24,128]{1,0:T(8,128)S(1)} %add.23.part_ref, bf16[32,16384]{1,0:T(8,128)(2,1)S(1)} %get-tuple-element.21.near_ref, bf16[16,16384]{1,0:T(8,128)(2,1)S(1)} %get-tuple-element.22.sums_ref), custom_call_target="tpu_custom_call" | custom-call | flops 33554432000 | bytes 10000000 | tf_op jit(solution)/shard_map/pairs/pallas_call | solution.py:407
  41.9 0.0 all-to-all-done.arrived_ref
  41.9 2.9 %ends.1 = f32[32,3,32]{2,1,0:T(4,128)} custom-call(f32[32,24,128]{2,1,0:T(8,128)S(1)} %all-to-all-done.arrived_ref, bf16[256,256]{1,0:T(8,128)(2,1)S(1)} %get-tuple-element.18.next_ref, bf16[256,256]{1,0:T(8,128)(2,1)S(1)} %get-tuple-element.19.prev_ref, bf16[32,1024]{1,0:T(8,128)(2,1)S(1)} %get-tuple-element.23.side_ref, ...), custom_call_target="tpu_custom_call" | custom-call | tf_op jit(solution)/shard_map/ends/pallas_call | solution.py:423
  44.8 5.7 %all-to-all-start.1 = ((f32[32,3,32]{2,1,0:T(4,128)}), f32[32,3,32]{2,1,0:T(4,128)S(1)}, u32[]{:S(2)}, u32[]{:S(2)}) async-start(f32[32,3,32]{2,1,0:T(4,128)} %ends.1), calls=%async_computation.1 | async-start | bytes 131072 | tf_op jit(solution)/shard_map/all_to_all | solution.py:446
  50.5 1.8 %smooth.1 = f32[3,256,128]{2,1,0:T(8,128)} custom-call(f32[32,24,128]{2,1,0:T(8,128)S(1)} %all-to-all-done.arrived_ref, bf16[256,256]{1,0:T(8,128)(2,1)S(1)} %get-tuple-element.18.next_ref, bf16[256,256]{1,0:T(8,128)(2,1)S(1)} %get-tuple-element.19.prev_ref), custom_call_target="tpu_custom_call" | custom-call | flops 1000000000 | bytes 10000000 | tf_op jit(solution)/shard_map/smooth/pallas_call | solution.py:436
  52.3 5.6 %all-to-all-done.1 = f32[32,3,32]{2,1,0:T(4,128)S(1)} async-done(((f32[32,3,32]{2,1,0:T(4,128)}), f32[32,3,32]{2,1,0:T(4,128)S(1)}, u32[]{:S(2)}, u32[]{:S(2)}) %all-to-all-start.1) | async-done | bytes 12320 | tf_op jit(solution)/shard_map/all_to_all | solution.py:446
  57.9 0.6 copy.5
  (5 shorter events, 0.1 us)
Async XLA Ops:
  0.6 8.2 %copy-start = (f32[3,128,128]{2,1,0:T(8,128)S(1)}, f32[3,128,128]{2,1,0:T(8,128)}, u32[]{:S(2)}) copy-start(f32[3,128,128]{2,1,0:T(8,128)} %pos_ref) | copy-start | bytes 589828
  3.1 5.7 %copy-start.1 = (s32[2,4096]{1,0:T(2,128)S(1)}, s32[2,4096]{1,0:T(2,128)}, u32[]{:S(2)}) copy-start(s32[2,4096]{1,0:T(2,128)} %links_ref.1) | copy-start | bytes 98308
  3.2 1.4 %collective-permute-start = (f32[24,128]{1,0:T(8,128)S(1)}, f32[24,128]{1,0:T(8,128)S(1)}, u32[]{:S(2)}, u32[]{:S(2)}) collective-permute-start(f32[24,128]{1,0:T(8,128)S(1)} %targets.1), channel_id=1, source_target_pairs={{0,1},{1,0},{2,3},{3,2},{4,5},{5,4},{6,7},{7,6},{8,9},{9,8},{10,11... | collective-permute-start | bytes 36872 | tf_op jit(solution)/shard_map/ppermute | solution.py:344
  4.5 7.4 %collective-permute-start.1 = (f32[24,128]{1,0:T(8,128)S(1)}, f32[24,128]{1,0:T(8,128)S(1)}, u32[]{:S(2)}, u32[]{:S(2)}) collective-permute-start(f32[24,128]{1,0:T(8,128)S(1)} %add.18), channel_id=1, source_target_pairs={{0,8},{8,0},{16,24},{24,16},{1,9},{9,1},{17,25},{25,17},{2,10},{10... | collective-permute-start | bytes 36872 | tf_op jit(solution)/shard_map/ppermute | solution.py:344
  7.3 4.6 %collective-permute-start.2 = (f32[24,128]{1,0:T(8,128)S(1)}, f32[24,128]{1,0:T(8,128)S(1)}, u32[]{:S(2)}, u32[]{:S(2)}) collective-permute-start(f32[24,128]{1,0:T(8,128)S(1)} %add.18), channel_id=1, source_target_pairs={{0,16},{8,24},{16,0},{24,8},{1,17},{9,25},{17,1},{25,9},{2,18},{10... | collective-permute-start | bytes 36872 | tf_op jit(solution)/shard_map/ppermute | solution.py:344
  8.9 4.6 %collective-permute-start.3 = (f32[24,128]{1,0:T(8,128)S(1)}, f32[24,128]{1,0:T(8,128)S(1)}, u32[]{:S(2)}, u32[]{:S(2)}) collective-permute-start(f32[24,128]{1,0:T(8,128)S(1)} %add.18), channel_id=1, source_target_pairs={{0,24},{8,16},{16,8},{24,0},{1,25},{9,17},{17,9},{25,1},{2,26},{10... | collective-permute-start | bytes 36872 | tf_op jit(solution)/shard_map/ppermute | solution.py:344
  13.5 3.7 %collective-permute-start.4 = (f32[24,128]{1,0:T(8,128)S(1)}, f32[24,128]{1,0:T(8,128)S(1)}, u32[]{:S(2)}, u32[]{:S(2)}) collective-permute-start(f32[24,128]{1,0:T(8,128)S(1)} %add_add_fusion), channel_id=1, source_target_pairs={{0,2},{1,3},{2,0},{3,1},{4,6},{5,7},{6,4},{7,5},{8,10},{9,11},{10,... | collective-permute-start | bytes 36872 | tf_op jit(solution)/shard_map/ppermute | solution.py:344
  17.2 5.6 %collective-permute-start.5 = (f32[24,128]{1,0:T(8,128)S(1)}, f32[24,128]{1,0:T(8,128)S(1)}, u32[]{:S(2)}, u32[]{:S(2)}) collective-permute-start(f32[24,128]{1,0:T(8,128)S(1)} %add.22), channel_id=1, source_target_pairs={{0,4},{1,5},{2,6},{3,7},{4,0},{5,1},{6,2},{7,3},{8,12},{9,13},{10,... | collective-permute-start | bytes 36872 | tf_op jit(solution)/shard_map/ppermute | solution.py:344
  19.8 22.0 %all-to-all-start = ((f32[32,24,128]{2,1,0:T(8,128)}), f32[32,24,128]{2,1,0:T(8,128)S(1)}, u32[]{:S(2)}, u32[]{:S(2)}) async-start(f32[32,24,128]{2,1,0:T(8,128)} %get-tuple-element.17), calls=%async_computation | async-start | bytes 786432 | tf_op jit(solution)/shard_map/all_to_all | solution.py:406
  44.8 13.1 %all-to-all-start.1 = ((f32[32,3,32]{2,1,0:T(4,128)}), f32[32,3,32]{2,1,0:T(4,128)S(1)}, u32[]{:S(2)}, u32[]{:S(2)}) async-start(f32[32,3,32]{2,1,0:T(4,128)} %ends.1), calls=%async_computation.1 | async-start | bytes 131072 | tf_op jit(solution)/shard_map/all_to_all | solution.py:446

commit v4 on v3

--- a/solution.py
+++ b/solution.py
@@ -16,6 +16,7 @@
 DEPTH = 32
 FEATS = 16
 EDGES = 5
+EPIECE = 2
 AXES = ("row", "col")
 
 
@@ -104,18 +105,15 @@
     return lax.axis_index("row") * lax.axis_size("col") + lax.axis_index("col")
 
 
-def fetch(pairs, sems):
-    copies = [
-        pltpu.make_async_copy(source, target, sems.at[k]) for k, (source, target) in enumerate(pairs)
-    ]
-    for copy in copies:
-        copy.start()
-    for copy in copies:
-        copy.wait()
-
-
 def target_kernel(pos_hbm, links_hbm, panel_hbm, part_ref, pos_ref, links_ref, panel_ref, sems):
-    fetch([(pos_hbm, pos_ref), (links_hbm, links_ref), (panel_hbm, panel_ref)], sems)
+    links_in = pltpu.make_async_copy(links_hbm, links_ref, sems.at[0])
+    panel_in = pltpu.make_async_copy(panel_hbm, panel_ref, sems.at[1])
+    pos_in = pltpu.make_async_copy(pos_hbm, pos_ref, sems.at[2])
+    links_in.start()
+    panel_in.start()
+    pos_in.start()
+    links_in.wait()
+    panel_in.wait()
     blocks = pos_ref.shape[1]
     total = links_ref.shape[1]
     base = my_place() * blocks
@@ -147,6 +145,7 @@
         axis=0,
     )
 
+    pos_in.wait()
     stacked = []
     for c in range(3):
         x = pos_ref[c]
@@ -209,41 +208,43 @@
     return to_next, to_prev
 
 
-def source_kernel(cap, pos_ref, links_ref, out_ref, near_ref, sums_ref, next_ref, prev_ref, near_scr, sums_scr, owner_scr, follow_scr):
-    me = my_place()
+def owner_kernel(cap, pos_ref, links_ref, out_ref):
     blocks = pos_ref.shape[1]
     devices = out_ref.shape[0]
     held = devices * cap
-    mine = pl.ds(pl.multiple_of(me * blocks, LANES), blocks)
-    lane = iota((blocks, LANES), 1)
-
+    mine = pl.ds(pl.multiple_of(my_place() * blocks, LANES), blocks)
     owner_row = links_ref[0:1, mine]
     owner_col = as_columns(owner_row).astype(jnp.int32)
     same = jnp.logical_and(owner_col == owner_row, iota((blocks, blocks), 0) < iota((blocks, blocks), 1))
     rank = jnp.sum(jnp.where(same, 1.0, 0.0), axis=0, keepdims=True).astype(jnp.int32)
     slot = owner_row * cap + rank
     into = jnp.where(iota((held, blocks), 0) == slot, 1.0, 0.0).astype(BF16)
+    placed = pick(into, jnp.concatenate([pos_ref[c] for c in range(3)], axis=1))
+    for c in range(3):
+        for d in range(devices):
+            out_ref[d, c * cap : (c + 1) * cap, :] = placed[
+                d * cap : (d + 1) * cap, c * LANES : (c + 1) * LANES
+            ]
+
+
+def source_kernel(cap, pos_ref, links_ref, near_ref, sums_ref, next_ref, prev_ref, owner_scr, follow_scr):
+    blocks = pos_ref.shape[1]
+    lane = iota((blocks, LANES), 1)
     here_all = []
     for c in range(3):
         x = pos_ref[c]
-        placed = pick(into, x)
-        for d in range(devices):
-            out_ref[d, c * cap : (c + 1) * cap, :] = placed[d * cap : (d + 1) * cap, :]
         here_all.append(five_taps(shifted(x, -2), shifted(x, -1), x, shifted(x, 1), shifted(x, 2)))
-
     ahead_all = [shifted(v, 1) for v in here_all]
     keep = jnp.logical_and(lane >= 2, lane <= LANES - 4)
     near, sums = source_rows(here_all, ahead_all, keep)
-    near_scr[...] = jnp.zeros_like(near_scr)
-    sums_scr[...] = jnp.zeros_like(sums_scr)
-    for k, value in enumerate(near):
-        near_scr[pl.ds(k, blocks, stride=DEPTH), :] = value
-    for k, value in enumerate(sums):
-        sums_scr[pl.ds(k, blocks, stride=FEATS), :] = value
-    for b in range(blocks):
-        near_ref[:, b * LANES : (b + 1) * LANES] = near_scr[b * DEPTH : (b + 1) * DEPTH, :].astype(BF16)
-        sums_ref[:, b * LANES : (b + 1) * LANES] = sums_scr[b * FEATS : (b + 1) * FEATS, :].astype(BF16)
-    next_ref[...], prev_ref[...] = owner_links(cap, held, me, links_ref, owner_scr, follow_scr)
+    near += [jnp.zeros_like(near[0])] * (DEPTH - len(near))
+    sums += [jnp.zeros_like(sums[0])] * (FEATS - len(sums))
+    for rows, out_ref in ((near, near_ref), (sums, sums_ref)):
+        by_block = jnp.transpose(jnp.stack(rows), (1, 0, 2)).astype(BF16)
+        for b in range(blocks):
+            out_ref[:, b * LANES : (b + 1) * LANES] = by_block[b]
+    held = next_ref.shape[0]
+    next_ref[...], prev_ref[...] = owner_links(cap, held, my_place(), links_ref, owner_scr, follow_scr)
 
 
 def pair_kernel(tile, parts, part_ref, near_ref, sums_ref, acc_ref, side_ref, target_ref, rows_scr):
@@ -289,7 +290,7 @@
     return five_taps(*[rows[k : k + n] for k in range(5)])
 
 
-def end_kernel(cap, scale, arrived_ref, next_ref, prev_ref, side_ref, target_ref, acc_ref, vel_ref, x_scr, near_scr, sums_scr):
+def end_kernel(cap, scale, share, arrived_ref, next_ref, prev_ref, side_ref, target_ref, acc_ref, vel_ref, x_scr, near_scr, sums_scr):
     held_blocks(cap, arrived_ref, x_scr)
     held = x_scr.shape[1]
     turned = [jnp.transpose(x_scr[c]) for c in range(3)]
@@ -311,16 +312,19 @@
     for k, value in enumerate(sums):
         for e in range(EDGES):
             sums_scr[k : k + 1, e * held : (e + 1) * held] = value[e : e + 1, :]
-    acc = pair_sums(acc_ref[...], near_scr[...].astype(BF16), sums_scr[...].astype(BF16), side_ref[...])
+    acc = acc_ref[...]
+    for e in range(0, EDGES * held, EPIECE * held):
+        at = slice(e, min(e + EPIECE * held, EDGES * held))
+        acc = pair_sums(acc, near_scr[:, at].astype(BF16), sums_scr[:, at].astype(BF16), side_ref[...])
     terms = acc[0:6] + acc[6:12]
     targets = [target_ref[c : c + 1, :] for c in range(3)]
     turned = cross([terms[c : c + 1, :] for c in range(3)], targets)
     velocity = jnp.concatenate(
         [scale * (turned[c] - terms[3 + c : 4 + c, :]) for c in range(3)], axis=0
     )
-    share = vel_ref.shape[2]
+    group = LANES // share
     for d in range(vel_ref.shape[0]):
-        vel_ref[d] = velocity[:, d * share : (d + 1) * share]
+        vel_ref[d] = velocity[:, d // group * LANES : (d // group + 1) * LANES]
 
 
 def smooth_kernel(cap, arrived_ref, next_ref, prev_ref, smooth_ref, x_scr):
@@ -375,23 +379,30 @@
         compiler_params=pltpu.CompilerParams(vmem_limit_bytes=32 << 20),
         name="targets",
     )(*[pltpu.with_memory_space_constraint(v, pltpu.HBM) for v in (positions, block_links, panel_points)])
+    part, positions, block_links = lax.optimization_barrier((part, positions, block_links))
+    outgoing = pl.pallas_call(
+        functools.partial(owner_kernel, cap),
+        out_shape=shape((devices, 3 * cap, LANES), F32),
+        in_specs=[vmem] * 2,
+        out_specs=vmem,
+        compiler_params=params,
+        cost_estimate=pl.CostEstimate(flops=10**9, bytes_accessed=10**6, transcendentals=0),
+        name="outgoing",
+    )(positions, block_links)
     part = part + swapped(part, "col", [1])[0]
-    part, positions = lax.optimization_barrier((part, positions))
+    part, positions, outgoing = lax.optimization_barrier((part, positions, outgoing))
     part = sum(swapped(part, "row", range(1, lax.axis_size("row"))), part)
-    outgoing, near, sums, to_next, to_prev = pl.pallas_call(
+    near, sums, to_next, to_prev = pl.pallas_call(
         functools.partial(source_kernel, cap),
         out_shape=(
-            shape((devices, 3 * cap, LANES), F32),
             shape((DEPTH, points), BF16),
             shape((FEATS, points), BF16),
             shape((held, held), BF16),
             shape((held, held), BF16),
         ),
         in_specs=[vmem] * 2,
-        out_specs=[vmem] * 5,
+        out_specs=[vmem] * 4,
         scratch_shapes=[
-            pltpu.VMEM((blocks * DEPTH, LANES), F32),
-            pltpu.VMEM((blocks * FEATS, LANES), F32),
             pltpu.VMEM((devices, LANES), jnp.int32),
             pltpu.VMEM((devices, LANES), jnp.int32),
         ],
@@ -399,10 +410,10 @@
         cost_estimate=pl.CostEstimate(flops=10**9, bytes_accessed=10**7, transcendentals=0),
         name="sources",
     )(positions, block_links)
-
+    near, part = lax.optimization_barrier((near, part))
     outgoing, part = lax.optimization_barrier((outgoing, part))
-    near_by = part + swapped(part, "col", [2])[0]
-    parts = near_by + swapped(near_by, "col", [4])[0]
+    far = swapped(part, "col", range(2, lax.axis_size("col"), 2))
+    parts = sum(far, part)
     arrived = lax.all_to_all(outgoing, AXES, split_axis=0, concat_axis=0, tiled=True)
     acc, side, targets = pl.pallas_call(
         functools.partial(pair_kernel, min(points, 8192), 16),
@@ -421,8 +432,8 @@
         name="pairs",
     )(parts, near, sums)
     velocity = pl.pallas_call(
-        functools.partial(end_kernel, cap, scale),
-        out_shape=shape((devices, 3, share), F32),
+        functools.partial(end_kernel, cap, scale, share),
+        out_shape=shape((devices, 3, LANES), F32),
         in_specs=[vmem] * 6,
         out_specs=vmem,
         scratch_shapes=[
@@ -444,7 +455,9 @@
         name="smooth",
     )(arrived, to_next, to_prev)
     shares = lax.all_to_all(velocity, AXES, split_axis=0, concat_axis=0, tiled=True)
-    return (smoothed, jnp.sum(shares, axis=0)[None])
+    start = my_place() % (LANES // share) * share
+    summed = lax.dynamic_slice_in_dim(jnp.sum(shares, axis=0), start, share, 1)
+    return (smoothed, summed[None])
 
 
 def solution(mesh):

time: 58.8 us -> 57.9 us (0.985)
  Pallas kernels: 29.4 us -> 28.5 us
    all_to_all x1, starting transfers between devices: 2.94 us -> 4.15 us  [shards(): lax.all_to_all(outgoing, AXES, split_axis=0, concat_axis=0, tiled=True)]
    all_to_all x1, starting transfers between devices: 5.66 us -> 4.59 us  [shards(): lax.all_to_all(velocity, AXES, split_axis=0, concat_axis=0, tiled=True)]
    pallas_call x2 -> x3, Pallas kernels: 5.97 us -> 5.13 us  [the longest x1 2.73 us: shards(): pl.pallas_call(functools.partial(end_kernel, cap, scale, share), out_shap...]
    ppermute x6 -> x7, starting transfers between devices: 9.09 us -> 8.95 us  [swapped(): lax.ppermute(value, axis, [(k, k ^ step) for k in range(size)])]
    ppermute x6 -> x7, waiting for transfers between devices: 4.51 us -> 4.43 us  [swapped(): lax.ppermute(value, axis, [(k, k ^ step) for k in range(size)])]
  transfers between devices with their start and end apart: 8 -> 9, of which waited for: 4 -> 4; matrix products, arithmetic and copies ran while one was open for 0% -> 0% of each run, Pallas kernels for 41% -> 40%
where the time goes in v4:
time: 57.9 us; the launch traced here: 57.6 us
  Pallas kernels  28.5 us (49%)
  starting transfers between devices  17.7 us (31%)
  waiting for transfers between devices  9.97 us (17%)
  between operations  0.73 us (1%)
  local copies, waits for them, and re-layouts  0.65 us (1%)
    pallas_call x1, Pallas kernels, shards(): pl.pallas_call(functools.partial(pair_kernel, min(points, 8192), 16), out...  19.1 us
    ppermute x7, starting transfers between devices, swapped(): lax.ppermute(value, axis, [(k, k ^ step) for k in range(size)])  8.95 us
    all_to_all x1, waiting for transfers between devices, shards(): lax.all_to_all(velocity, AXES, split_axis=0, concat_axis=0, tiled=True)  5.54 us
    all_to_all x1, starting transfers between devices, shards(): lax.all_to_all(velocity, AXES, split_axis=0, concat_axis=0, tiled=True)  4.59 us
    ppermute x7, waiting for transfers between devices, swapped(): lax.ppermute(value, axis, [(k, k ^ step) for k in range(size)])  4.43 us
    all_to_all x1, starting transfers between devices, shards(): lax.all_to_all(outgoing, AXES, split_axis=0, concat_axis=0, tiled=True)  4.15 us
    pallas_call x1, Pallas kernels, shards(): pl.pallas_call(functools.partial(end_kernel, cap, scale, share), out_shap...  2.73 us
    pallas_call x1, Pallas kernels, shards(): pl.pallas_call(target_kernel, out_shape=shape((rows, LANES), F32), in_spe...  2.48 us
  transfers between devices with their start and end apart: 9, of which 4 were waited for; matrix products, arithmetic and copies ran while one was open for 0% of the time, Pallas kernels for 40%

profile of v4, /device:TPU:0, one launch (start us, length us, event | category | flops | bytes accessed | tf_op | source)
XLA Modules:
  0.0 57.6 jit_solution(2710656484018859954)
XLA Ops:
  0.6 0.0 copy-start
  0.6 0.0 copy-start.1
  0.6 2.5 %targets.1 = f32[24,128]{1,0:T(8,128)S(1)} custom-call(f32[3,128,128]{2,1,0:T(8,128)} %pos_ref.1, s32[2,4096]{1,0:T(2,128)} %links_ref.1, s32[4,256]{1,0:T(4,128)} %panel_hbm.1), custom_call_target="tpu_custom_call" | custom-call | tf_op jit(solution)/shard_map/targets/pallas_call | solution.py:368
  3.1 0.5 collective-permute-start
  3.7 0.0 copy-done
  3.7 0.0 copy-done.1
  3.7 1.2 %outgoing.1 = f32[32,24,128]{2,1,0:T(8,128)} custom-call(f32[3,128,128]{2,1,0:T(8,128)S(1)} %copy-done, s32[2,4096]{1,0:T(2,128)S(1)} %copy-done.1), custom_call_target="tpu_custom_call" | custom-call | flops 1000000000 | bytes 1000000 | tf_op jit(solution)/shard_map/outgoing/pallas_call | solution.py:383
  4.8 0.0 collective-permute-done
  4.8 2.5 %collective-permute-start.1 = (f32[24,128]{1,0:T(8,128)S(1)}, f32[24,128]{1,0:T(8,128)S(1)}, u32[]{:S(2)}, u32[]{:S(2)}) collective-permute-start(f32[24,128]{1,0:T(8,128)S(1)} %add.31), channel_id=1, source_target_pairs={{0,8},{8,0},{16,24},{24,16},{1,9},{9,1},{17,25},{25,17},{2,10},{10... | collective-permute-start | bytes 36872 | tf_op jit(solution)/shard_map/ppermute | solution.py:348
  7.3 1.5 %collective-permute-start.2 = (f32[24,128]{1,0:T(8,128)S(1)}, f32[24,128]{1,0:T(8,128)S(1)}, u32[]{:S(2)}, u32[]{:S(2)}) collective-permute-start(f32[24,128]{1,0:T(8,128)S(1)} %add.31), channel_id=1, source_target_pairs={{0,16},{8,24},{16,0},{24,8},{1,17},{9,25},{17,1},{25,9},{2,18},{10... | collective-permute-start | bytes 36872 | tf_op jit(solution)/shard_map/ppermute | solution.py:348
  8.9 0.0 collective-permute-start.3
  8.9 1.2 %sources.1 = (bf16[32,16384]{1,0:T(8,128)(2,1)S(1)}, bf16[16,16384]{1,0:T(8,128)(2,1)S(1)}, bf16[256,256]{1,0:T(8,128)(2,1)S(1)}, bf16[256,256]{1,0:T(8,128)(2,1)S(1)}) custom-call(f32[3,128,128]{2,1,0:T(8,128)S(1)} %copy-done, s32[2,4096]{1,0:T(2,128)S(1)} %copy-done.1), custom_call_target="tpu_custom_call" | custom-call | flops 1000000000 | bytes 10000000 | tf_op jit(solution)/shard_map/sources/pallas_call | solution.py:395
  10.1 0.0 collective-permute-done.1
  10.1 0.9 %collective-permute-done.2 = f32[24,128]{1,0:T(8,128)S(1)} collective-permute-done((f32[24,128]{1,0:T(8,128)S(1)}, f32[24,128]{1,0:T(8,128)S(1)}, u32[]{:S(2)}, u32[]{:S(2)}) %collective-permute-start.2) | collective-permute-done | bytes 12320 | tf_op jit(solution)/shard_map/ppermute | solution.py:348
  11.0 2.4 %collective-permute-done.3 = f32[24,128]{1,0:T(8,128)S(1)} collective-permute-done((f32[24,128]{1,0:T(8,128)S(1)}, f32[24,128]{1,0:T(8,128)S(1)}, u32[]{:S(2)}, u32[]{:S(2)}) %collective-permute-start.3) | collective-permute-done | bytes 12320 | tf_op jit(solution)/shard_map/ppermute | solution.py:348
  13.5 1.6 %collective-permute-start.4 = (f32[24,128]{1,0:T(8,128)S(1)}, f32[24,128]{1,0:T(8,128)S(1)}, u32[]{:S(2)}, u32[]{:S(2)}) collective-permute-start(f32[24,128]{1,0:T(8,128)S(1)} %add_add_fusion.1), channel_id=1, source_target_pairs={{0,2},{1,3},{2,0},{3,1},{4,6},{5,7},{6,4},{7,5},{8,10},{9,11},{10,... | collective-permute-start | bytes 36872 | tf_op jit(solution)/shard_map/ppermute | solution.py:348
  15.0 2.6 %collective-permute-start.5 = (f32[24,128]{1,0:T(8,128)S(1)}, f32[24,128]{1,0:T(8,128)S(1)}, u32[]{:S(2)}, u32[]{:S(2)}) collective-permute-start(f32[24,128]{1,0:T(8,128)S(1)} %add_add_fusion.1), channel_id=1, source_target_pairs={{0,4},{1,5},{2,6},{3,7},{4,0},{5,1},{6,2},{7,3},{8,12},{9,13},{10,... | collective-permute-start | bytes 36872 | tf_op jit(solution)/shard_map/ppermute | solution.py:348
  17.6 0.2 collective-permute-start.6
  17.9 4.1 %all-to-all-start = ((f32[32,24,128]{2,1,0:T(8,128)}), f32[32,24,128]{2,1,0:T(8,128)S(1)}, u32[]{:S(2)}, u32[]{:S(2)}) async-start(f32[32,24,128]{2,1,0:T(8,128)} %outgoing.1), calls=%async_computation | async-start | bytes 786432 | tf_op jit(solution)/shard_map/all_to_all | solution.py:417
  22.0 0.0 collective-permute-done.4
  22.0 0.0 collective-permute-done.5
  22.0 1.1 %collective-permute-done.6 = f32[24,128]{1,0:T(8,128)S(1)} collective-permute-done((f32[24,128]{1,0:T(8,128)S(1)}, f32[24,128]{1,0:T(8,128)S(1)}, u32[]{:S(2)}, u32[]{:S(2)}) %collective-permute-start.6) | collective-permute-done | bytes 12320 | tf_op jit(solution)/shard_map/ppermute | solution.py:348
  23.1 19.1 %pairs.1 = (f32[16,1024]{1,0:T(8,128)S(1)}, bf16[32,1024]{1,0:T(8,128)(2,1)S(1)}, f32[3,1024]{1,0:T(4,128)S(1)}) custom-call(f32[24,128]{1,0:T(8,128)S(1)} %add_add_fusion.part_ref, bf16[32,16384]{1,0:T(8,128)(2,1)S(1)} %get-tuple-element.31.near_ref, bf16[16,16384]{1,0:T(8,128)(2,1)S(1)} %get-tuple-element.32.sums_ref), custom_call_target="tpu_custom_call" | custom-call | flops 33554432000 | bytes 10000000 | tf_op jit(solution)/shard_map/pairs/pallas_call | solution.py:418
  42.2 0.0 all-to-all-done.arrived_ref
  42.2 2.7 %ends.1 = f32[32,3,128]{2,1,0:T(4,128)} custom-call(f32[32,24,128]{2,1,0:T(8,128)S(1)} %all-to-all-done.arrived_ref, bf16[256,256]{1,0:T(8,128)(2,1)S(1)} %get-tuple-element.28.next_ref, bf16[256,256]{1,0:T(8,128)(2,1)S(1)} %get-tuple-element.29.prev_ref, bf16[32,1024]{1,0:T(8,128)(2,1)S(1)} %get-tuple-element.33.side_ref, ...), custom_call_target="tpu_custom_call" | custom-call | tf_op jit(solution)/shard_map/ends/pallas_call | solution.py:434
  44.9 4.6 %all-to-all-start.1 = ((f32[32,3,128]{2,1,0:T(4,128)}), f32[32,3,128]{2,1,0:T(4,128)S(1)}, u32[]{:S(2)}, u32[]{:S(2)}) async-start(f32[32,3,128]{2,1,0:T(4,128)} %ends.1), calls=%async_computation.1 | async-start | bytes 131072 | tf_op jit(solution)/shard_map/all_to_all | solution.py:457
  49.5 1.8 %smooth.1 = f32[3,256,128]{2,1,0:T(8,128)} custom-call(f32[32,24,128]{2,1,0:T(8,128)S(1)} %all-to-all-done.arrived_ref, bf16[256,256]{1,0:T(8,128)(2,1)S(1)} %get-tuple-element.28.next_ref, bf16[256,256]{1,0:T(8,128)(2,1)S(1)} %get-tuple-element.29.prev_ref), custom_call_target="tpu_custom_call" | custom-call | flops 1000000000 | bytes 10000000 | tf_op jit(solution)/shard_map/smooth/pallas_call | solution.py:447
  51.4 5.5 %all-to-all-done.1 = f32[32,3,128]{2,1,0:T(4,128)S(1)} async-done(((f32[32,3,128]{2,1,0:T(4,128)}), f32[32,3,128]{2,1,0:T(4,128)S(1)}, u32[]{:S(2)}, u32[]{:S(2)}) %all-to-all-start.1) | async-done | bytes 49184 | tf_op jit(solution)/shard_map/all_to_all | solution.py:457
  57.0 0.1 dynamic-slice_bitcast_fusion
  57.0 0.6 copy.5
  (4 shorter events, 0.1 us)
Async XLA Ops:
  0.6 3.0 %copy-start = (f32[3,128,128]{2,1,0:T(8,128)S(1)}, f32[3,128,128]{2,1,0:T(8,128)}, u32[]{:S(2)}) copy-start(f32[3,128,128]{2,1,0:T(8,128)} %pos_ref.1) | copy-start | bytes 589828
  0.6 3.0 %copy-start.1 = (s32[2,4096]{1,0:T(2,128)S(1)}, s32[2,4096]{1,0:T(2,128)}, u32[]{:S(2)}) copy-start(s32[2,4096]{1,0:T(2,128)} %links_ref.1) | copy-start | bytes 98308
  3.1 1.7 %collective-permute-start = (f32[24,128]{1,0:T(8,128)S(1)}, f32[24,128]{1,0:T(8,128)S(1)}, u32[]{:S(2)}, u32[]{:S(2)}) collective-permute-start(f32[24,128]{1,0:T(8,128)S(1)} %targets.1), channel_id=1, source_target_pairs={{0,1},{1,0},{2,3},{3,2},{4,5},{5,4},{6,7},{7,6},{8,9},{9,8},{10,11... | collective-permute-start | bytes 36872 | tf_op jit(solution)/shard_map/ppermute | solution.py:348
  4.8 5.3 %collective-permute-start.1 = (f32[24,128]{1,0:T(8,128)S(1)}, f32[24,128]{1,0:T(8,128)S(1)}, u32[]{:S(2)}, u32[]{:S(2)}) collective-permute-start(f32[24,128]{1,0:T(8,128)S(1)} %add.31), channel_id=1, source_target_pairs={{0,8},{8,0},{16,24},{24,16},{1,9},{9,1},{17,25},{25,17},{2,10},{10... | collective-permute-start | bytes 36872 | tf_op jit(solution)/shard_map/ppermute | solution.py:348
  7.3 3.7 %collective-permute-start.2 = (f32[24,128]{1,0:T(8,128)S(1)}, f32[24,128]{1,0:T(8,128)S(1)}, u32[]{:S(2)}, u32[]{:S(2)}) collective-permute-start(f32[24,128]{1,0:T(8,128)S(1)} %add.31), channel_id=1, source_target_pairs={{0,16},{8,24},{16,0},{24,8},{1,17},{9,25},{17,1},{25,9},{2,18},{10... | collective-permute-start | bytes 36872 | tf_op jit(solution)/shard_map/ppermute | solution.py:348
  8.9 4.6 %collective-permute-start.3 = (f32[24,128]{1,0:T(8,128)S(1)}, f32[24,128]{1,0:T(8,128)S(1)}, u32[]{:S(2)}, u32[]{:S(2)}) collective-permute-start(f32[24,128]{1,0:T(8,128)S(1)} %add.31), channel_id=1, source_target_pairs={{0,24},{8,16},{16,8},{24,0},{1,25},{9,17},{17,9},{25,1},{2,26},{10... | collective-permute-start | bytes 36872 | tf_op jit(solution)/shard_map/ppermute | solution.py:348
  13.5 8.5 %collective-permute-start.4 = (f32[24,128]{1,0:T(8,128)S(1)}, f32[24,128]{1,0:T(8,128)S(1)}, u32[]{:S(2)}, u32[]{:S(2)}) collective-permute-start(f32[24,128]{1,0:T(8,128)S(1)} %add_add_fusion.1), channel_id=1, source_target_pairs={{0,2},{1,3},{2,0},{3,1},{4,6},{5,7},{6,4},{7,5},{8,10},{9,11},{10,... | collective-permute-start | bytes 36872 | tf_op jit(solution)/shard_map/ppermute | solution.py:348
  15.0 7.0 %collective-permute-start.5 = (f32[24,128]{1,0:T(8,128)S(1)}, f32[24,128]{1,0:T(8,128)S(1)}, u32[]{:S(2)}, u32[]{:S(2)}) collective-permute-start(f32[24,128]{1,0:T(8,128)S(1)} %add_add_fusion.1), channel_id=1, source_target_pairs={{0,4},{1,5},{2,6},{3,7},{4,0},{5,1},{6,2},{7,3},{8,12},{9,13},{10,... | collective-permute-start | bytes 36872 | tf_op jit(solution)/shard_map/ppermute | solution.py:348
  17.6 5.5 %collective-permute-start.6 = (f32[24,128]{1,0:T(8,128)S(1)}, f32[24,128]{1,0:T(8,128)S(1)}, u32[]{:S(2)}, u32[]{:S(2)}) collective-permute-start(f32[24,128]{1,0:T(8,128)S(1)} %add_add_fusion.1), channel_id=1, source_target_pairs={{0,6},{1,7},{2,4},{3,5},{4,2},{5,3},{6,0},{7,1},{8,14},{9,15},{10,... | collective-permute-start | bytes 36872 | tf_op jit(solution)/shard_map/ppermute | solution.py:348
  17.9 24.3 %all-to-all-start = ((f32[32,24,128]{2,1,0:T(8,128)}), f32[32,24,128]{2,1,0:T(8,128)S(1)}, u32[]{:S(2)}, u32[]{:S(2)}) async-start(f32[32,24,128]{2,1,0:T(8,128)} %outgoing.1), calls=%async_computation | async-start | bytes 786432 | tf_op jit(solution)/shard_map/all_to_all | solution.py:417
  44.9 12.0 %all-to-all-start.1 = ((f32[32,3,128]{2,1,0:T(4,128)}), f32[32,3,128]{2,1,0:T(4,128)S(1)}, u32[]{:S(2)}, u32[]{:S(2)}) async-start(f32[32,3,128]{2,1,0:T(4,128)} %ends.1), calls=%async_computation.1 | async-start | bytes 131072 | tf_op jit(solution)/shard_map/all_to_all | solution.py:457

commit v5 on v4

--- a/solution.py
+++ b/solution.py
@@ -16,6 +16,7 @@
 DEPTH = 32
 FEATS = 16
 EDGES = 5
+INNER = LANES - EDGES
 EPIECE = 2
 AXES = ("row", "col")
 
@@ -61,11 +62,9 @@
     ]
 
 
-def source_rows(here, ahead, keep=None):
+def source_rows(here, ahead):
     segment = [a - h for a, h in zip(ahead, here)]
     centre = [0.5 * (a + h) for a, h in zip(ahead, here)]
-    if keep is not None:
-        segment = [jnp.where(keep, s, 0.0) for s in segment]
     near = []
     for value in centre:
         one, two, three = [part.astype(F32) for part in three_parts(value)]
@@ -229,25 +228,26 @@
 
 def source_kernel(cap, pos_ref, links_ref, near_ref, sums_ref, next_ref, prev_ref, owner_scr, follow_scr):
     blocks = pos_ref.shape[1]
-    lane = iota((blocks, LANES), 1)
     here_all = []
     for c in range(3):
         x = pos_ref[c]
         here_all.append(five_taps(shifted(x, -2), shifted(x, -1), x, shifted(x, 1), shifted(x, 2)))
     ahead_all = [shifted(v, 1) for v in here_all]
-    keep = jnp.logical_and(lane >= 2, lane <= LANES - 4)
-    near, sums = source_rows(here_all, ahead_all, keep)
+    near, sums = source_rows(here_all, ahead_all)
     near += [jnp.zeros_like(near[0])] * (DEPTH - len(near))
     sums += [jnp.zeros_like(sums[0])] * (FEATS - len(sums))
     for rows, out_ref in ((near, near_ref), (sums, sums_ref)):
         by_block = jnp.transpose(jnp.stack(rows), (1, 0, 2)).astype(BF16)
         for b in range(blocks):
-            out_ref[:, b * LANES : (b + 1) * LANES] = by_block[b]
+            out_ref[:, b * INNER : (b + 1) * INNER] = by_block[b][:, 2 : 2 + INNER]
+        tail = out_ref.shape[1] - blocks * INNER
+        rest = by_block[0][:, :tail] if out_ref is near_ref else jnp.zeros((FEATS, tail), BF16)
+        out_ref[:, blocks * INNER :] = rest
     held = next_ref.shape[0]
     next_ref[...], prev_ref[...] = owner_links(cap, held, my_place(), links_ref, owner_scr, follow_scr)
 
 
-def pair_kernel(tile, parts, part_ref, near_ref, sums_ref, acc_ref, side_ref, target_ref, rows_scr):
+def pair_kernel(tile, piece, part_ref, near_ref, sums_ref, acc_ref, side_ref, target_ref, rows_scr):
     per = part_ref.shape[0] // 3
     targets = [
         jnp.concatenate([part_ref[c * per + i : c * per + i + 1, :] for i in range(per)], axis=1)
@@ -260,11 +260,11 @@
         rows_scr[k : k + 1, :] = row
     side_ref[...] = rows_scr[...].astype(BF16)
     count = side_ref.shape[1]
-    piece = tile // parts
 
     def one_tile(turn, running):
-        for s in range(parts):
-            at = pl.ds(pl.multiple_of(turn * tile + s * piece, piece), piece)
+        for start in range(0, tile, piece):
+            size = min(piece, tile - start)
+            at = pl.ds(pl.multiple_of(turn * tile + start, LANES), size)
             running = pair_sums(running, near_ref[:, at], sums_ref[:, at], side_ref[...])
         return running
 
@@ -354,7 +354,7 @@
     cap = 2 * blocks // devices
     held = devices * cap
     total = block_links.shape[1]
-    points = blocks * LANES
+    points = -(-blocks * INNER // 512) * 512
     panel = panel_points.shape[1]
     count = panel_points.shape[0] * panel
     share = panel // lax.axis_size("col")
@@ -416,7 +416,7 @@
     parts = sum(far, part)
     arrived = lax.all_to_all(outgoing, AXES, split_axis=0, concat_axis=0, tiled=True)
     acc, side, targets = pl.pallas_call(
-        functools.partial(pair_kernel, min(points, 8192), 16),
+        functools.partial(pair_kernel, points // 2, 512),
         out_shape=(
             shape((FEATS, count), F32),
             shape((DEPTH, count), BF16),

time: 57.9 us -> 57.6 us (level)
  transfers between devices with their start and end apart: 9 -> 9, of which waited for: 4 -> 4; matrix products, arithmetic and copies ran while one was open for 0% -> 0% of each run, Pallas kernels for 40% -> 41%
where the time goes in v5:
time: 57.6 us; the launch traced here: 57.3 us
  Pallas kernels  28.6 us (50%)
  starting transfers between devices  17.7 us (31%)
  waiting for transfers between devices  9.57 us (17%)
  between operations  0.73 us (1%)
  local copies, waits for them, and re-layouts  0.65 us (1%)
    pallas_call x1, Pallas kernels, shards(): pl.pallas_call(functools.partial(pair_kernel, points // 2, 512), out_shap...  18.8 us
    ppermute x7, starting transfers between devices, swapped(): lax.ppermute(value, axis, [(k, k ^ step) for k in range(size)])  8.95 us
    all_to_all x1, waiting for transfers between devices, shards(): lax.all_to_all(velocity, AXES, split_axis=0, concat_axis=0, tiled=True)  5.54 us
    all_to_all x1, starting transfers between devices, shards(): lax.all_to_all(velocity, AXES, split_axis=0, concat_axis=0, tiled=True)  4.59 us
    all_to_all x1, starting transfers between devices, shards(): lax.all_to_all(outgoing, AXES, split_axis=0, concat_axis=0, tiled=True)  4.15 us
    ppermute x7, waiting for transfers between devices, swapped(): lax.ppermute(value, axis, [(k, k ^ step) for k in range(size)])  4.03 us
    pallas_call x1, Pallas kernels, shards(): pl.pallas_call(functools.partial(end_kernel, cap, scale, share), out_shap...  2.73 us
    pallas_call x1, Pallas kernels, shards(): pl.pallas_call(target_kernel, out_shape=shape((rows, LANES), F32), in_spe...  2.48 us
  transfers between devices with their start and end apart: 9, of which 4 were waited for; matrix products, arithmetic and copies ran while one was open for 0% of the time, Pallas kernels for 41%

profile of v5, /device:TPU:0, one launch (start us, length us, event | category | flops | bytes accessed | tf_op | source)
XLA Modules:
  0.0 57.3 jit_solution(14768498960202142975)
XLA Ops:
  0.6 0.0 copy-start
  0.6 0.0 copy-start.1
  0.6 2.5 %targets.1 = f32[24,128]{1,0:T(8,128)S(1)} custom-call(f32[3,128,128]{2,1,0:T(8,128)} %pos_ref.1, s32[2,4096]{1,0:T(2,128)} %links_ref.1, s32[4,256]{1,0:T(4,128)} %panel_hbm.1), custom_call_target="tpu_custom_call" | custom-call | tf_op jit(solution)/shard_map/targets/pallas_call | solution.py:368
  3.1 0.5 collective-permute-start
  3.7 0.0 copy-done
  3.7 0.0 copy-done.1
  3.7 1.2 %outgoing.1 = f32[32,24,128]{2,1,0:T(8,128)} custom-call(f32[3,128,128]{2,1,0:T(8,128)S(1)} %copy-done, s32[2,4096]{1,0:T(2,128)S(1)} %copy-done.1), custom_call_target="tpu_custom_call" | custom-call | flops 1000000000 | bytes 1000000 | tf_op jit(solution)/shard_map/outgoing/pallas_call | solution.py:383
  4.8 0.0 collective-permute-done
  4.8 2.5 %collective-permute-start.1 = (f32[24,128]{1,0:T(8,128)S(1)}, f32[24,128]{1,0:T(8,128)S(1)}, u32[]{:S(2)}, u32[]{:S(2)}) collective-permute-start(f32[24,128]{1,0:T(8,128)S(1)} %add.31), channel_id=1, source_target_pairs={{0,8},{8,0},{16,24},{24,16},{1,9},{9,1},{17,25},{25,17},{2,10},{10... | collective-permute-start | bytes 36872 | tf_op jit(solution)/shard_map/ppermute | solution.py:348
  7.3 1.5 %collective-permute-start.2 = (f32[24,128]{1,0:T(8,128)S(1)}, f32[24,128]{1,0:T(8,128)S(1)}, u32[]{:S(2)}, u32[]{:S(2)}) collective-permute-start(f32[24,128]{1,0:T(8,128)S(1)} %add.31), channel_id=1, source_target_pairs={{0,16},{8,24},{16,0},{24,8},{1,17},{9,25},{17,1},{25,9},{2,18},{10... | collective-permute-start | bytes 36872 | tf_op jit(solution)/shard_map/ppermute | solution.py:348
  8.9 0.0 collective-permute-start.3
  8.9 1.6 %sources.1 = (bf16[32,15872]{1,0:T(8,128)(2,1)S(1)}, bf16[16,15872]{1,0:T(8,128)(2,1)S(1)}, bf16[256,256]{1,0:T(8,128)(2,1)S(1)}, bf16[256,256]{1,0:T(8,128)(2,1)S(1)}) custom-call(f32[3,128,128]{2,1,0:T(8,128)S(1)} %copy-done, s32[2,4096]{1,0:T(2,128)S(1)} %copy-done.1), custom_call_target="tpu_custom_call" | custom-call | flops 1000000000 | bytes 10000000 | tf_op jit(solution)/shard_map/sources/pallas_call | solution.py:395
  10.5 0.0 collective-permute-done.1
  10.5 0.5 collective-permute-done.2
  11.0 2.4 %collective-permute-done.3 = f32[24,128]{1,0:T(8,128)S(1)} collective-permute-done((f32[24,128]{1,0:T(8,128)S(1)}, f32[24,128]{1,0:T(8,128)S(1)}, u32[]{:S(2)}, u32[]{:S(2)}) %collective-permute-start.3) | collective-permute-done | bytes 12320 | tf_op jit(solution)/shard_map/ppermute | solution.py:348
  13.5 1.6 %collective-permute-start.4 = (f32[24,128]{1,0:T(8,128)S(1)}, f32[24,128]{1,0:T(8,128)S(1)}, u32[]{:S(2)}, u32[]{:S(2)}) collective-permute-start(f32[24,128]{1,0:T(8,128)S(1)} %add_add_fusion.1), channel_id=1, source_target_pairs={{0,2},{1,3},{2,0},{3,1},{4,6},{5,7},{6,4},{7,5},{8,10},{9,11},{10,... | collective-permute-start | bytes 36872 | tf_op jit(solution)/shard_map/ppermute | solution.py:348
  15.0 2.6 %collective-permute-start.5 = (f32[24,128]{1,0:T(8,128)S(1)}, f32[24,128]{1,0:T(8,128)S(1)}, u32[]{:S(2)}, u32[]{:S(2)}) collective-permute-start(f32[24,128]{1,0:T(8,128)S(1)} %add_add_fusion.1), channel_id=1, source_target_pairs={{0,4},{1,5},{2,6},{3,7},{4,0},{5,1},{6,2},{7,3},{8,12},{9,13},{10,... | collective-permute-start | bytes 36872 | tf_op jit(solution)/shard_map/ppermute | solution.py:348
  17.6 0.2 collective-permute-start.6
  17.9 4.1 %all-to-all-start = ((f32[32,24,128]{2,1,0:T(8,128)}), f32[32,24,128]{2,1,0:T(8,128)S(1)}, u32[]{:S(2)}, u32[]{:S(2)}) async-start(f32[32,24,128]{2,1,0:T(8,128)} %outgoing.1), calls=%async_computation | async-start | bytes 786432 | tf_op jit(solution)/shard_map/all_to_all | solution.py:417
  22.0 0.0 collective-permute-done.4
  22.0 0.0 collective-permute-done.5
  22.0 1.1 %collective-permute-done.6 = f32[24,128]{1,0:T(8,128)S(1)} collective-permute-done((f32[24,128]{1,0:T(8,128)S(1)}, f32[24,128]{1,0:T(8,128)S(1)}, u32[]{:S(2)}, u32[]{:S(2)}) %collective-permute-start.6) | collective-permute-done | bytes 12320 | tf_op jit(solution)/shard_map/ppermute | solution.py:348
  23.1 18.8 %pairs.1 = (f32[16,1024]{1,0:T(8,128)S(1)}, bf16[32,1024]{1,0:T(8,128)(2,1)S(1)}, f32[3,1024]{1,0:T(4,128)S(1)}) custom-call(f32[24,128]{1,0:T(8,128)S(1)} %add_add_fusion.part_ref, bf16[32,15872]{1,0:T(8,128)(2,1)S(1)} %get-tuple-element.31.near_ref, bf16[16,15872]{1,0:T(8,128)(2,1)S(1)} %get-tuple-element.32.sums_ref), custom_call_target="tpu_custom_call" | custom-call | flops 32505856000 | bytes 10000000 | tf_op jit(solution)/shard_map/pairs/pallas_call | solution.py:418
  41.9 0.0 all-to-all-done.arrived_ref
  41.9 2.7 %ends.1 = f32[32,3,128]{2,1,0:T(4,128)} custom-call(f32[32,24,128]{2,1,0:T(8,128)S(1)} %all-to-all-done.arrived_ref, bf16[256,256]{1,0:T(8,128)(2,1)S(1)} %get-tuple-element.28.next_ref, bf16[256,256]{1,0:T(8,128)(2,1)S(1)} %get-tuple-element.29.prev_ref, bf16[32,1024]{1,0:T(8,128)(2,1)S(1)} %get-tuple-element.33.side_ref, ...), custom_call_target="tpu_custom_call" | custom-call | tf_op jit(solution)/shard_map/ends/pallas_call | solution.py:434
  44.6 4.6 %all-to-all-start.1 = ((f32[32,3,128]{2,1,0:T(4,128)}), f32[32,3,128]{2,1,0:T(4,128)S(1)}, u32[]{:S(2)}, u32[]{:S(2)}) async-start(f32[32,3,128]{2,1,0:T(4,128)} %ends.1), calls=%async_computation.1 | async-start | bytes 131072 | tf_op jit(solution)/shard_map/all_to_all | solution.py:457
  49.3 1.8 %smooth.1 = f32[3,256,128]{2,1,0:T(8,128)} custom-call(f32[32,24,128]{2,1,0:T(8,128)S(1)} %all-to-all-done.arrived_ref, bf16[256,256]{1,0:T(8,128)(2,1)S(1)} %get-tuple-element.28.next_ref, bf16[256,256]{1,0:T(8,128)(2,1)S(1)} %get-tuple-element.29.prev_ref), custom_call_target="tpu_custom_call" | custom-call | flops 1000000000 | bytes 10000000 | tf_op jit(solution)/shard_map/smooth/pallas_call | solution.py:447
  51.1 5.5 %all-to-all-done.1 = f32[32,3,128]{2,1,0:T(4,128)S(1)} async-done(((f32[32,3,128]{2,1,0:T(4,128)}), f32[32,3,128]{2,1,0:T(4,128)S(1)}, u32[]{:S(2)}, u32[]{:S(2)}) %all-to-all-start.1) | async-done | bytes 49184 | tf_op jit(solution)/shard_map/all_to_all | solution.py:457
  56.7 0.1 dynamic-slice_bitcast_fusion
  56.7 0.6 copy.5
  (4 shorter events, 0.1 us)
Async XLA Ops:
  0.6 3.0 %copy-start = (f32[3,128,128]{2,1,0:T(8,128)S(1)}, f32[3,128,128]{2,1,0:T(8,128)}, u32[]{:S(2)}) copy-start(f32[3,128,128]{2,1,0:T(8,128)} %pos_ref.1) | copy-start | bytes 589828
  0.6 3.0 %copy-start.1 = (s32[2,4096]{1,0:T(2,128)S(1)}, s32[2,4096]{1,0:T(2,128)}, u32[]{:S(2)}) copy-start(s32[2,4096]{1,0:T(2,128)} %links_ref.1) | copy-start | bytes 98308
  3.1 1.7 %collective-permute-start = (f32[24,128]{1,0:T(8,128)S(1)}, f32[24,128]{1,0:T(8,128)S(1)}, u32[]{:S(2)}, u32[]{:S(2)}) collective-permute-start(f32[24,128]{1,0:T(8,128)S(1)} %targets.1), channel_id=1, source_target_pairs={{0,1},{1,0},{2,3},{3,2},{4,5},{5,4},{6,7},{7,6},{8,9},{9,8},{10,11... | collective-permute-start | bytes 36872 | tf_op jit(solution)/shard_map/ppermute | solution.py:348
  4.8 5.7 %collective-permute-start.1 = (f32[24,128]{1,0:T(8,128)S(1)}, f32[24,128]{1,0:T(8,128)S(1)}, u32[]{:S(2)}, u32[]{:S(2)}) collective-permute-start(f32[24,128]{1,0:T(8,128)S(1)} %add.31), channel_id=1, source_target_pairs={{0,8},{8,0},{16,24},{24,16},{1,9},{9,1},{17,25},{25,17},{2,10},{10... | collective-permute-start | bytes 36872 | tf_op jit(solution)/shard_map/ppermute | solution.py:348
  7.3 3.7 %collective-permute-start.2 = (f32[24,128]{1,0:T(8,128)S(1)}, f32[24,128]{1,0:T(8,128)S(1)}, u32[]{:S(2)}, u32[]{:S(2)}) collective-permute-start(f32[24,128]{1,0:T(8,128)S(1)} %add.31), channel_id=1, source_target_pairs={{0,16},{8,24},{16,0},{24,8},{1,17},{9,25},{17,1},{25,9},{2,18},{10... | collective-permute-start | bytes 36872 | tf_op jit(solution)/shard_map/ppermute | solution.py:348
  8.9 4.6 %collective-permute-start.3 = (f32[24,128]{1,0:T(8,128)S(1)}, f32[24,128]{1,0:T(8,128)S(1)}, u32[]{:S(2)}, u32[]{:S(2)}) collective-permute-start(f32[24,128]{1,0:T(8,128)S(1)} %add.31), channel_id=1, source_target_pairs={{0,24},{8,16},{16,8},{24,0},{1,25},{9,17},{17,9},{25,1},{2,26},{10... | collective-permute-start | bytes 36872 | tf_op jit(solution)/shard_map/ppermute | solution.py:348
  13.5 8.5 %collective-permute-start.4 = (f32[24,128]{1,0:T(8,128)S(1)}, f32[24,128]{1,0:T(8,128)S(1)}, u32[]{:S(2)}, u32[]{:S(2)}) collective-permute-start(f32[24,128]{1,0:T(8,128)S(1)} %add_add_fusion.1), channel_id=1, source_target_pairs={{0,2},{1,3},{2,0},{3,1},{4,6},{5,7},{6,4},{7,5},{8,10},{9,11},{10,... | collective-permute-start | bytes 36872 | tf_op jit(solution)/shard_map/ppermute | solution.py:348
  15.0 7.0 %collective-permute-start.5 = (f32[24,128]{1,0:T(8,128)S(1)}, f32[24,128]{1,0:T(8,128)S(1)}, u32[]{:S(2)}, u32[]{:S(2)}) collective-permute-start(f32[24,128]{1,0:T(8,128)S(1)} %add_add_fusion.1), channel_id=1, source_target_pairs={{0,4},{1,5},{2,6},{3,7},{4,0},{5,1},{6,2},{7,3},{8,12},{9,13},{10,... | collective-permute-start | bytes 36872 | tf_op jit(solution)/shard_map/ppermute | solution.py:348
  17.6 5.5 %collective-permute-start.6 = (f32[24,128]{1,0:T(8,128)S(1)}, f32[24,128]{1,0:T(8,128)S(1)}, u32[]{:S(2)}, u32[]{:S(2)}) collective-permute-start(f32[24,128]{1,0:T(8,128)S(1)} %add_add_fusion.1), channel_id=1, source_target_pairs={{0,6},{1,7},{2,4},{3,5},{4,2},{5,3},{6,0},{7,1},{8,14},{9,15},{10,... | collective-permute-start | bytes 36872 | tf_op jit(solution)/shard_map/ppermute | solution.py:348
  17.9 24.1 %all-to-all-start = ((f32[32,24,128]{2,1,0:T(8,128)}), f32[32,24,128]{2,1,0:T(8,128)S(1)}, u32[]{:S(2)}, u32[]{:S(2)}) async-start(f32[32,24,128]{2,1,0:T(8,128)} %outgoing.1), calls=%async_computation | async-start | bytes 786432 | tf_op jit(solution)/shard_map/all_to_all | solution.py:417
  44.6 12.0 %all-to-all-start.1 = ((f32[32,3,128]{2,1,0:T(4,128)}), f32[32,3,128]{2,1,0:T(4,128)S(1)}, u32[]{:S(2)}, u32[]{:S(2)}) async-start(f32[32,3,128]{2,1,0:T(4,128)} %ends.1), calls=%async_computation.1 | async-start | bytes 131072 | tf_op jit(solution)/shard_map/all_to_all | solution.py:457

commit v6 on v5

--- a/solution.py
+++ b/solution.py
@@ -290,32 +290,33 @@
     return five_taps(*[rows[k : k + n] for k in range(5)])
 
 
-def end_kernel(cap, scale, share, arrived_ref, next_ref, prev_ref, side_ref, target_ref, acc_ref, vel_ref, x_scr, near_scr, sums_scr):
+def end_kernel(cap, scale, share, arrived_ref, next_ref, prev_ref, side_ref, target_ref, acc_ref, vel_ref, x_scr):
     held_blocks(cap, arrived_ref, x_scr)
     held = x_scr.shape[1]
     turned = [jnp.transpose(x_scr[c]) for c in range(3)]
     after = pick_rows(jnp.concatenate([t[:3] for t in turned], axis=0), prev_ref[...])
     before = pick_rows(jnp.concatenate([t[LANES - 2 :] for t in turned], axis=0), next_ref[...])
+    spare = jnp.zeros((8 - EDGES, held), F32)
     here = []
     ahead = []
     for c in range(3):
         first = taps_down(jnp.concatenate([before[2 * c : 2 * c + 2], turned[c][:5]], axis=0))
         last = taps_down(jnp.concatenate([turned[c][LANES - 5 :], after[3 * c : 3 * c + 3]], axis=0))
-        here.append(jnp.concatenate([first[:2], last[:3]], axis=0))
-        ahead.append(jnp.concatenate([first[1:], last[1:]], axis=0))
+        here.append(jnp.concatenate([first[:2], last[:3], spare], axis=0))
+        ahead.append(jnp.concatenate([first[1:], last[1:], spare], axis=0))
     near, sums = source_rows(here, ahead)
-    near_scr[...] = jnp.zeros_like(near_scr)
-    sums_scr[...] = jnp.zeros_like(sums_scr)
-    for k, value in enumerate(near):
-        for e in range(EDGES):
-            near_scr[k : k + 1, e * held : (e + 1) * held] = value[e : e + 1, :]
-    for k, value in enumerate(sums):
-        for e in range(EDGES):
-            sums_scr[k : k + 1, e * held : (e + 1) * held] = value[e : e + 1, :]
+    near += [jnp.zeros_like(near[0])] * (DEPTH - len(near))
+    sums += [jnp.zeros_like(sums[0])] * (FEATS - len(sums))
+    near, sums = [jnp.transpose(jnp.stack(v), (1, 0, 2)).astype(BF16) for v in (near, sums)]
     acc = acc_ref[...]
-    for e in range(0, EDGES * held, EPIECE * held):
-        at = slice(e, min(e + EPIECE * held, EDGES * held))
-        acc = pair_sums(acc, near_scr[:, at].astype(BF16), sums_scr[:, at].astype(BF16), side_ref[...])
+    for e in range(0, EDGES, EPIECE):
+        edges = range(e, min(e + EPIECE, EDGES))
+        acc = pair_sums(
+            acc,
+            jnp.concatenate([near[k] for k in edges], axis=1),
+            jnp.concatenate([sums[k] for k in edges], axis=1),
+            side_ref[...],
+        )
     terms = acc[0:6] + acc[6:12]
     targets = [target_ref[c : c + 1, :] for c in range(3)]
     turned = cross([terms[c : c + 1, :] for c in range(3)], targets)
@@ -391,7 +392,7 @@
     )(positions, block_links)
     part = part + swapped(part, "col", [1])[0]
     part, positions, outgoing = lax.optimization_barrier((part, positions, outgoing))
-    part = sum(swapped(part, "row", range(1, lax.axis_size("row"))), part)
+    part = sum(swapped(part, "row", range(lax.axis_size("row") - 1, 0, -1)), part)
     near, sums, to_next, to_prev = pl.pallas_call(
         functools.partial(source_kernel, cap),
         out_shape=(
@@ -412,7 +413,7 @@
     )(positions, block_links)
     near, part = lax.optimization_barrier((near, part))
     outgoing, part = lax.optimization_barrier((outgoing, part))
-    far = swapped(part, "col", range(2, lax.axis_size("col"), 2))
+    far = swapped(part, "col", range(lax.axis_size("col") - 2, 0, -2))
     parts = sum(far, part)
     arrived = lax.all_to_all(outgoing, AXES, split_axis=0, concat_axis=0, tiled=True)
     acc, side, targets = pl.pallas_call(
@@ -436,11 +437,7 @@
         out_shape=shape((devices, 3, LANES), F32),
         in_specs=[vmem] * 6,
         out_specs=vmem,
-        scratch_shapes=[
-            pltpu.VMEM((3, held, LANES), F32),
-            pltpu.VMEM((DEPTH, EDGES * held), F32),
-            pltpu.VMEM((FEATS, EDGES * held), F32),
-        ],
+        scratch_shapes=[pltpu.VMEM((3, held, LANES), F32)],
         compiler_params=params,
         name="ends",
     )(arrived, to_next, to_prev, side, targets, acc)

time: 57.6 us -> 57.6 us (level)
  waiting for transfers between devices: 9.57 us -> 7.45 us
  starting transfers between devices: 17.7 us -> 19.8 us
    ppermute x7, waiting for transfers between devices: 4.03 us -> 1.92 us  [swapped(): lax.ppermute(value, axis, [(k, k ^ step) for k in range(size)])]
    all_to_all x1, starting transfers between devices: 4.59 us -> 5.66 us  [shards(): lax.all_to_all(velocity, AXES, split_axis=0, concat_axis=0, tiled=True)]
    all_to_all x1, starting transfers between devices: 4.15 us -> 5.11 us  [shards(): lax.all_to_all(outgoing, AXES, split_axis=0, concat_axis=0, tiled=True)]
  transfers between devices with their start and end apart: 9 -> 9, of which waited for: 4 -> 3; matrix products, arithmetic and copies ran while one was open for 0% -> 0% of each run, Pallas kernels for 41% -> 41%
where the time goes in v6:
time: 57.6 us; the launch traced here: 57.3 us
  Pallas kernels  28.6 us (50%)
  starting transfers between devices  19.8 us (34%)
  waiting for transfers between devices  7.45 us (13%)
  between operations  0.75 us (1%)
  local copies, waits for them, and re-layouts  0.65 us (1%)
    pallas_call x1, Pallas kernels, shards(): pl.pallas_call(functools.partial(pair_kernel, points // 2, 512), out_shap...  18.8 us
    ppermute x7, starting transfers between devices, swapped(): lax.ppermute(value, axis, [(k, k ^ step) for k in range(size)])  9.01 us
    all_to_all x1, starting transfers between devices, shards(): lax.all_to_all(velocity, AXES, split_axis=0, concat_axis=0, tiled=True)  5.66 us
    all_to_all x1, waiting for transfers between devices, shards(): lax.all_to_all(velocity, AXES, split_axis=0, concat_axis=0, tiled=True)  5.53 us
    all_to_all x1, starting transfers between devices, shards(): lax.all_to_all(outgoing, AXES, split_axis=0, concat_axis=0, tiled=True)  5.11 us
    pallas_call x1, Pallas kernels, shards(): pl.pallas_call(functools.partial(end_kernel, cap, scale, share), out_shap...  2.7 us
    pallas_call x1, Pallas kernels, shards(): pl.pallas_call(target_kernel, out_shape=shape((rows, LANES), F32), in_spe...  2.48 us
    ppermute x7, waiting for transfers between devices, swapped(): lax.ppermute(value, axis, [(k, k ^ step) for k in range(size)])  1.92 us
  transfers between devices with their start and end apart: 9, of which 3 were waited for; matrix products, arithmetic and copies ran while one was open for 0% of the time, Pallas kernels for 41%

profile of v6, /device:TPU:0, one launch (start us, length us, event | category | flops | bytes accessed | tf_op | source)
XLA Modules:
  0.0 57.3 jit_solution(8342270046367490911)
XLA Ops:
  0.6 0.0 copy-start
  0.6 0.0 copy-start.1
  0.6 2.5 %targets.1 = f32[24,128]{1,0:T(8,128)S(1)} custom-call(f32[3,128,128]{2,1,0:T(8,128)} %pos_ref.1, s32[2,4096]{1,0:T(2,128)} %links_ref.1, s32[4,256]{1,0:T(4,128)} %panel_hbm.1), custom_call_target="tpu_custom_call" | custom-call | tf_op jit(solution)/shard_map/targets/pallas_call | solution.py:369
  3.1 0.5 collective-permute-start
  3.7 0.0 copy-done
  3.7 0.0 copy-done.1
  3.7 1.2 %outgoing.1 = f32[32,24,128]{2,1,0:T(8,128)} custom-call(f32[3,128,128]{2,1,0:T(8,128)S(1)} %copy-done, s32[2,4096]{1,0:T(2,128)S(1)} %copy-done.1), custom_call_target="tpu_custom_call" | custom-call | flops 1000000000 | bytes 1000000 | tf_op jit(solution)/shard_map/outgoing/pallas_call | solution.py:384
  4.8 0.0 collective-permute-done
  4.8 3.5 %collective-permute-start.1 = (f32[24,128]{1,0:T(8,128)S(1)}, f32[24,128]{1,0:T(8,128)S(1)}, u32[]{:S(2)}, u32[]{:S(2)}) collective-permute-start(f32[24,128]{1,0:T(8,128)S(1)} %add.31), channel_id=1, source_target_pairs={{0,24},{8,16},{16,8},{24,0},{1,25},{9,17},{17,9},{25,1},{2,26},{10... | collective-permute-start | bytes 36872 | tf_op jit(solution)/shard_map/ppermute | solution.py:349
  8.3 0.5 collective-permute-start.2
  8.8 0.1 collective-permute-start.3
  8.9 1.6 %sources.1 = (bf16[32,15872]{1,0:T(8,128)(2,1)S(1)}, bf16[16,15872]{1,0:T(8,128)(2,1)S(1)}, bf16[256,256]{1,0:T(8,128)(2,1)S(1)}, bf16[256,256]{1,0:T(8,128)(2,1)S(1)}) custom-call(f32[3,128,128]{2,1,0:T(8,128)S(1)} %copy-done, s32[2,4096]{1,0:T(2,128)S(1)} %copy-done.1), custom_call_target="tpu_custom_call" | custom-call | flops 1000000000 | bytes 10000000 | tf_op jit(solution)/shard_map/sources/pallas_call | solution.py:396
  10.6 0.0 collective-permute-done.1
  10.6 1.4 %collective-permute-done.2 = f32[24,128]{1,0:T(8,128)S(1)} collective-permute-done((f32[24,128]{1,0:T(8,128)S(1)}, f32[24,128]{1,0:T(8,128)S(1)}, u32[]{:S(2)}, u32[]{:S(2)}) %collective-permute-start.2) | collective-permute-done | bytes 12320 | tf_op jit(solution)/shard_map/ppermute | solution.py:349
  12.0 0.5 collective-permute-done.3
  12.5 3.6 %collective-permute-start.4 = (f32[24,128]{1,0:T(8,128)S(1)}, f32[24,128]{1,0:T(8,128)S(1)}, u32[]{:S(2)}, u32[]{:S(2)}) collective-permute-start(f32[24,128]{1,0:T(8,128)S(1)} %add_add_fusion.1), channel_id=1, source_target_pairs={{0,6},{1,7},{2,4},{3,5},{4,2},{5,3},{6,0},{7,1},{8,14},{9,15},{10,... | collective-permute-start | bytes 36872 | tf_op jit(solution)/shard_map/ppermute | solution.py:349
  16.1 0.0 collective-permute-start.5
  16.1 0.8 %collective-permute-start.6 = (f32[24,128]{1,0:T(8,128)S(1)}, f32[24,128]{1,0:T(8,128)S(1)}, u32[]{:S(2)}, u32[]{:S(2)}) collective-permute-start(f32[24,128]{1,0:T(8,128)S(1)} %add_add_fusion.1), channel_id=1, source_target_pairs={{0,2},{1,3},{2,0},{3,1},{4,6},{5,7},{6,4},{7,5},{8,10},{9,11},{10,... | collective-permute-start | bytes 36872 | tf_op jit(solution)/shard_map/ppermute | solution.py:349
  16.9 5.1 %all-to-all-start = ((f32[32,24,128]{2,1,0:T(8,128)}), f32[32,24,128]{2,1,0:T(8,128)S(1)}, u32[]{:S(2)}, u32[]{:S(2)}) async-start(f32[32,24,128]{2,1,0:T(8,128)} %outgoing.1), calls=%async_computation | async-start | bytes 786432 | tf_op jit(solution)/shard_map/all_to_all | solution.py:418
  22.0 0.0 collective-permute-done.4
  22.0 0.0 collective-permute-done.5
  22.0 0.0 collective-permute-done.6
  22.1 18.8 %pairs.1 = (f32[16,1024]{1,0:T(8,128)S(1)}, bf16[32,1024]{1,0:T(8,128)(2,1)S(1)}, f32[3,1024]{1,0:T(4,128)S(1)}) custom-call(f32[24,128]{1,0:T(8,128)S(1)} %add_add_fusion.part_ref, bf16[32,15872]{1,0:T(8,128)(2,1)S(1)} %get-tuple-element.31.near_ref, bf16[16,15872]{1,0:T(8,128)(2,1)S(1)} %get-tuple-element.32.sums_ref), custom_call_target="tpu_custom_call" | custom-call | flops 32505856000 | bytes 10000000 | tf_op jit(solution)/shard_map/pairs/pallas_call | solution.py:419
  40.8 0.0 all-to-all-done.arrived_ref
  40.8 2.7 %ends.1 = f32[32,3,128]{2,1,0:T(4,128)} custom-call(f32[32,24,128]{2,1,0:T(8,128)S(1)} %all-to-all-done.arrived_ref, bf16[256,256]{1,0:T(8,128)(2,1)S(1)} %get-tuple-element.28.next_ref, bf16[256,256]{1,0:T(8,128)(2,1)S(1)} %get-tuple-element.29.prev_ref, bf16[32,1024]{1,0:T(8,128)(2,1)S(1)} %get-tuple-element.33.side_ref, ...), custom_call_target="tpu_custom_call" | custom-call | tf_op jit(solution)/shard_map/ends/pallas_call | solution.py:435
  43.5 5.7 %all-to-all-start.1 = ((f32[32,3,128]{2,1,0:T(4,128)}), f32[32,3,128]{2,1,0:T(4,128)S(1)}, u32[]{:S(2)}, u32[]{:S(2)}) async-start(f32[32,3,128]{2,1,0:T(4,128)} %ends.1), calls=%async_computation.1 | async-start | bytes 131072 | tf_op jit(solution)/shard_map/all_to_all | solution.py:454
  49.2 1.8 %smooth.1 = f32[3,256,128]{2,1,0:T(8,128)} custom-call(f32[32,24,128]{2,1,0:T(8,128)S(1)} %all-to-all-done.arrived_ref, bf16[256,256]{1,0:T(8,128)(2,1)S(1)} %get-tuple-element.28.next_ref, bf16[256,256]{1,0:T(8,128)(2,1)S(1)} %get-tuple-element.29.prev_ref), custom_call_target="tpu_custom_call" | custom-call | flops 1000000000 | bytes 10000000 | tf_op jit(solution)/shard_map/smooth/pallas_call | solution.py:444
  51.1 5.5 %all-to-all-done.1 = f32[32,3,128]{2,1,0:T(4,128)S(1)} async-done(((f32[32,3,128]{2,1,0:T(4,128)}), f32[32,3,128]{2,1,0:T(4,128)S(1)}, u32[]{:S(2)}, u32[]{:S(2)}) %all-to-all-start.1) | async-done | bytes 49184 | tf_op jit(solution)/shard_map/all_to_all | solution.py:454
  56.6 0.1 dynamic-slice_bitcast_fusion
  56.7 0.6 copy.5
  (4 shorter events, 0.1 us)
Async XLA Ops:
  0.6 3.0 %copy-start = (f32[3,128,128]{2,1,0:T(8,128)S(1)}, f32[3,128,128]{2,1,0:T(8,128)}, u32[]{:S(2)}) copy-start(f32[3,128,128]{2,1,0:T(8,128)} %pos_ref.1) | copy-start | bytes 589828
  0.6 3.0 %copy-start.1 = (s32[2,4096]{1,0:T(2,128)S(1)}, s32[2,4096]{1,0:T(2,128)}, u32[]{:S(2)}) copy-start(s32[2,4096]{1,0:T(2,128)} %links_ref.1) | copy-start | bytes 98308
  3.1 1.7 %collective-permute-start = (f32[24,128]{1,0:T(8,128)S(1)}, f32[24,128]{1,0:T(8,128)S(1)}, u32[]{:S(2)}, u32[]{:S(2)}) collective-permute-start(f32[24,128]{1,0:T(8,128)S(1)} %targets.1), channel_id=1, source_target_pairs={{0,1},{1,0},{2,3},{3,2},{4,5},{5,4},{6,7},{7,6},{8,9},{9,8},{10,11... | collective-permute-start | bytes 36872 | tf_op jit(solution)/shard_map/ppermute | solution.py:349
  4.8 5.8 %collective-permute-start.1 = (f32[24,128]{1,0:T(8,128)S(1)}, f32[24,128]{1,0:T(8,128)S(1)}, u32[]{:S(2)}, u32[]{:S(2)}) collective-permute-start(f32[24,128]{1,0:T(8,128)S(1)} %add.31), channel_id=1, source_target_pairs={{0,24},{8,16},{16,8},{24,0},{1,25},{9,17},{17,9},{25,1},{2,26},{10... | collective-permute-start | bytes 36872 | tf_op jit(solution)/shard_map/ppermute | solution.py:349
  8.3 3.7 %collective-permute-start.2 = (f32[24,128]{1,0:T(8,128)S(1)}, f32[24,128]{1,0:T(8,128)S(1)}, u32[]{:S(2)}, u32[]{:S(2)}) collective-permute-start(f32[24,128]{1,0:T(8,128)S(1)} %add.31), channel_id=1, source_target_pairs={{0,16},{8,24},{16,0},{24,8},{1,17},{9,25},{17,1},{25,9},{2,18},{10... | collective-permute-start | bytes 36872 | tf_op jit(solution)/shard_map/ppermute | solution.py:349
  8.8 3.7 %collective-permute-start.3 = (f32[24,128]{1,0:T(8,128)S(1)}, f32[24,128]{1,0:T(8,128)S(1)}, u32[]{:S(2)}, u32[]{:S(2)}) collective-permute-start(f32[24,128]{1,0:T(8,128)S(1)} %add.31), channel_id=1, source_target_pairs={{0,8},{8,0},{16,24},{24,16},{1,9},{9,1},{17,25},{25,17},{2,10},{10... | collective-permute-start | bytes 36872 | tf_op jit(solution)/shard_map/ppermute | solution.py:349
  12.5 9.5 %collective-permute-start.4 = (f32[24,128]{1,0:T(8,128)S(1)}, f32[24,128]{1,0:T(8,128)S(1)}, u32[]{:S(2)}, u32[]{:S(2)}) collective-permute-start(f32[24,128]{1,0:T(8,128)S(1)} %add_add_fusion.1), channel_id=1, source_target_pairs={{0,6},{1,7},{2,4},{3,5},{4,2},{5,3},{6,0},{7,1},{8,14},{9,15},{10,... | collective-permute-start | bytes 36872 | tf_op jit(solution)/shard_map/ppermute | solution.py:349
  16.1 5.9 %collective-permute-start.5 = (f32[24,128]{1,0:T(8,128)S(1)}, f32[24,128]{1,0:T(8,128)S(1)}, u32[]{:S(2)}, u32[]{:S(2)}) collective-permute-start(f32[24,128]{1,0:T(8,128)S(1)} %add_add_fusion.1), channel_id=1, source_target_pairs={{0,4},{1,5},{2,6},{3,7},{4,0},{5,1},{6,2},{7,3},{8,12},{9,13},{10,... | collective-permute-start | bytes 36872 | tf_op jit(solution)/shard_map/ppermute | solution.py:349
  16.1 5.9 %collective-permute-start.6 = (f32[24,128]{1,0:T(8,128)S(1)}, f32[24,128]{1,0:T(8,128)S(1)}, u32[]{:S(2)}, u32[]{:S(2)}) collective-permute-start(f32[24,128]{1,0:T(8,128)S(1)} %add_add_fusion.1), channel_id=1, source_target_pairs={{0,2},{1,3},{2,0},{3,1},{4,6},{5,7},{6,4},{7,5},{8,10},{9,11},{10,... | collective-permute-start | bytes 36872 | tf_op jit(solution)/shard_map/ppermute | solution.py:349
  16.9 23.9 %all-to-all-start = ((f32[32,24,128]{2,1,0:T(8,128)}), f32[32,24,128]{2,1,0:T(8,128)S(1)}, u32[]{:S(2)}, u32[]{:S(2)}) async-start(f32[32,24,128]{2,1,0:T(8,128)} %outgoing.1), calls=%async_computation | async-start | bytes 786432 | tf_op jit(solution)/shard_map/all_to_all | solution.py:418
  43.5 13.1 %all-to-all-start.1 = ((f32[32,3,128]{2,1,0:T(4,128)}), f32[32,3,128]{2,1,0:T(4,128)S(1)}, u32[]{:S(2)}, u32[]{:S(2)}) async-start(f32[32,3,128]{2,1,0:T(4,128)} %ends.1), calls=%async_computation.1 | async-start | bytes 131072 | tf_op jit(solution)/shard_map/all_to_all | solution.py:454

commit v7 on v6

--- a/solution.py
+++ b/solution.py
@@ -157,8 +157,9 @@
         own = five_taps(inner[-2], inner[-1], x, inner[1], inner[2])
         other = five_taps(outer[-2], outer[-1], 0.0, outer[1], outer[2])
         stacked.append(jnp.transpose(jnp.concatenate([own, other], axis=0)))
-    one, two, three = three_parts(jnp.concatenate(stacked, axis=0))
-    values = dot(one, onehot) + dot(two, onehot) + dot(three, onehot)
+    parts = dot(jnp.concatenate(three_parts(jnp.concatenate(stacked, axis=0)), axis=0), onehot)
+    size = 3 * LANES
+    values = parts[:size] + parts[size : 2 * size] + parts[2 * size :]
     at_point = iota((LANES, count), 0) == wanted_point
     per = count // LANES
     for c in range(3):

time: 57.6 us -> 57.5 us (level)
  no operation moved by 1% of the time
where the time goes in v7:
time: 57.5 us; the launch traced here: 57.3 us
  Pallas kernels  28.6 us (50%)
  starting transfers between devices  19.8 us (34%)
  waiting for transfers between devices  7.46 us (13%)
  between operations  0.75 us (1%)
  local copies, waits for them, and re-layouts  0.65 us (1%)
    pallas_call x1, Pallas kernels, shards(): pl.pallas_call(functools.partial(pair_kernel, points // 2, 512), out_shap...  18.8 us
    ppermute x7, starting transfers between devices, swapped(): lax.ppermute(value, axis, [(k, k ^ step) for k in range(size)])  9.01 us
    all_to_all x1, starting transfers between devices, shards(): lax.all_to_all(velocity, AXES, split_axis=0, concat_axis=0, tiled=True)  5.66 us
    all_to_all x1, waiting for transfers between devices, shards(): lax.all_to_all(velocity, AXES, split_axis=0, concat_axis=0, tiled=True)  5.53 us
    all_to_all x1, starting transfers between devices, shards(): lax.all_to_all(outgoing, AXES, split_axis=0, concat_axis=0, tiled=True)  5.1 us
    pallas_call x1, Pallas kernels, shards(): pl.pallas_call(functools.partial(end_kernel, cap, scale, share), out_shap...  2.7 us
    pallas_call x1, Pallas kernels, shards(): pl.pallas_call(target_kernel, out_shape=shape((rows, LANES), F32), in_spe...  2.44 us
    ppermute x7, waiting for transfers between devices, swapped(): lax.ppermute(value, axis, [(k, k ^ step) for k in range(size)])  1.93 us
  transfers between devices with their start and end apart: 9, of which 3 were waited for; matrix products, arithmetic and copies ran while one was open for 0% of the time, Pallas kernels for 41%

profile of v7, /device:TPU:0, one launch (start us, length us, event | category | flops | bytes accessed | tf_op | source)
XLA Modules:
  0.0 57.3 jit_solution(4101425573177288281)
XLA Ops:
  0.6 0.0 copy-start
  0.6 0.0 copy-start.1
  0.6 2.4 %targets.1 = f32[24,128]{1,0:T(8,128)S(1)} custom-call(f32[3,128,128]{2,1,0:T(8,128)} %pos_ref.1, s32[2,4096]{1,0:T(2,128)} %links_ref.1, s32[4,256]{1,0:T(4,128)} %panel_hbm.1), custom_call_target="tpu_custom_call" | custom-call | tf_op jit(solution)/shard_map/targets/pallas_call | solution.py:370
  3.1 0.5 collective-permute-start
  3.6 0.0 copy-done
  3.6 0.0 copy-done.1
  3.6 1.2 %outgoing.1 = f32[32,24,128]{2,1,0:T(8,128)} custom-call(f32[3,128,128]{2,1,0:T(8,128)S(1)} %copy-done, s32[2,4096]{1,0:T(2,128)S(1)} %copy-done.1), custom_call_target="tpu_custom_call" | custom-call | flops 1000000000 | bytes 1000000 | tf_op jit(solution)/shard_map/outgoing/pallas_call | solution.py:385
  4.8 0.0 collective-permute-done
  4.8 3.5 %collective-permute-start.1 = (f32[24,128]{1,0:T(8,128)S(1)}, f32[24,128]{1,0:T(8,128)S(1)}, u32[]{:S(2)}, u32[]{:S(2)}) collective-permute-start(f32[24,128]{1,0:T(8,128)S(1)} %add.31), channel_id=1, source_target_pairs={{0,24},{8,16},{16,8},{24,0},{1,25},{9,17},{17,9},{25,1},{2,26},{10... | collective-permute-start | bytes 36872 | tf_op jit(solution)/shard_map/ppermute | solution.py:350
  8.3 0.5 collective-permute-start.2
  8.8 0.1 collective-permute-start.3
  8.9 1.6 %sources.1 = (bf16[32,15872]{1,0:T(8,128)(2,1)S(1)}, bf16[16,15872]{1,0:T(8,128)(2,1)S(1)}, bf16[256,256]{1,0:T(8,128)(2,1)S(1)}, bf16[256,256]{1,0:T(8,128)(2,1)S(1)}) custom-call(f32[3,128,128]{2,1,0:T(8,128)S(1)} %copy-done, s32[2,4096]{1,0:T(2,128)S(1)} %copy-done.1), custom_call_target="tpu_custom_call" | custom-call | flops 1000000000 | bytes 10000000 | tf_op jit(solution)/shard_map/sources/pallas_call | solution.py:397
  10.5 0.0 collective-permute-done.1
  10.6 1.4 %collective-permute-done.2 = f32[24,128]{1,0:T(8,128)S(1)} collective-permute-done((f32[24,128]{1,0:T(8,128)S(1)}, f32[24,128]{1,0:T(8,128)S(1)}, u32[]{:S(2)}, u32[]{:S(2)}) %collective-permute-start.2) | collective-permute-done | bytes 12320 | tf_op jit(solution)/shard_map/ppermute | solution.py:350
  12.0 0.5 collective-permute-done.3
  12.5 3.6 %collective-permute-start.4 = (f32[24,128]{1,0:T(8,128)S(1)}, f32[24,128]{1,0:T(8,128)S(1)}, u32[]{:S(2)}, u32[]{:S(2)}) collective-permute-start(f32[24,128]{1,0:T(8,128)S(1)} %add_add_fusion.1), channel_id=1, source_target_pairs={{0,6},{1,7},{2,4},{3,5},{4,2},{5,3},{6,0},{7,1},{8,14},{9,15},{10,... | collective-permute-start | bytes 36872 | tf_op jit(solution)/shard_map/ppermute | solution.py:350
  16.1 0.0 collective-permute-start.5
  16.1 0.8 %collective-permute-start.6 = (f32[24,128]{1,0:T(8,128)S(1)}, f32[24,128]{1,0:T(8,128)S(1)}, u32[]{:S(2)}, u32[]{:S(2)}) collective-permute-start(f32[24,128]{1,0:T(8,128)S(1)} %add_add_fusion.1), channel_id=1, source_target_pairs={{0,2},{1,3},{2,0},{3,1},{4,6},{5,7},{6,4},{7,5},{8,10},{9,11},{10,... | collective-permute-start | bytes 36872 | tf_op jit(solution)/shard_map/ppermute | solution.py:350
  16.9 5.1 %all-to-all-start = ((f32[32,24,128]{2,1,0:T(8,128)}), f32[32,24,128]{2,1,0:T(8,128)S(1)}, u32[]{:S(2)}, u32[]{:S(2)}) async-start(f32[32,24,128]{2,1,0:T(8,128)} %outgoing.1), calls=%async_computation | async-start | bytes 786432 | tf_op jit(solution)/shard_map/all_to_all | solution.py:419
  22.0 0.0 collective-permute-done.4
  22.0 0.0 collective-permute-done.5
  22.0 0.0 collective-permute-done.6
  22.0 18.8 %pairs.1 = (f32[16,1024]{1,0:T(8,128)S(1)}, bf16[32,1024]{1,0:T(8,128)(2,1)S(1)}, f32[3,1024]{1,0:T(4,128)S(1)}) custom-call(f32[24,128]{1,0:T(8,128)S(1)} %add_add_fusion.part_ref, bf16[32,15872]{1,0:T(8,128)(2,1)S(1)} %get-tuple-element.31.near_ref, bf16[16,15872]{1,0:T(8,128)(2,1)S(1)} %get-tuple-element.32.sums_ref), custom_call_target="tpu_custom_call" | custom-call | flops 32505856000 | bytes 10000000 | tf_op jit(solution)/shard_map/pairs/pallas_call | solution.py:420
  40.8 0.0 all-to-all-done.arrived_ref
  40.8 2.7 %ends.1 = f32[32,3,128]{2,1,0:T(4,128)} custom-call(f32[32,24,128]{2,1,0:T(8,128)S(1)} %all-to-all-done.arrived_ref, bf16[256,256]{1,0:T(8,128)(2,1)S(1)} %get-tuple-element.28.next_ref, bf16[256,256]{1,0:T(8,128)(2,1)S(1)} %get-tuple-element.29.prev_ref, bf16[32,1024]{1,0:T(8,128)(2,1)S(1)} %get-tuple-element.33.side_ref, ...), custom_call_target="tpu_custom_call" | custom-call | tf_op jit(solution)/shard_map/ends/pallas_call | solution.py:436
  43.5 5.7 %all-to-all-start.1 = ((f32[32,3,128]{2,1,0:T(4,128)}), f32[32,3,128]{2,1,0:T(4,128)S(1)}, u32[]{:S(2)}, u32[]{:S(2)}) async-start(f32[32,3,128]{2,1,0:T(4,128)} %ends.1), calls=%async_computation.1 | async-start | bytes 131072 | tf_op jit(solution)/shard_map/all_to_all | solution.py:455
  49.2 1.8 %smooth.1 = f32[3,256,128]{2,1,0:T(8,128)} custom-call(f32[32,24,128]{2,1,0:T(8,128)S(1)} %all-to-all-done.arrived_ref, bf16[256,256]{1,0:T(8,128)(2,1)S(1)} %get-tuple-element.28.next_ref, bf16[256,256]{1,0:T(8,128)(2,1)S(1)} %get-tuple-element.29.prev_ref), custom_call_target="tpu_custom_call" | custom-call | flops 1000000000 | bytes 10000000 | tf_op jit(solution)/shard_map/smooth/pallas_call | solution.py:445
  51.0 5.5 %all-to-all-done.1 = f32[32,3,128]{2,1,0:T(4,128)S(1)} async-done(((f32[32,3,128]{2,1,0:T(4,128)}), f32[32,3,128]{2,1,0:T(4,128)S(1)}, u32[]{:S(2)}, u32[]{:S(2)}) %all-to-all-start.1) | async-done | bytes 49184 | tf_op jit(solution)/shard_map/all_to_all | solution.py:455
  56.6 0.1 dynamic-slice_bitcast_fusion
  56.7 0.6 copy.5
  (4 shorter events, 0.1 us)
Async XLA Ops:
  0.6 3.0 %copy-start = (f32[3,128,128]{2,1,0:T(8,128)S(1)}, f32[3,128,128]{2,1,0:T(8,128)}, u32[]{:S(2)}) copy-start(f32[3,128,128]{2,1,0:T(8,128)} %pos_ref.1) | copy-start | bytes 589828
  0.6 3.0 %copy-start.1 = (s32[2,4096]{1,0:T(2,128)S(1)}, s32[2,4096]{1,0:T(2,128)}, u32[]{:S(2)}) copy-start(s32[2,4096]{1,0:T(2,128)} %links_ref.1) | copy-start | bytes 98308
  3.1 1.7 %collective-permute-start = (f32[24,128]{1,0:T(8,128)S(1)}, f32[24,128]{1,0:T(8,128)S(1)}, u32[]{:S(2)}, u32[]{:S(2)}) collective-permute-start(f32[24,128]{1,0:T(8,128)S(1)} %targets.1), channel_id=1, source_target_pairs={{0,1},{1,0},{2,3},{3,2},{4,5},{5,4},{6,7},{7,6},{8,9},{9,8},{10,11... | collective-permute-start | bytes 36872 | tf_op jit(solution)/shard_map/ppermute | solution.py:350
  4.8 5.8 %collective-permute-start.1 = (f32[24,128]{1,0:T(8,128)S(1)}, f32[24,128]{1,0:T(8,128)S(1)}, u32[]{:S(2)}, u32[]{:S(2)}) collective-permute-start(f32[24,128]{1,0:T(8,128)S(1)} %add.31), channel_id=1, source_target_pairs={{0,24},{8,16},{16,8},{24,0},{1,25},{9,17},{17,9},{25,1},{2,26},{10... | collective-permute-start | bytes 36872 | tf_op jit(solution)/shard_map/ppermute | solution.py:350
  8.3 3.7 %collective-permute-start.2 = (f32[24,128]{1,0:T(8,128)S(1)}, f32[24,128]{1,0:T(8,128)S(1)}, u32[]{:S(2)}, u32[]{:S(2)}) collective-permute-start(f32[24,128]{1,0:T(8,128)S(1)} %add.31), channel_id=1, source_target_pairs={{0,16},{8,24},{16,0},{24,8},{1,17},{9,25},{17,1},{25,9},{2,18},{10... | collective-permute-start | bytes 36872 | tf_op jit(solution)/shard_map/ppermute | solution.py:350
  8.8 3.7 %collective-permute-start.3 = (f32[24,128]{1,0:T(8,128)S(1)}, f32[24,128]{1,0:T(8,128)S(1)}, u32[]{:S(2)}, u32[]{:S(2)}) collective-permute-start(f32[24,128]{1,0:T(8,128)S(1)} %add.31), channel_id=1, source_target_pairs={{0,8},{8,0},{16,24},{24,16},{1,9},{9,1},{17,25},{25,17},{2,10},{10... | collective-permute-start | bytes 36872 | tf_op jit(solution)/shard_map/ppermute | solution.py:350
  12.5 9.5 %collective-permute-start.4 = (f32[24,128]{1,0:T(8,128)S(1)}, f32[24,128]{1,0:T(8,128)S(1)}, u32[]{:S(2)}, u32[]{:S(2)}) collective-permute-start(f32[24,128]{1,0:T(8,128)S(1)} %add_add_fusion.1), channel_id=1, source_target_pairs={{0,6},{1,7},{2,4},{3,5},{4,2},{5,3},{6,0},{7,1},{8,14},{9,15},{10,... | collective-permute-start | bytes 36872 | tf_op jit(solution)/shard_map/ppermute | solution.py:350
  16.1 5.9 %collective-permute-start.5 = (f32[24,128]{1,0:T(8,128)S(1)}, f32[24,128]{1,0:T(8,128)S(1)}, u32[]{:S(2)}, u32[]{:S(2)}) collective-permute-start(f32[24,128]{1,0:T(8,128)S(1)} %add_add_fusion.1), channel_id=1, source_target_pairs={{0,4},{1,5},{2,6},{3,7},{4,0},{5,1},{6,2},{7,3},{8,12},{9,13},{10,... | collective-permute-start | bytes 36872 | tf_op jit(solution)/shard_map/ppermute | solution.py:350
  16.1 5.9 %collective-permute-start.6 = (f32[24,128]{1,0:T(8,128)S(1)}, f32[24,128]{1,0:T(8,128)S(1)}, u32[]{:S(2)}, u32[]{:S(2)}) collective-permute-start(f32[24,128]{1,0:T(8,128)S(1)} %add_add_fusion.1), channel_id=1, source_target_pairs={{0,2},{1,3},{2,0},{3,1},{4,6},{5,7},{6,4},{7,5},{8,10},{9,11},{10,... | collective-permute-start | bytes 36872 | tf_op jit(solution)/shard_map/ppermute | solution.py:350
  16.9 23.9 %all-to-all-start = ((f32[32,24,128]{2,1,0:T(8,128)}), f32[32,24,128]{2,1,0:T(8,128)S(1)}, u32[]{:S(2)}, u32[]{:S(2)}) async-start(f32[32,24,128]{2,1,0:T(8,128)} %outgoing.1), calls=%async_computation | async-start | bytes 786432 | tf_op jit(solution)/shard_map/all_to_all | solution.py:419
  43.5 13.1 %all-to-all-start.1 = ((f32[32,3,128]{2,1,0:T(4,128)}), f32[32,3,128]{2,1,0:T(4,128)S(1)}, u32[]{:S(2)}, u32[]{:S(2)}) async-start(f32[32,3,128]{2,1,0:T(4,128)} %ends.1), calls=%async_computation.1 | async-start | bytes 131072 | tf_op jit(solution)/shard_map/all_to_all | solution.py:455
